TPU v7x, 512 devices: a whole 4x8x8 slice. The times are simulated.
512 devices in a mesh: view: 8 (over x, y_hi), row: 16 (over z, core), mat: 4 (over y_lo).
Axes of the slice: x: 4, y: 8 (y_hi: 2, y_lo: 4; y = y_hi * 4 + y_lo), z: 8, core: 2. Of those that a mesh axis runs over, the one named last changes fastest.
Arguments:
- volume: float32 [512, 3, 2048], P(('row', 'mat')), may hold values from 0 to 1
- projector: bfloat16 [32, 1024, 2048], P(('view', 'mat')), may hold values from -0.125 to 0.125
- counts: bfloat16 [32, 512, 4, 1024], P(('view', 'mat'), 'row'), may hold values from 0.049804688 to 1
- atten: float32 [4, 3], replicated, may hold values from 0.1 to 1
- newton: bfloat16 [512, 3, 3, 2048], P(('row', 'mat')), may hold values from -0.25 to 0.80078125, as said below
Outputs:
- updated: float32 [512, 3, 2048], P(('row', 'mat'))
Inputs may be any that keep to these rules, and one draw needn't show every extreme that they name: newton is symmetric in its two material dimensions; after rounding to bfloat16 its diagonal lies in 0.2 to 0.80078125 and each off-diagonal entry is at most about 0.3 times the root of the two diagonal entries in magnitude.
All inputs are finite; a program needn't handle non-finite values.
Results may differ from a plain program's by a relative error of at most 0.0028.
The roundings to bfloat16 on the way count: a program that leaves them out, or rounds other values in their place, can miss the bound.
Values may be sent and summed in bfloat16 or wider, within the bound.
No kernel may reach another device: no remote copies, remote signals or barrier semaphores. Data moves between devices by JAX's collectives and lax.ppermute only.
A program may use at most 64 MiB of HBM per device.

v0:
```python
import jax
import jax.numpy as jnp
from jax import lax
from jax.sharding import PartitionSpec as P

PX = 1024


def from_behind(array, axis, by):
    count = lax.axis_size(axis)
    pairs = [(i, i + by) for i in range(count) if 0 <= i + by < count]
    return lax.ppermute(array, axis, pairs)


def planar(field):
    column = lax.broadcasted_iota(jnp.int32, field.shape, 2) % PX
    zero_row = jnp.zeros(field.shape[:2] + (PX,), jnp.float32)
    zero_one = jnp.zeros(field.shape[:2] + (1,), jnp.float32)
    next_row = jnp.concatenate([field[:, :, PX:], zero_row], 2)
    next_pix = jnp.concatenate([field[:, :, 1:], zero_one], 2)
    next_pix = jnp.where(column == PX - 1, 0.0, next_pix)
    return (next_row - field, next_pix - field)


def fluxes(lower, upper):
    diff_z = upper - lower
    diff_y, diff_x = planar(lower)
    scale = jnp.sqrt(
        0.25 + jnp.sum(diff_z * diff_z + diff_y * diff_y + diff_x * diff_x, axis=1, keepdims=True)
    )
    return (diff_z / scale, diff_y / scale, diff_x / scale)


def inflow(flux_y, flux_x):
    column = lax.broadcasted_iota(jnp.int32, flux_x.shape, 2) % PX
    zero_row = jnp.zeros(flux_y.shape[:2] + (PX,), jnp.float32)
    zero_one = jnp.zeros(flux_x.shape[:2] + (1,), jnp.float32)
    prev_y = jnp.concatenate([zero_row, flux_y[:, :, :-PX]], 2)
    prev_x = jnp.concatenate([zero_one, flux_x[:, :, :-1]], 2)
    prev_x = jnp.where(column == 0, 0.0, prev_x)
    return prev_y - flux_y + (prev_x - flux_x)


def body(volume, projector, counts, atten, newton):
    slab_len = volume.shape[0]
    views_all = projector.shape[0] * lax.axis_size("view") * lax.axis_size("mat")
    x_half = volume.astype(jnp.bfloat16)
    line = jnp.einsum(
        "zmp,vup->vzmu",
        lax.all_gather(x_half, "mat", axis=0, tiled=True),
        projector,
        preferred_element_type=jnp.float32,
    )
    measured_photon_counts = counts.astype(jnp.float32)
    parts = [None] * line.shape[2]
    for energy_band_index in range(atten.shape[0]):
        exponent_attenuation = atten[energy_band_index, 0] * line[:, :, 0]
        for mat in range(1, line.shape[2]):
            exponent_attenuation = (
                exponent_attenuation + atten[energy_band_index, mat] * line[:, :, mat]
            )
        forward_difference = measured_photon_counts[:, :, energy_band_index] - jnp.exp(
            -exponent_attenuation
        )
        for mat in range(line.shape[2]):
            term = atten[energy_band_index, mat] * forward_difference
            parts[mat] = term if parts[mat] is None else parts[mat] + term
    resid = jnp.stack(parts, 2).astype(jnp.bfloat16)
    partial_rows = jnp.einsum("vzmu,vup->zmp", resid, projector, preferred_element_type=jnp.float32)
    total = lax.psum(partial_rows, ("view", "mat"))
    own = lax.dynamic_slice_in_dim(total, lax.axis_index("mat") * slab_len, slab_len, 0)
    grad = own * float(views_all) ** (-0.5)
    above = from_behind(volume[:1], ("row", "mat"), -1)
    upper = jnp.concatenate([volume[1:], above], 0)
    flux_z, flux_y, flux_x = fluxes(volume, upper)
    below = from_behind(flux_z[-1:], ("row", "mat"), 1)
    prev_z = jnp.concatenate([below, flux_z[:-1]], 0)
    smooth = prev_z - flux_z + inflow(flux_y, flux_x)
    step_dir = grad + 0.5 * smooth
    hess = newton.astype(jnp.float32)
    return volume - jnp.sum(hess * step_dir[:, None], axis=2)


def solution(mesh):
    in_specs = (
        P(("row", "mat"), None, None),
        P(("view", "mat"), None, None),
        P(("view", "mat"), "row", None, None),
        P(),
        P(("row", "mat"), None, None, None),
    )
    out_specs = P(("row", "mat"), None, None)
    return jax.shard_map(body, mesh=mesh, in_specs=in_specs, out_specs=out_specs, check_vma=False)
```

profile of v0, /device:TPU:8, one launch (start us, length us, event | category | flops | bytes accessed | tf_op | source)
XLA Modules:
  0.0 221.1 jit_solution(449843029183955524)
XLA Ops:
  6.5 0.0 all-reduce.6.cloned.1.call-start
  6.5 0.0 copy-start
  6.5 1.1 slice.122
  7.6 7.9 %collective-permute-start = (f32[1,3,2048]{2,0,1:T(1,128)S(1)}, f32[1,3,2048]{2,0,1:T(1,128)S(1)}, u32[]{:S(2)}, u32[]{:S(2)}) collective-permute-start(f32[1,3,2048]{2,0,1:T(1,128)S(1)} %slice.122), channel_id=1, source_target_pairs={{1,0},{2,1},{3,2},{4,3},{5,4},{6,5},{7,6},{8,7},{9,8},{10,9},{11,1... | collective-permute-start | bytes 73736 | tf_op jit(solution)/shard_map/ppermute | solution.py:12
  15.5 1.8 fusion.24
  17.3 1.0 copy_convert_fusion
  18.4 0.9 slice.121
  19.3 1.0 slice.124
  20.4 0.9 slice.123
  21.3 0.0 collective-permute-done
  21.3 1.1 add_reduce_fusion
  22.4 1.1 fusion.15
  23.5 13.5 %all_gather.3 = bf16[32,3,2048]{2,0,1:T(8,128)(2,1)S(1)} all-gather(bf16[8,3,2048]{2,0,1:T(8,128)(2,1)S(1)} %get-tuple-element.15), channel_id=1, replica_groups=mesh['view'=8,'row'=16,'mat'=4] {'mat'}, dimensions={0}, use_global_device_ids=true | all-gather | bytes 491520 | tf_op jit(solution)/shard_map/all_gather | solution.py:50
  37.0 0.0 copy-done
  37.0 1.4 fusion.4
  38.5 7.6 %fusion.16 = (bf16[32,1,1024]{2,0,1:T(8,128)(2,1)S(1)}, f32[1,32,1,1024]{3,1,2,0:T(8,128)S(1)}, f32[1,32,1,1024]{3,1,2,0:T(8,128)S(1)}, f32[1,32,1,1024]{3,1,2,0:T(8,128)S(1)}, f32[1,32,1,1024]{3,1,2,0:T(8,128)S(1)}) fusion(f32[]{:T(128)} %bitcast.14, f32[]{:T(128)} %bitcast.11, f32[]{:T(128)} %bitcast.8, f32[]{:T(128)} %bitcast, ...), kind=kLoop, calls=%fused_computation.32 | loop fusion | flops 1179648 | bytes 1507376 | tf_op jit(solution)/shard_map/stack | solution.py:68
  46.1 5.2 %fusion.17 = (bf16[32,1,1024]{2,0,1:T(8,128)(2,1)S(1)}, bf16[32,1,1024]{2,0,1:T(8,128)(2,1)S(1)}) fusion(f32[1,32,1,1024]{3,1,2,0:T(8,128)S(1)} %get-tuple-element.9, f32[1,32,1,1024]{3,1,2,0:T(8,128)S(1)} %get-tuple-element.8, f32[1,32,1,1024]{3,1,2,0:T(8,128)S(1)} %get-tuple-element.7, f32[1,32,1,1024]{3,1,2,0:T(8,128)S(1)} %get-tuple-element.6, ...), kind=kLoop, calls=%fused_computation.33 | loop fusion | flops 524288 | bytes 655392 | tf_op jit(solution)/shard_map/stack | solution.py:68
  51.3 0.0 copy-start.2
  51.3 0.0 copy-start.1
  51.3 1.7 fusion
  53.0 0.0 all-reduce.6.cloned.1.call-update
  53.1 1.9 collective-permute-start.1
  55.0 3.8 %collective-permute-done.1 = f32[1,3,2048]{2,0,1:T(1,128)S(1)} collective-permute-done((f32[1,3,2048]{2,0,1:T(1,128)S(1)}, f32[1,3,2048]{2,0,1:T(1,128)S(1)}, u32[]{:S(2)}, u32[]{:S(2)}) %collective-permute-start.1) | collective-permute-done | bytes 24608 | tf_op jit(solution)/shard_map/ppermute | solution.py:12
  58.8 153.6 %all-reduce.6.cloned.1.call-done = f32[32,3,2048]{2,0,1:T(8,128)} async-done(((f32[32,3,2048]{2,0,1:T(8,128)}), f32[32,3,2048]{2,0,1:T(8,128)}) %all-reduce.6.cloned.1.call-update) | async-done | bytes 786448 | tf_op jit(solution)/shard_map/psum | solution.py:70
  212.4 1.1 fusion.14
  213.5 0.0 copy-done.2
  213.5 0.1 multiply_reduce_fusion
  213.6 0.0 copy-done.1
  213.6 0.7 sub.71
  (5 shorter events, 0.1 us)
Async XLA Ops:
  6.5 205.8 %all-reduce.6.cloned.1.call-start = ((), (), s32[]{:S(2)}) async-start(), calls=%async_computation | async-start | bytes 1572864 | tf_op jit(solution)/shard_map/psum | solution.py:70
  6.5 30.5 %copy-start = (bf16[1,1024,2048]{2,1,0:T(8,128)(2,1)S(1)}, bf16[1,1024,2048]{2,1,0:T(8,128)(2,1)}, u32[]{:S(2)}) copy-start(bf16[1,1024,2048]{2,1,0:T(8,128)(2,1)} %param.6) | copy-start | bytes 12582916
  7.6 13.6 %collective-permute-start = (f32[1,3,2048]{2,0,1:T(1,128)S(1)}, f32[1,3,2048]{2,0,1:T(1,128)S(1)}, u32[]{:S(2)}, u32[]{:S(2)}) collective-permute-start(f32[1,3,2048]{2,0,1:T(1,128)S(1)} %slice.122), channel_id=1, source_target_pairs={{1,0},{2,1},{3,2},{4,3},{5,4},{6,5},{7,6},{8,7},{9,8},{10,9},{11,1... | collective-permute-start | bytes 73736 | tf_op jit(solution)/shard_map/ppermute | solution.py:12
  51.3 162.2 %copy-start.2 = (bf16[8,3,3,2048]{3,0,2,1:T(8,128)(2,1)S(1)}, bf16[8,3,3,2048]{3,0,2,1:T(8,128)(2,1)}, u32[]{:S(2)}) copy-start(bf16[8,3,3,2048]{3,0,2,1:T(8,128)(2,1)} %param.9) | copy-start | bytes 884740
  51.3 162.3 %copy-start.1 = (f32[8,3,2048]{2,0,1:T(8,128)S(1)}, f32[8,3,2048]{2,0,1:T(8,128)}, u32[]{:S(2)}) copy-start(f32[8,3,2048]{2,0,1:T(8,128)} %param.5) | copy-start | bytes 589828
  53.1 5.7 %collective-permute-start.1 = (f32[1,3,2048]{2,0,1:T(1,128)S(1)}, f32[1,3,2048]{2,0,1:T(1,128)S(1)}, u32[]{:S(2)}, u32[]{:S(2)}) collective-permute-start(f32[1,3,2048]{2,0,1:T(1,128)S(1)} %slice.136), channel_id=1, source_target_pairs={{0,1},{1,2},{2,3},{3,4},{4,5},{5,6},{6,7},{7,8},{8,9},{9,10},{10,1... | collective-permute-start | bytes 73736 | tf_op jit(solution)/shard_map/ppermute | solution.py:12
Sparse Core Ops, SparseCore 0:
  53.2 159.1 all-reduce.5
where the time goes:
time: 222 us; the launch traced here: 221 us
  waiting for transfers between devices  157 us (71%)
  other arithmetic  17.9 us (8%)
  blocking collectives  13.5 us (6%)
  between operations  13.5 us (6%)
  starting transfers between devices  9.79 us (4%)
  local copies, waits for them, and re-layouts  5.83 us (3%)
  matrix products  3.16 us (1%)
    psum x1, waiting for transfers between devices, body(): total = lax.psum(partial_rows, ('view', 'mat'))  154 us
    all_gather x1, blocking collectives, body(): lax.all_gather(x_half, 'mat', axis=0, tiled=True)  13.5 us
    another operation x2, other arithmetic, body(): resid = jnp.stack(parts, 2).astype(jnp.bfloat16)  12.8 us
    ppermute x2, starting transfers between devices, from_behind(): return lax.ppermute(array, axis, pairs)  9.78 us
  transfers between devices with their start and end apart: 3, of which 2 were waited for; matrix products, arithmetic and copies ran while one was open for 3% of the time, Pallas kernels for 0%

commit v1 on v0

v1 whole, which is shorter than its diff:
```python
import functools

import jax
import jax.numpy as jnp
from jax import lax
from jax.experimental import pallas as pl
from jax.experimental.pallas import tpu as pltpu
from jax.sharding import PartitionSpec as P

PX = 1024
BF16 = jnp.bfloat16
F32 = jnp.float32
VMEM = pl.BlockSpec(memory_space=pltpu.VMEM)
SMEM = pl.BlockSpec(memory_space=pltpu.SMEM)
LIMIT = 40 * 1024 * 1024


def project_kernel(mats, bins, slabs, atten_ref, x_ref, proj_ref, counts_ref, out_ref, resid_ref):
    rows, pix = x_ref.shape
    cols = proj_ref.shape[0]
    per_slab = rows // slabs
    depth = per_slab // mats
    wide = 256
    for at in range(0, cols, wide):
        line = lax.dot_general(
            x_ref[...], proj_ref[at : at + wide, :], (((1,), (1,)), ((), ())), preferred_element_type=F32
        )
        blocks = []
        for slab in range(slabs):
            lines = [line[slab * per_slab + m * depth :][:depth] for m in range(mats)]
            parts = [None] * mats
            for b in range(bins):
                power = atten_ref[b, 0] * lines[0]
                for m in range(1, mats):
                    power = power + atten_ref[b, m] * lines[m]
                seen = counts_ref[b, slab * depth : (slab + 1) * depth, at : at + wide]
                diff = seen - jnp.exp(-power)
                for m in range(mats):
                    term = atten_ref[b, m] * diff
                    parts[m] = term if parts[m] is None else parts[m] + term
            blocks += parts
        resid_ref[:, at : at + wide] = jnp.concatenate(blocks, 0).astype(BF16)
    owners = out_ref.shape[0]
    span = pix // owners
    for owner in range(owners):
        back = jnp.dot(
            resid_ref[...], proj_ref[:, owner * span : (owner + 1) * span], preferred_element_type=F32
        )
        for slab in range(slabs):
            out_ref[owner, slab] = back[slab * per_slab : (slab + 1) * per_slab].astype(BF16)


def project(atten, x_all, projector, counts, owners, slabs, mats):
    rows, pix = x_all.shape
    cols = projector.shape[0]
    return pl.pallas_call(
        functools.partial(project_kernel, mats, counts.shape[0], slabs),
        out_shape=jax.ShapeDtypeStruct((owners, slabs, rows // slabs, pix // owners), BF16),
        in_specs=[SMEM, VMEM, VMEM, VMEM],
        out_specs=VMEM,
        scratch_shapes=[pltpu.VMEM((rows, cols), BF16)],
        compiler_params=pltpu.CompilerParams(vmem_limit_bytes=LIMIT),
        cost_estimate=pl.CostEstimate(
            flops=4 * rows * cols * pix, bytes_accessed=2 * cols * pix, transcendentals=rows * cols
        ),
    )(atten, x_all, projector, counts)


def next_pixel(field):
    column = lax.broadcasted_iota(jnp.int32, field.shape, 1) % PX
    return jnp.where(column == PX - 1, 0.0, pltpu.roll(field, field.shape[1] - 1, 1))


def next_row(field):
    return jnp.concatenate([field[:, PX:], jnp.zeros((field.shape[0], PX), F32)], 1)


def prev_pixel(flux):
    column = lax.broadcasted_iota(jnp.int32, flux.shape, 1) % PX
    return jnp.where(column == 0, 0.0, pltpu.roll(flux, 1, 1))


def prev_row(flux):
    return jnp.concatenate([jnp.zeros((flux.shape[0], PX), F32), flux[:, :-PX]], 1)


def smooth_kernel(where_ref, vol_ref, x_ref, edge_ref, out_ref):
    mats, depth, pix = vol_ref.shape
    slabs = x_ref.shape[0] // (mats * depth)
    slab, first = where_ref[0], where_ref[1]
    row = lax.broadcasted_iota(jnp.int32, (depth, pix), 0)
    vol, above, below = [], [], []
    for m in range(mats):
        vol.append(vol_ref[m])
        up = down = edge_ref[m : m + 1]
        for other in range(1, slabs):
            at = (other * mats + m) * depth
            up = jnp.where(slab == other - 1, x_ref[at : at + depth].astype(F32)[:1], up)
            at = ((other - 1) * mats + m) * depth
            down = jnp.where(slab == other, x_ref[at : at + depth].astype(F32)[-1:], down)
        above.append(jnp.where(row == depth - 1, up, pltpu.roll(vol[m], depth - 1, 0)))
        below.append(down)
    square = jnp.full((depth, pix), 0.25, F32)
    square_below = jnp.full((1, pix), 0.25, F32)
    diffs, steps = [], []
    for m in range(mats):
        dz, dy, dx = above[m] - vol[m], next_row(vol[m]) - vol[m], next_pixel(vol[m]) - vol[m]
        square = square + (dz * dz + dy * dy + dx * dx)
        diffs.append((dz, dy, dx))
        dz, dy, dx = vol[m][:1] - below[m], next_row(below[m]) - below[m], next_pixel(below[m]) - below[m]
        square_below = square_below + (dz * dz + dy * dy + dx * dx)
        steps.append(dz)
    scale = lax.rsqrt(square)
    scale_below = jnp.where(first == 1, 0.0, lax.rsqrt(square_below))
    for m in range(mats):
        qz, qy, qx = (d * scale for d in diffs[m])
        prev_z = jnp.where(row == 0, steps[m] * scale_below, pltpu.roll(qz, 1, 0))
        out_ref[m] = prev_z - qz + (prev_row(qy) - qy) + (prev_pixel(qx) - qx)


def smooth(where, volume, x_all, edge):
    return pl.pallas_call(
        smooth_kernel,
        out_shape=jax.ShapeDtypeStruct(volume.shape, F32),
        in_specs=[SMEM, VMEM, VMEM, VMEM],
        out_specs=VMEM,
        compiler_params=pltpu.CompilerParams(vmem_limit_bytes=LIMIT),
        cost_estimate=pl.CostEstimate(
            flops=40 * volume.size, bytes_accessed=12 * volume.size, transcendentals=volume.size
        ),
    )(where, volume, x_all, edge)


def total_kernel(factor, part_ref, out_ref):
    total = jnp.sum(part_ref[...].astype(F32), axis=0) * factor
    total = total.astype(BF16)
    for copy in range(out_ref.shape[0]):
        out_ref[copy] = total


def total_copies(parts, factor, copies):
    return pl.pallas_call(
        functools.partial(total_kernel, factor),
        out_shape=jax.ShapeDtypeStruct((copies,) + parts.shape[1:], BF16),
        in_specs=[VMEM],
        out_specs=VMEM,
        compiler_params=pltpu.CompilerParams(vmem_limit_bytes=LIMIT),
    )(parts)


def step_kernel(grad_ref, smooth_ref, newton_ref, vol_ref, out_ref):
    mats, depth, pix = vol_ref.shape
    span = grad_ref.shape[2]
    for owner in range(grad_ref.shape[0]):
        own = slice(owner * span, (owner + 1) * span)
        grad = grad_ref[owner].astype(F32)
        steps = [grad[k * depth : (k + 1) * depth] + 0.5 * smooth_ref[k, :, own] for k in range(mats)]
        for m in range(mats):
            moved = newton_ref[m, 0, :, own].astype(F32) * steps[0]
            for k in range(1, mats):
                moved = moved + newton_ref[m, k, :, own].astype(F32) * steps[k]
            out_ref[m, :, own] = vol_ref[m, :, own] - moved


def newton_step(grad, smoothed, newton, volume):
    return pl.pallas_call(
        step_kernel,
        out_shape=jax.ShapeDtypeStruct(volume.shape, F32),
        in_specs=[VMEM] * 4,
        out_specs=VMEM,
        compiler_params=pltpu.CompilerParams(vmem_limit_bytes=LIMIT),
    )(grad, smoothed, newton, volume)


def body(volume, projector, counts, atten, newton):
    depth, mats, pix = volume.shape
    owners, slabs, groups = (lax.axis_size(name) for name in ("view", "mat", "row"))
    views_all = projector.shape[0] * owners * slabs
    slab, group = lax.axis_index("mat"), lax.axis_index("row")
    vol = volume.transpose(1, 0, 2)
    x_all = lax.all_gather(vol.astype(BF16).reshape(mats * depth, pix), "mat", axis=0, tiled=True)
    counts_binned = counts[0].astype(F32).transpose(1, 0, 2)
    parts = project(atten, x_all, projector[0], counts_binned, owners, slabs, mats)
    parts = parts.reshape(owners * slabs, mats * depth, pix // owners)
    parts = lax.all_to_all(parts, ("view", "mat"), 0, 0, tiled=True)
    mine = total_copies(parts, float(views_all) ** (-0.5), owners)
    grad = lax.all_to_all(mine, "view", 0, 0, tiled=True)
    edge = jnp.where(slab == 0, vol[:, 0], vol[:, -1])
    pairs = []
    for g in range(groups - 1):
        last, start = g * slabs + slabs - 1, (g + 1) * slabs
        pairs += [(last, start), (start, last)]
    edge = lax.ppermute(edge, ("row", "mat"), pairs)
    is_first = jnp.logical_and(slab == 0, group == 0).astype(jnp.int32)
    smoothed = smooth(jnp.stack([slab, is_first]).astype(jnp.int32), vol, x_all, edge)
    updated = newton_step(grad, smoothed, newton.transpose(1, 2, 0, 3), vol)
    return updated.transpose(1, 0, 2)


def solution(mesh):
    in_specs = (
        P(("row", "mat"), None, None),
        P(("view", "mat"), None, None),
        P(("view", "mat"), "row", None, None),
        P(),
        P(("row", "mat"), None, None, None),
    )
    out_specs = P(("row", "mat"), None, None)
    return jax.shard_map(body, mesh=mesh, in_specs=in_specs, out_specs=out_specs, check_vma=False)
```

time: 222 us -> 62.8 us (0.28)
  the two profiles are of different devices: /device:TPU:8 before, /device:TPU:448 now
where the time goes in v1:
time: 62.8 us; the launch traced here: 62.1 us
  waiting for transfers between devices  19.1 us (30%)
  starting transfers between devices  17 us (27%)
  blocking collectives  14.9 us (24%)
  Pallas kernels  5.95 us (9%)
  local copies, waits for them, and re-layouts  2.89 us (5%)
  other arithmetic  2.12 us (3%)
    all_gather x1, blocking collectives, body(): lax.all_gather(vol.astype(BF16).reshape(mats * depth, pix), 'mat', axis=0...  14.9 us
    all_to_all x1, waiting for transfers between devices, body(): parts = lax.all_to_all(parts, ('view', 'mat'), 0, 0, tiled=True)  11.6 us
    all_to_all x1, starting transfers between devices, body(): parts = lax.all_to_all(parts, ('view', 'mat'), 0, 0, tiled=True)  10.1 us
    ppermute x1, waiting for transfers between devices, body(): edge = lax.ppermute(edge, ('row', 'mat'), pairs)  5.92 us
    all_to_all x1, starting transfers between devices, body(): grad = lax.all_to_all(mine, 'view', 0, 0, tiled=True)  5.01 us
    pallas_call x1, Pallas kernels, project(): pl.pallas_call(functools.partial(project_kernel, mats, counts.shape[0], s...  3.6 us
    unnamed x9, local copies, waits for them, and re-layouts  2.89 us
    ppermute x1, starting transfers between devices, body(): edge = lax.ppermute(edge, ('row', 'mat'), pairs)  1.92 us
  transfers between devices with their start and end apart: 3, of which 3 were waited for; matrix products, arithmetic and copies ran while one was open for 0% of the time, Pallas kernels for 1%

profile of v1, /device:TPU:448, one launch (start us, length us, event | category | flops | bytes accessed | tf_op | source)
XLA Modules:
  0.0 62.1 jit_solution(7953987272566710832)
XLA Ops:
  0.0 0.9 %convert_bitcast_fusion.1 = bf16[24,2048]{1,0:T(8,128)(2,1)S(1)} fusion(f32[8,3,2048]{2,0,1:T(8,128)} %param.5), kind=kLoop, calls=%fused_computation.1 | loop fusion | flops 49152 | bytes 294912 | tf_op jit(solution)/shard_map/reshape | solution.py:181
  0.9 0.0 copy-start.1
  1.0 14.9 %all_gather.3.x_ref = bf16[96,2048]{1,0:T(8,128)(2,1)S(1)} all-gather(bf16[24,2048]{1,0:T(8,128)(2,1)S(1)} %convert_bitcast_fusion.1), channel_id=1, replica_groups=mesh['view'=8,'row'=16,'mat'=4] {'mat'}, dimensions={0}, use_global_device_ids=true | all-gather | bytes 491520 | tf_op jit(solution)/shard_map/all_gather | solution.py:181
  15.9 0.0 copy-start.2
  15.9 1.1 %convert_bitcast_fusion.counts_ref = f32[4,32,1024]{2,1,0:T(8,128)S(1)} fusion(bf16[1,32,4,1024]{3,2,1,0:T(4,128)(2,1)} %param.7), kind=kLoop, calls=%fused_computation | loop fusion | flops 131072 | bytes 786432 | tf_op jit(solution)/shard_map/transpose | solution.py:182
  17.0 0.0 copy-start
  17.0 2.2 %copy-done = bf16[1,1024,2048]{2,1,0:T(8,128)(2,1)S(1)} copy-done((bf16[1,1024,2048]{2,1,0:T(8,128)(2,1)S(1)}, bf16[1,1024,2048]{2,1,0:T(8,128)(2,1)}, u32[]{:S(2)}) %copy-start) | copy-done | bytes 4194328
  19.2 0.0 copy-start.3
  19.2 0.7 %copy-done.3 = f32[4,3]{1,0:T(4,128)S(1)} copy-done((f32[4,3]{1,0:T(4,128)S(1)}, f32[4,3]{1,0:T(4,128)}, u32[]{:S(2)}) %copy-start.3) | copy-done | bytes 72
  19.8 3.6 %shard_map.55 = bf16[8,4,24,256]{3,2,1,0:T(8,128)(2,1)} custom-call(f32[4,3]{1,0:T(4,128)S(1)} %copy-done.3, bf16[96,2048]{1,0:T(8,128)(2,1)S(1)} %all_gather.3.x_ref, bf16[1024,2048]{1,0:T(8,128)(2,1)S(1)} %bitcast.18, f32[4,32,1024]{2,1,0:T(8,128)S(1)} %convert_bitcast_fusion.counts_ref), custom_call_target="tpu_custom_call" | custom-call | flops 805306368 | bytes 4194304 | tf_op jit(solution)/shard_map/pallas_call | solution.py:56
  23.4 10.1 %all-to-all-start = ((bf16[32,24,256]{2,1,0:T(8,128)(2,1)}), bf16[32,24,256]{2,1,0:T(8,128)(2,1)S(1)}, u32[]{:S(2)}, u32[]{:S(2)}) async-start(bf16[32,24,256]{2,1,0:T(8,128)(2,1)} %bitcast.5), calls=%async_computation | async-start | bytes 786432 | tf_op jit(solution)/shard_map/all_to_all | solution.py:185
  33.6 11.6 %all-to-all-done.part_ref = bf16[32,24,256]{2,1,0:T(8,128)(2,1)S(1)} async-done(((bf16[32,24,256]{2,1,0:T(8,128)(2,1)}), bf16[32,24,256]{2,1,0:T(8,128)(2,1)S(1)}, u32[]{:S(2)}, u32[]{:S(2)}) %all-to-all-start) | async-done | bytes 393248 | tf_op jit(solution)/shard_map/all_to_all | solution.py:185
  45.1 0.7 %shard_map.56 = bf16[8,24,256]{2,1,0:T(8,128)(2,1)} custom-call(bf16[32,24,256]{2,1,0:T(8,128)(2,1)S(1)} %all-to-all-done.part_ref), custom_call_target="tpu_custom_call" | custom-call | tf_op jit(solution)/shard_map/pallas_call | solution.py:142
  45.8 5.0 %all-to-all-start.1 = ((bf16[8,24,256]{2,1,0:T(8,128)(2,1)}), bf16[8,24,256]{2,1,0:T(8,128)(2,1)S(1)}, u32[]{:S(2)}, u32[]{:S(2)}) async-start(bf16[8,24,256]{2,1,0:T(8,128)(2,1)} %shard_map.56), calls=%async_computation.1 | async-start | bytes 196608 | tf_op jit(solution)/shard_map/all_to_all | solution.py:187
  50.8 0.0 copy-done.1
  50.9 1.9 %collective-permute-start = (f32[3,2048]{1,0:T(4,128)S(1)}, f32[3,2048]{1,0:T(4,128)S(1)}, u32[]{:S(2)}, u32[]{:S(2)}) collective-permute-start(f32[3,2048]{1,0:T(4,128)S(1)} %bitcast.23), channel_id=1, source_target_pairs={{3,4},{4,3},{7,8},{8,7},{11,12},{12,11},{15,16},{16,15},{19,20},{2... | collective-permute-start | bytes 73736 | tf_op jit(solution)/shard_map/ppermute | solution.py:193
  52.8 0.1 pad_add_fusion.where_ref
  52.9 5.9 %collective-permute-done.edge_ref = f32[3,2048]{1,0:T(4,128)S(1)} collective-permute-done((f32[3,2048]{1,0:T(4,128)S(1)}, f32[3,2048]{1,0:T(4,128)S(1)}, u32[]{:S(2)}, u32[]{:S(2)}) %collective-permute-start) | collective-permute-done | bytes 24608 | tf_op jit(solution)/shard_map/ppermute | solution.py:193
  58.8 0.9 %shard_map.57.smooth_ref = f32[3,8,2048]{2,1,0:T(8,128)S(1)} custom-call(s32[2]{0:T(128)S(1)} %pad_add_fusion.where_ref, f32[3,8,2048]{2,1,0:T(8,128)S(1)} %bitcast.20, bf16[96,2048]{1,0:T(8,128)(2,1)S(1)} %all_gather.3.x_ref, f32[3,2048]{1,0:T(4,128)S(1)} %collective-permute-done.edge_ref), custom_call_target="tpu_custom_call" | custom-call | flops 1966080 | bytes 589824 | tf_op jit(solution)/shard_map/pallas_call | solution.py:122
  59.7 1.7 %all-to-all-done.1.grad_ref = bf16[8,24,256]{2,1,0:T(8,128)(2,1)S(1)} async-done(((bf16[8,24,256]{2,1,0:T(8,128)(2,1)}), bf16[8,24,256]{2,1,0:T(8,128)(2,1)S(1)}, u32[]{:S(2)}, u32[]{:S(2)}) %all-to-all-start.1) | async-done | bytes 98336 | tf_op jit(solution)/shard_map/all_to_all | solution.py:187
  61.4 0.0 copy-done.2
  61.4 0.8 %shard_map.58 = f32[3,8,2048]{2,1,0:T(8,128)} custom-call(bf16[8,24,256]{2,1,0:T(8,128)(2,1)S(1)} %all-to-all-done.1.grad_ref, f32[3,8,2048]{2,1,0:T(8,128)S(1)} %shard_map.57.smooth_ref, bf16[3,3,8,2048]{3,2,1,0:T(8,128)(2,1)S(1)} %bitcast.22, f32[3,8,2048]{2,1,0:T(8,128)S(1)} %bitcast.21), custom_call_target="tpu_custom_call" | custom-call | tf_op jit(solution)/shard_map/pallas_call | solution.py:166
  (2 shorter events, 0.0 us)
Async XLA Ops:
  0.9 49.9 %copy-start.1 = (f32[8,3,2048]{2,0,1:T(8,128)S(1)}, f32[8,3,2048]{2,0,1:T(8,128)}, u32[]{:S(2)}) copy-start(f32[8,3,2048]{2,0,1:T(8,128)} %param.5) | copy-start | bytes 589828
  15.9 45.5 %copy-start.2 = (bf16[8,3,3,2048]{3,0,2,1:T(8,128)(2,1)S(1)}, bf16[8,3,3,2048]{3,0,2,1:T(8,128)(2,1)}, u32[]{:S(2)}) copy-start(bf16[8,3,3,2048]{3,0,2,1:T(8,128)(2,1)} %param.9) | copy-start | bytes 884740
  17.0 2.2 %copy-start = (bf16[1,1024,2048]{2,1,0:T(8,128)(2,1)S(1)}, bf16[1,1024,2048]{2,1,0:T(8,128)(2,1)}, u32[]{:S(2)}) copy-start(bf16[1,1024,2048]{2,1,0:T(8,128)(2,1)} %param.6) | copy-start | bytes 12582916
  19.2 0.7 %copy-start.3 = (f32[4,3]{1,0:T(4,128)S(1)}, f32[4,3]{1,0:T(4,128)}, u32[]{:S(2)}) copy-start(f32[4,3]{1,0:T(4,128)} %atten_ref.1) | copy-start | bytes 148
  23.4 21.7 %all-to-all-start = ((bf16[32,24,256]{2,1,0:T(8,128)(2,1)}), bf16[32,24,256]{2,1,0:T(8,128)(2,1)S(1)}, u32[]{:S(2)}, u32[]{:S(2)}) async-start(bf16[32,24,256]{2,1,0:T(8,128)(2,1)} %bitcast.5), calls=%async_computation | async-start | bytes 786432 | tf_op jit(solution)/shard_map/all_to_all | solution.py:185
  45.8 15.6 %all-to-all-start.1 = ((bf16[8,24,256]{2,1,0:T(8,128)(2,1)}), bf16[8,24,256]{2,1,0:T(8,128)(2,1)S(1)}, u32[]{:S(2)}, u32[]{:S(2)}) async-start(bf16[8,24,256]{2,1,0:T(8,128)(2,1)} %shard_map.56), calls=%async_computation.1 | async-start | bytes 196608 | tf_op jit(solution)/shard_map/all_to_all | solution.py:187
  50.9 7.9 %collective-permute-start = (f32[3,2048]{1,0:T(4,128)S(1)}, f32[3,2048]{1,0:T(4,128)S(1)}, u32[]{:S(2)}, u32[]{:S(2)}) collective-permute-start(f32[3,2048]{1,0:T(4,128)S(1)} %bitcast.23), channel_id=1, source_target_pairs={{3,4},{4,3},{7,8},{8,7},{11,12},{12,11},{15,16},{16,15},{19,20},{2... | collective-permute-start | bytes 73736 | tf_op jit(solution)/shard_map/ppermute | solution.py:193

commit v2 on v1

--- a/solution.py
+++ b/solution.py
@@ -12,58 +12,113 @@
 F32 = jnp.float32
 VMEM = pl.BlockSpec(memory_space=pltpu.VMEM)
 SMEM = pl.BlockSpec(memory_space=pltpu.SMEM)
-LIMIT = 40 * 1024 * 1024
-
-
-def project_kernel(mats, bins, slabs, atten_ref, x_ref, proj_ref, counts_ref, out_ref, resid_ref):
+SMALL = 8 * 1024 * 1024
+LARGE = 52 * 1024 * 1024
+
+
+def spread_kernel(vol_ref, out_ref):
+    mats, depth, _ = vol_ref.shape
+    rounded = jnp.concatenate([vol_ref[m] for m in range(mats)], 0).astype(BF16)
+    for copy in range(out_ref.shape[0]):
+        out_ref[copy] = rounded
+
+
+def spread(volume, copies):
+    mats, depth, pix = volume.shape
+    return pl.pallas_call(
+        spread_kernel,
+        out_shape=jax.ShapeDtypeStruct((copies, mats * depth, pix), BF16),
+        in_specs=[VMEM],
+        out_specs=VMEM,
+        compiler_params=pltpu.CompilerParams(vmem_limit_bytes=SMALL),
+    )(volume)
+
+
+def tiles_kernel(atten_ref, tiles_ref):
+    bins, mats = atten_ref.shape
+    for b in range(bins):
+        for m in range(mats):
+            tiles_ref[b * mats + m] = jnp.full(tiles_ref.shape[1:], atten_ref[b, m], F32)
+
+
+def attenuation_tiles(atten):
+    return pl.pallas_call(
+        tiles_kernel,
+        out_shape=jax.ShapeDtypeStruct((atten.size, 8, 128), F32),
+        in_specs=[SMEM],
+        out_specs=VMEM,
+        compiler_params=pltpu.CompilerParams(vmem_limit_bytes=SMALL),
+    )(atten)
+
+
+def wide_tile(tile, wide):
+    return jnp.concatenate([tile] * (wide // tile.shape[1]), 1)
+
+
+def project_kernel(mats, bins, slabs, tiles_ref, x_ref, proj_ref, counts_ref, out_ref, resid_ref, near_ref, sems):
     rows, pix = x_ref.shape
     cols = proj_ref.shape[0]
     per_slab = rows // slabs
     depth = per_slab // mats
-    wide = 256
+    wide = cols // sems.shape[0]
+    copies_in = [
+        pltpu.make_async_copy(
+            proj_ref.at[at : at + wide], near_ref.at[at : at + wide], sems.at[at // wide]
+        )
+        for at in range(0, cols, wide)
+    ]
+    for copy_in in copies_in:
+        copy_in.start()
+    atten = [[wide_tile(tiles_ref[b * mats + m], wide) for m in range(mats)] for b in range(bins)]
     for at in range(0, cols, wide):
+        copies_in[at // wide].wait()
         line = lax.dot_general(
-            x_ref[...], proj_ref[at : at + wide, :], (((1,), (1,)), ((), ())), preferred_element_type=F32
+            x_ref[...], near_ref[at : at + wide, :], (((1,), (1,)), ((), ())), preferred_element_type=F32
         )
         blocks = []
         for slab in range(slabs):
             lines = [line[slab * per_slab + m * depth :][:depth] for m in range(mats)]
             parts = [None] * mats
             for b in range(bins):
-                power = atten_ref[b, 0] * lines[0]
+                power = atten[b][0] * lines[0]
                 for m in range(1, mats):
-                    power = power + atten_ref[b, m] * lines[m]
+                    power = power + atten[b][m] * lines[m]
                 seen = counts_ref[b, slab * depth : (slab + 1) * depth, at : at + wide]
                 diff = seen - jnp.exp(-power)
                 for m in range(mats):
-                    term = atten_ref[b, m] * diff
+                    term = atten[b][m] * diff
                     parts[m] = term if parts[m] is None else parts[m] + term
             blocks += parts
         resid_ref[:, at : at + wide] = jnp.concatenate(blocks, 0).astype(BF16)
-    owners = out_ref.shape[0]
-    span = pix // owners
+    owners, copies, _, _, span = out_ref.shape
     for owner in range(owners):
         back = jnp.dot(
-            resid_ref[...], proj_ref[:, owner * span : (owner + 1) * span], preferred_element_type=F32
+            resid_ref[...], near_ref[:, owner * span : (owner + 1) * span], preferred_element_type=F32
         )
         for slab in range(slabs):
-            out_ref[owner, slab] = back[slab * per_slab : (slab + 1) * per_slab].astype(BF16)
-
-
-def project(atten, x_all, projector, counts, owners, slabs, mats):
+            part = back[slab * per_slab : (slab + 1) * per_slab].astype(BF16)
+            for copy in range(copies):
+                out_ref[owner, copy, slab] = part
+
+
+def project(tiles, x_all, projector, counts, owners, copies, slabs, mats):
     rows, pix = x_all.shape
     cols = projector.shape[0]
     return pl.pallas_call(
         functools.partial(project_kernel, mats, counts.shape[0], slabs),
-        out_shape=jax.ShapeDtypeStruct((owners, slabs, rows // slabs, pix // owners), BF16),
-        in_specs=[SMEM, VMEM, VMEM, VMEM],
-        out_specs=VMEM,
-        scratch_shapes=[pltpu.VMEM((rows, cols), BF16)],
-        compiler_params=pltpu.CompilerParams(vmem_limit_bytes=LIMIT),
+        out_shape=jax.ShapeDtypeStruct((owners, copies, slabs, rows // slabs, pix // owners), BF16),
+        in_specs=[VMEM, VMEM, pl.BlockSpec(memory_space=pltpu.HBM), VMEM],
+        out_specs=VMEM,
+        scratch_shapes=[
+            pltpu.VMEM((rows, cols), BF16),
+            pltpu.VMEM((cols, pix), BF16),
+            pltpu.SemaphoreType.DMA((4,)),
+        ],
+        compiler_params=pltpu.CompilerParams(vmem_limit_bytes=LARGE),
         cost_estimate=pl.CostEstimate(
             flops=4 * rows * cols * pix, bytes_accessed=2 * cols * pix, transcendentals=rows * cols
         ),
-    )(atten, x_all, projector, counts)
+    )(tiles, x_all, projector, counts)
 
 
 def next_pixel(field):
@@ -124,7 +179,7 @@
         out_shape=jax.ShapeDtypeStruct(volume.shape, F32),
         in_specs=[SMEM, VMEM, VMEM, VMEM],
         out_specs=VMEM,
-        compiler_params=pltpu.CompilerParams(vmem_limit_bytes=LIMIT),
+        compiler_params=pltpu.CompilerParams(vmem_limit_bytes=SMALL),
         cost_estimate=pl.CostEstimate(
             flops=40 * volume.size, bytes_accessed=12 * volume.size, transcendentals=volume.size
         ),
@@ -144,7 +199,7 @@
         out_shape=jax.ShapeDtypeStruct((copies,) + parts.shape[1:], BF16),
         in_specs=[VMEM],
         out_specs=VMEM,
-        compiler_params=pltpu.CompilerParams(vmem_limit_bytes=LIMIT),
+        compiler_params=pltpu.CompilerParams(vmem_limit_bytes=SMALL),
     )(parts)
 
 
@@ -168,23 +223,25 @@
         out_shape=jax.ShapeDtypeStruct(volume.shape, F32),
         in_specs=[VMEM] * 4,
         out_specs=VMEM,
-        compiler_params=pltpu.CompilerParams(vmem_limit_bytes=LIMIT),
+        compiler_params=pltpu.CompilerParams(vmem_limit_bytes=SMALL),
     )(grad, smoothed, newton, volume)
 
 
 def body(volume, projector, counts, atten, newton):
     depth, mats, pix = volume.shape
-    owners, slabs, groups = (lax.axis_size(name) for name in ("view", "mat", "row"))
-    views_all = projector.shape[0] * owners * slabs
+    owners, copies, slabs, groups = (lax.axis_size(name) for name in ("x", "half", "mat", "row"))
+    views_all = projector.shape[0] * owners * copies * slabs
     slab, group = lax.axis_index("mat"), lax.axis_index("row")
+    rows = mats * depth
     vol = volume.transpose(1, 0, 2)
-    x_all = lax.all_gather(vol.astype(BF16).reshape(mats * depth, pix), "mat", axis=0, tiled=True)
+    x_all = lax.all_to_all(spread(vol, slabs), "mat", 0, 0, tiled=True)
+    x_all = x_all.reshape(slabs * rows, pix)
     counts_binned = counts[0].astype(F32).transpose(1, 0, 2)
-    parts = project(atten, x_all, projector[0], counts_binned, owners, slabs, mats)
-    parts = parts.reshape(owners * slabs, mats * depth, pix // owners)
-    parts = lax.all_to_all(parts, ("view", "mat"), 0, 0, tiled=True)
+    parts = project(attenuation_tiles(atten), x_all, projector[0], counts_binned, owners, copies, slabs, mats)
+    parts = parts.reshape(owners * copies * slabs, rows, pix // owners)
+    parts = lax.all_to_all(parts, ("x", "half", "mat"), 0, 0, tiled=True)
     mine = total_copies(parts, float(views_all) ** (-0.5), owners)
-    grad = lax.all_to_all(mine, "view", 0, 0, tiled=True)
+    grad = lax.all_to_all(mine, "x", 0, 0, tiled=True)
     edge = jnp.where(slab == 0, vol[:, 0], vol[:, -1])
     pairs = []
     for g in range(groups - 1):
@@ -198,10 +255,15 @@
 
 
 def solution(mesh):
+    shape = mesh.devices.shape
+    mesh = jax.sharding.Mesh(
+        mesh.devices.reshape(shape[0] // 2, 2, *shape[1:]), ("x", "half", "row", "mat")
+    )
+    view = ("x", "half", "mat")
     in_specs = (
         P(("row", "mat"), None, None),
-        P(("view", "mat"), None, None),
-        P(("view", "mat"), "row", None, None),
+        P(view, None, None),
+        P(view, "row", None, None),
         P(),
         P(("row", "mat"), None, None, None),
     )

time: 62.8 us -> 66.6 us (1.061)
  blocking collectives: 14.9 us -> 0 us
  waiting for transfers between devices: 19.1 us -> 32.5 us
  starting transfers between devices: 17 us -> 20.6 us
  Pallas kernels: 5.95 us -> 9.51 us
  local copies, waits for them, and re-layouts: 2.89 us -> 1.63 us
  other arithmetic: 2.12 us -> 1.14 us
    all_to_all x2 -> x3, waiting for transfers between devices: 13.2 us -> 32.5 us  [the longest x1 18.3 us: body(): parts = lax.all_to_all(parts, ('x', 'half', 'mat'), 0, 0, tiled=True)]
    all_gather x1 -> x0, blocking collectives: 14.9 us -> none  [body(): lax.all_gather(vol.astype(BF16).reshape(mats * depth, pix), 'mat', axis=0...]
    ppermute x1, waiting for transfers between devices: 5.92 us -> 0.01 us  [body(): edge = lax.ppermute(edge, ('row', 'mat'), pairs)]
    pallas_call x1, Pallas kernels: 3.6 us -> 5.76 us  [project(): pl.pallas_call(functools.partial(project_kernel, mats, counts.shape[0], s...]
    all_to_all x2 -> x3, starting transfers between devices: 15.1 us -> 17 us  [the longest x1 8.8 us: body(): parts = lax.all_to_all(parts, ('x', 'half', 'mat'), 0, 0, tiled=True)]
    ppermute x1, starting transfers between devices: 1.92 us -> 3.63 us  [body(): edge = lax.ppermute(edge, ('row', 'mat'), pairs)]
    pallas_call x0 -> x2, Pallas kernels: none -> 1.35 us  [the longest x1 0.77 us: spread(): pl.pallas_call(spread_kernel, out_shape=jax.ShapeDtypeStruct((copies, mat...]
    unnamed x9, local copies, waits for them, and re-layouts: 2.89 us -> 1.63 us
  transfers between devices with their start and end apart: 3 -> 4, of which waited for: 3 -> 3; matrix products, arithmetic and copies ran while one was open for 0% -> 2% of each run, Pallas kernels for 1% -> 3%
where the time goes in v2:
time: 66.6 us; the launch traced here: 65.5 us
  waiting for transfers between devices  32.5 us (49%)
  starting transfers between devices  20.6 us (31%)
  Pallas kernels  9.51 us (14%)
  local copies, waits for them, and re-layouts  1.63 us (2%)
  other arithmetic  1.14 us (2%)
    all_to_all x1, waiting for transfers between devices, body(): parts = lax.all_to_all(parts, ('x', 'half', 'mat'), 0, 0, tiled=True)  18.3 us
    all_to_all x1, waiting for transfers between devices, body(): x_all = lax.all_to_all(spread(vol, slabs), 'mat', 0, 0, tiled=True)  9.38 us
    all_to_all x1, starting transfers between devices, body(): parts = lax.all_to_all(parts, ('x', 'half', 'mat'), 0, 0, tiled=True)  8.8 us
    pallas_call x1, Pallas kernels, project(): pl.pallas_call(functools.partial(project_kernel, mats, counts.shape[0], s...  5.76 us
    all_to_all x1, starting transfers between devices, body(): x_all = lax.all_to_all(spread(vol, slabs), 'mat', 0, 0, tiled=True)  4.87 us
    all_to_all x1, waiting for transfers between devices, body(): grad = lax.all_to_all(mine, 'x', 0, 0, tiled=True)  4.79 us
    ppermute x1, starting transfers between devices, body(): edge = lax.ppermute(edge, ('row', 'mat'), pairs)  3.63 us
    all_to_all x1, starting transfers between devices, body(): grad = lax.all_to_all(mine, 'x', 0, 0, tiled=True)  3.3 us
  transfers between devices with their start and end apart: 4, of which 3 were waited for; matrix products, arithmetic and copies ran while one was open for 2% of the time, Pallas kernels for 3%

profile of v2, /device:TPU:448, one launch (start us, length us, event | category | flops | bytes accessed | tf_op | source)
XLA Modules:
  0.0 65.5 jit_solution(16683876910086372743)
XLA Ops:
  0.0 0.0 copy-start
  0.0 0.9 %copy-done = f32[8,3,2048]{2,0,1:T(8,128)S(1)} copy-done((f32[8,3,2048]{2,0,1:T(8,128)S(1)}, f32[8,3,2048]{2,0,1:T(8,128)}, u32[]{:S(2)}) %copy-start) | copy-done | bytes 196632
  0.9 0.8 %shard_map.56 = bf16[4,24,2048]{2,1,0:T(8,128)(2,1)} custom-call(f32[3,8,2048]{2,1,0:T(8,128)S(1)} %bitcast.18), custom_call_target="tpu_custom_call" | custom-call | tf_op jit(solution)/shard_map/pallas_call | solution.py:28
  1.7 4.9 %all-to-all-start = ((bf16[4,24,2048]{2,1,0:T(8,128)(2,1)}), bf16[4,24,2048]{2,1,0:T(8,128)(2,1)S(1)}, u32[]{:S(2)}, u32[]{:S(2)}) async-start(bf16[4,24,2048]{2,1,0:T(8,128)(2,1)} %shard_map.56), calls=%async_computation | async-start | bytes 786432 | tf_op jit(solution)/shard_map/all_to_all | solution.py:237
  6.6 0.0 copy-start.3
  6.6 0.7 %copy-done.3 = f32[4,3]{1,0:T(4,128)S(1)} copy-done((f32[4,3]{1,0:T(4,128)S(1)}, f32[4,3]{1,0:T(4,128)}, u32[]{:S(2)}) %copy-start.3) | copy-done | bytes 72
  7.3 0.0 copy-start.1
  7.3 0.6 shard_map.55.tiles_ref
  7.8 1.0 %convert_bitcast_fusion.counts_ref = f32[4,32,1024]{2,1,0:T(8,128)S(1)} fusion(bf16[1,32,4,1024]{3,2,1,0:T(4,128)(2,1)} %param.7), kind=kLoop, calls=%fused_computation | loop fusion | flops 131072 | bytes 786432 | tf_op jit(solution)/shard_map/transpose | solution.py:239
  8.9 9.4 %all-to-all-done = bf16[4,24,2048]{2,1,0:T(8,128)(2,1)S(1)} async-done(((bf16[4,24,2048]{2,1,0:T(8,128)(2,1)}), bf16[4,24,2048]{2,1,0:T(8,128)(2,1)S(1)}, u32[]{:S(2)}, u32[]{:S(2)}) %all-to-all-start) | async-done | bytes 393248 | tf_op jit(solution)/shard_map/all_to_all | solution.py:237
  18.3 0.0 copy-start.2
  18.3 5.8 %shard_map.57 = bf16[4,2,4,24,512]{4,3,2,1,0:T(8,128)(2,1)} custom-call(f32[12,8,128]{2,1,0:T(8,128)S(1)} %shard_map.55.tiles_ref, bf16[96,2048]{1,0:T(8,128)(2,1)S(1)} %bitcast.16, bf16[1024,2048]{1,0:T(8,128)(2,1)} %bitcast.23, f32[4,32,1024]{2,1,0:T(8,128)S(1)} %convert_bitcast_fusion.counts_ref), custom_call_target="tpu_custom_call" | custom-call | flops 805306368 | bytes 4194304 | tf_op jit(solution)/shard_map/pallas_call | solution.py:107
  24.0 8.8 %all-to-all-start.1 = ((bf16[32,24,512]{2,1,0:T(8,128)(2,1)}), bf16[32,24,512]{2,1,0:T(8,128)(2,1)S(1)}, u32[]{:S(2)}, u32[]{:S(2)}) async-start(bf16[32,24,512]{2,1,0:T(8,128)(2,1)} %bitcast.5), calls=%async_computation.1 | async-start | bytes 1572864 | tf_op jit(solution)/shard_map/all_to_all | solution.py:242
  32.8 0.0 copy-done.1
  32.9 3.6 %collective-permute-start = (f32[3,2048]{1,0:T(4,128)S(1)}, f32[3,2048]{1,0:T(4,128)S(1)}, u32[]{:S(2)}, u32[]{:S(2)}) collective-permute-start(f32[3,2048]{1,0:T(4,128)S(1)} %bitcast.24), channel_id=1, source_target_pairs={{3,4},{4,3},{7,8},{8,7},{11,12},{12,11},{15,16},{16,15},{19,20},{2... | collective-permute-start | bytes 73736 | tf_op jit(solution)/shard_map/ppermute | solution.py:250
  36.6 18.3 %all-to-all-done.1.part_ref = bf16[32,24,512]{2,1,0:T(8,128)(2,1)S(1)} async-done(((bf16[32,24,512]{2,1,0:T(8,128)(2,1)}), bf16[32,24,512]{2,1,0:T(8,128)(2,1)S(1)}, u32[]{:S(2)}, u32[]{:S(2)}) %all-to-all-start.1) | async-done | bytes 786464 | tf_op jit(solution)/shard_map/all_to_all | solution.py:242
  54.9 0.8 %shard_map.58 = bf16[4,24,512]{2,1,0:T(8,128)(2,1)} custom-call(bf16[32,24,512]{2,1,0:T(8,128)(2,1)S(1)} %all-to-all-done.1.part_ref), custom_call_target="tpu_custom_call" | custom-call | tf_op jit(solution)/shard_map/pallas_call | solution.py:197
  55.6 3.3 %all-to-all-start.2 = ((bf16[4,24,512]{2,1,0:T(8,128)(2,1)}), bf16[4,24,512]{2,1,0:T(8,128)(2,1)S(1)}, u32[]{:S(2)}, u32[]{:S(2)}) async-start(bf16[4,24,512]{2,1,0:T(8,128)(2,1)} %shard_map.58), calls=%async_computation.2 | async-start | bytes 196608 | tf_op jit(solution)/shard_map/all_to_all | solution.py:244
  58.9 0.1 pad_add_fusion.where_ref
  59.0 0.0 collective-permute-done.edge_ref
  59.0 0.9 %shard_map.59.smooth_ref = f32[3,8,2048]{2,1,0:T(8,128)S(1)} custom-call(s32[2]{0:T(128)S(1)} %pad_add_fusion.where_ref, f32[3,8,2048]{2,1,0:T(8,128)S(1)} %bitcast.20, bf16[96,2048]{1,0:T(8,128)(2,1)S(1)} %bitcast.17, f32[3,2048]{1,0:T(4,128)S(1)} %collective-permute-done.edge_ref), custom_call_target="tpu_custom_call" | custom-call | flops 1966080 | bytes 589824 | tf_op jit(solution)/shard_map/pallas_call | solution.py:177
  59.9 4.8 %all-to-all-done.2.grad_ref = bf16[4,24,512]{2,1,0:T(8,128)(2,1)S(1)} async-done(((bf16[4,24,512]{2,1,0:T(8,128)(2,1)}), bf16[4,24,512]{2,1,0:T(8,128)(2,1)S(1)}, u32[]{:S(2)}, u32[]{:S(2)}) %all-to-all-start.2) | async-done | bytes 98336 | tf_op jit(solution)/shard_map/all_to_all | solution.py:244
  64.7 0.0 copy-done.2
  64.7 0.8 %shard_map.60 = f32[3,8,2048]{2,1,0:T(8,128)} custom-call(bf16[4,24,512]{2,1,0:T(8,128)(2,1)S(1)} %all-to-all-done.2.grad_ref, f32[3,8,2048]{2,1,0:T(8,128)S(1)} %shard_map.59.smooth_ref, bf16[3,3,8,2048]{3,2,1,0:T(8,128)(2,1)S(1)} %bitcast.22, f32[3,8,2048]{2,1,0:T(8,128)S(1)} %bitcast.21), custom_call_target="tpu_custom_call" | custom-call | tf_op jit(solution)/shard_map/pallas_call | solution.py:221
  (2 shorter events, 0.0 us)
Async XLA Ops:
  0.0 0.9 %copy-start = (f32[8,3,2048]{2,0,1:T(8,128)S(1)}, f32[8,3,2048]{2,0,1:T(8,128)}, u32[]{:S(2)}) copy-start(f32[8,3,2048]{2,0,1:T(8,128)} %param.5) | copy-start | bytes 589828
  1.7 16.6 %all-to-all-start = ((bf16[4,24,2048]{2,1,0:T(8,128)(2,1)}), bf16[4,24,2048]{2,1,0:T(8,128)(2,1)S(1)}, u32[]{:S(2)}, u32[]{:S(2)}) async-start(bf16[4,24,2048]{2,1,0:T(8,128)(2,1)} %shard_map.56), calls=%async_computation | async-start | bytes 786432 | tf_op jit(solution)/shard_map/all_to_all | solution.py:237
  6.6 0.7 %copy-start.3 = (f32[4,3]{1,0:T(4,128)S(1)}, f32[4,3]{1,0:T(4,128)}, u32[]{:S(2)}) copy-start(f32[4,3]{1,0:T(4,128)} %atten_ref.1) | copy-start | bytes 148
  7.3 25.6 %copy-start.1 = (f32[8,3,2048]{2,0,1:T(8,128)S(1)}, f32[8,3,2048]{2,0,1:T(8,128)}, u32[]{:S(2)}) copy-start(f32[8,3,2048]{2,0,1:T(8,128)} %param.5) | copy-start | bytes 589828
  18.3 46.5 %copy-start.2 = (bf16[8,3,3,2048]{3,0,2,1:T(8,128)(2,1)S(1)}, bf16[8,3,3,2048]{3,0,2,1:T(8,128)(2,1)}, u32[]{:S(2)}) copy-start(bf16[8,3,3,2048]{3,0,2,1:T(8,128)(2,1)} %param.9) | copy-start | bytes 884740
  24.0 30.8 %all-to-all-start.1 = ((bf16[32,24,512]{2,1,0:T(8,128)(2,1)}), bf16[32,24,512]{2,1,0:T(8,128)(2,1)S(1)}, u32[]{:S(2)}, u32[]{:S(2)}) async-start(bf16[32,24,512]{2,1,0:T(8,128)(2,1)} %bitcast.5), calls=%async_computation.1 | async-start | bytes 1572864 | tf_op jit(solution)/shard_map/all_to_all | solution.py:242
  32.9 26.1 %collective-permute-start = (f32[3,2048]{1,0:T(4,128)S(1)}, f32[3,2048]{1,0:T(4,128)S(1)}, u32[]{:S(2)}, u32[]{:S(2)}) collective-permute-start(f32[3,2048]{1,0:T(4,128)S(1)} %bitcast.24), channel_id=1, source_target_pairs={{3,4},{4,3},{7,8},{8,7},{11,12},{12,11},{15,16},{16,15},{19,20},{2... | collective-permute-start | bytes 73736 | tf_op jit(solution)/shard_map/ppermute | solution.py:250
  55.6 9.1 %all-to-all-start.2 = ((bf16[4,24,512]{2,1,0:T(8,128)(2,1)}), bf16[4,24,512]{2,1,0:T(8,128)(2,1)S(1)}, u32[]{:S(2)}, u32[]{:S(2)}) async-start(bf16[4,24,512]{2,1,0:T(8,128)(2,1)} %shard_map.58), calls=%async_computation.2 | async-start | bytes 196608 | tf_op jit(solution)/shard_map/all_to_all | solution.py:244

commit v3 on v2

--- a/solution.py
+++ b/solution.py
@@ -13,7 +13,8 @@
 VMEM = pl.BlockSpec(memory_space=pltpu.VMEM)
 SMEM = pl.BlockSpec(memory_space=pltpu.SMEM)
 SMALL = 8 * 1024 * 1024
-LARGE = 52 * 1024 * 1024
+MEDIUM = 49 * 1024 * 1024
+LARGE = 47 * 1024 * 1024
 
 
 def spread_kernel(vol_ref, out_ref):
@@ -34,46 +35,60 @@
     )(volume)
 
 
-def tiles_kernel(atten_ref, tiles_ref):
+def stage_kernel(atten_ref, proj_ref, counts_ref, near_ref, binned_ref, tiles_ref, sem):
+    copy = pltpu.make_async_copy(proj_ref.at[: near_ref.shape[0]], near_ref, sem)
+    copy.start()
     bins, mats = atten_ref.shape
+    for b in range(bins):
+        binned_ref[b] = counts_ref[:, b, :].astype(F32)
     for b in range(bins):
         for m in range(mats):
             tiles_ref[b * mats + m] = jnp.full(tiles_ref.shape[1:], atten_ref[b, m], F32)
-
-
-def attenuation_tiles(atten):
-    return pl.pallas_call(
-        tiles_kernel,
-        out_shape=jax.ShapeDtypeStruct((atten.size, 8, 128), F32),
-        in_specs=[SMEM],
-        out_specs=VMEM,
-        compiler_params=pltpu.CompilerParams(vmem_limit_bytes=SMALL),
-    )(atten)
+    copy.wait()
+
+
+def stage(atten, projector, counts, held):
+    slices, bins, cols = counts.shape
+    return pl.pallas_call(
+        stage_kernel,
+        out_shape=[
+            jax.ShapeDtypeStruct((held, projector.shape[1]), BF16),
+            jax.ShapeDtypeStruct((bins, slices, cols), F32),
+            jax.ShapeDtypeStruct((atten.size, 8, 128), F32),
+        ],
+        in_specs=[SMEM, pl.BlockSpec(memory_space=pltpu.HBM), VMEM],
+        out_specs=[VMEM] * 3,
+        scratch_shapes=[pltpu.SemaphoreType.DMA(())],
+        compiler_params=pltpu.CompilerParams(vmem_limit_bytes=LARGE),
+        cost_estimate=pl.CostEstimate(flops=0, bytes_accessed=4 * projector.size, transcendentals=0),
+    )(atten, projector, counts)
 
 
 def wide_tile(tile, wide):
     return jnp.concatenate([tile] * (wide // tile.shape[1]), 1)
 
 
-def project_kernel(mats, bins, slabs, tiles_ref, x_ref, proj_ref, counts_ref, out_ref, resid_ref, near_ref, sems):
+def project_kernel(mats, bins, slabs, tiles_ref, x_ref, near_ref, proj_ref, counts_ref, out_ref, resid_ref, rest_ref, sems):
     rows, pix = x_ref.shape
-    cols = proj_ref.shape[0]
+    cols, held = proj_ref.shape[0], near_ref.shape[0]
+    wide = 256
+    copies = [
+        pltpu.make_async_copy(
+            proj_ref.at[at : at + wide], rest_ref.at[at - held : at - held + wide], sems.at[i]
+        )
+        for i, at in enumerate(range(held, cols, wide))
+    ]
+    for copy in copies:
+        copy.start()
     per_slab = rows // slabs
     depth = per_slab // mats
-    wide = cols // sems.shape[0]
-    copies_in = [
-        pltpu.make_async_copy(
-            proj_ref.at[at : at + wide], near_ref.at[at : at + wide], sems.at[at // wide]
-        )
-        for at in range(0, cols, wide)
-    ]
-    for copy_in in copies_in:
-        copy_in.start()
     atten = [[wide_tile(tiles_ref[b * mats + m], wide) for m in range(mats)] for b in range(bins)]
     for at in range(0, cols, wide):
-        copies_in[at // wide].wait()
+        if at >= held:
+            copies[(at - held) // wide].wait()
+        block = near_ref[at : at + wide] if at < held else rest_ref[at - held : at - held + wide]
         line = lax.dot_general(
-            x_ref[...], near_ref[at : at + wide, :], (((1,), (1,)), ((), ())), preferred_element_type=F32
+            x_ref[...], block, (((1,), (1,)), ((), ())), preferred_element_type=F32
         )
         blocks = []
         for slab in range(slabs):
@@ -90,35 +105,33 @@
                     parts[m] = term if parts[m] is None else parts[m] + term
             blocks += parts
         resid_ref[:, at : at + wide] = jnp.concatenate(blocks, 0).astype(BF16)
-    owners, copies, _, _, span = out_ref.shape
+    owners, _, _, span = out_ref.shape
     for owner in range(owners):
-        back = jnp.dot(
-            resid_ref[...], near_ref[:, owner * span : (owner + 1) * span], preferred_element_type=F32
-        )
+        own = slice(owner * span, (owner + 1) * span)
+        back = jnp.dot(resid_ref[:, :held], near_ref[:, own], preferred_element_type=F32)
+        back = back + jnp.dot(resid_ref[:, held:], rest_ref[:, own], preferred_element_type=F32)
         for slab in range(slabs):
-            part = back[slab * per_slab : (slab + 1) * per_slab].astype(BF16)
-            for copy in range(copies):
-                out_ref[owner, copy, slab] = part
-
-
-def project(tiles, x_all, projector, counts, owners, copies, slabs, mats):
+            out_ref[owner, slab] = back[slab * per_slab : (slab + 1) * per_slab].astype(BF16)
+
+
+def project(tiles, x_all, near, projector, counts, owners, slabs, mats):
     rows, pix = x_all.shape
-    cols = projector.shape[0]
+    cols = counts.shape[2]
     return pl.pallas_call(
         functools.partial(project_kernel, mats, counts.shape[0], slabs),
-        out_shape=jax.ShapeDtypeStruct((owners, copies, slabs, rows // slabs, pix // owners), BF16),
-        in_specs=[VMEM, VMEM, pl.BlockSpec(memory_space=pltpu.HBM), VMEM],
+        out_shape=jax.ShapeDtypeStruct((owners, slabs, rows // slabs, pix // owners), BF16),
+        in_specs=[VMEM, VMEM, VMEM, pl.BlockSpec(memory_space=pltpu.HBM), VMEM],
         out_specs=VMEM,
         scratch_shapes=[
             pltpu.VMEM((rows, cols), BF16),
-            pltpu.VMEM((cols, pix), BF16),
-            pltpu.SemaphoreType.DMA((4,)),
+            pltpu.VMEM((cols - near.shape[0], pix), BF16),
+            pltpu.SemaphoreType.DMA(((cols - near.shape[0]) // 256,)),
         ],
-        compiler_params=pltpu.CompilerParams(vmem_limit_bytes=LARGE),
+        compiler_params=pltpu.CompilerParams(vmem_limit_bytes=MEDIUM),
         cost_estimate=pl.CostEstimate(
             flops=4 * rows * cols * pix, bytes_accessed=2 * cols * pix, transcendentals=rows * cols
         ),
-    )(tiles, x_all, projector, counts)
+    )(tiles, x_all, near, projector, counts)
 
 
 def next_pixel(field):
@@ -236,10 +249,11 @@
     vol = volume.transpose(1, 0, 2)
     x_all = lax.all_to_all(spread(vol, slabs), "mat", 0, 0, tiled=True)
     x_all = x_all.reshape(slabs * rows, pix)
-    counts_binned = counts[0].astype(F32).transpose(1, 0, 2)
-    parts = project(attenuation_tiles(atten), x_all, projector[0], counts_binned, owners, copies, slabs, mats)
-    parts = parts.reshape(owners * copies * slabs, rows, pix // owners)
-    parts = lax.all_to_all(parts, ("x", "half", "mat"), 0, 0, tiled=True)
+    near, binned, tiles = stage(atten, projector[0], counts[0], projector.shape[1] // 2)
+    parts = project(tiles, x_all, near, projector[0], binned, owners, slabs, mats)
+    parts = lax.all_to_all(parts, "x", 0, 0, tiled=True)
+    parts = total_copies(parts, 1.0, copies).reshape(copies * slabs, rows, pix // owners)
+    parts = lax.all_to_all(parts, ("half", "mat"), 0, 0, tiled=True)
     mine = total_copies(parts, float(views_all) ** (-0.5), owners)
     grad = lax.all_to_all(mine, "x", 0, 0, tiled=True)
     edge = jnp.where(slab == 0, vol[:, 0], vol[:, -1])

time: 66.6 us -> 61.9 us (0.929)
  waiting for transfers between devices: 32.5 us -> 26.5 us
  local copies, waits for them, and re-layouts: 1.63 us -> 4.77 us
  other arithmetic: 1.14 us -> 0.1 us
    all_to_all x1 -> x2, waiting for transfers between devices: 18.3 us -> 14.8 us  [the longest x1 7.45 us: body(): parts = lax.all_to_all(parts, ('half', 'mat'), 0, 0, tiled=True)]
    unnamed x9 -> x13, local copies, waits for them, and re-layouts: 1.63 us -> 4.77 us
    all_to_all x1, waiting for transfers between devices: 9.38 us -> 6.9 us  [body(): x_all = lax.all_to_all(spread(vol, slabs), 'mat', 0, 0, tiled=True)]
    pallas_call x1, Pallas kernels: 5.76 us -> 4.24 us  [project(): pl.pallas_call(functools.partial(project_kernel, mats, counts.shape[0], s...]
    all_to_all x1 -> x2, starting transfers between devices: 8.8 us -> 10.2 us  [the longest x1 5.94 us: body(): parts = lax.all_to_all(parts, ('half', 'mat'), 0, 0, tiled=True)]
    ppermute x1, starting transfers between devices: 3.63 us -> 2.44 us  [body(): edge = lax.ppermute(edge, ('row', 'mat'), pairs)]
    transpose x1 -> x0, other arithmetic: 1.04 us -> none  [body(): counts_binned = counts[0].astype(F32).transpose(1, 0, 2)]
    pallas_call x1 -> x2, Pallas kernels: 0.76 us -> 1.4 us  [total_copies(): pl.pallas_call(functools.partial(total_kernel, factor), out_shape=jax.Sha...]
  transfers between devices with their start and end apart: 4 -> 5, of which waited for: 3 -> 4; matrix products, arithmetic and copies ran while one was open for 2% -> 0% of each run, Pallas kernels for 3% -> 4%
where the time goes in v3:
time: 61.9 us; the launch traced here: 61.3 us
  waiting for transfers between devices  26.5 us (43%)
  starting transfers between devices  20.9 us (34%)
  Pallas kernels  9.01 us (15%)
  local copies, waits for them, and re-layouts  4.77 us (8%)
    all_to_all x1, waiting for transfers between devices, body(): parts = lax.all_to_all(parts, ('half', 'mat'), 0, 0, tiled=True)  7.45 us
    all_to_all x1, waiting for transfers between devices, body(): parts = lax.all_to_all(parts, 'x', 0, 0, tiled=True)  7.38 us
    all_to_all x1, waiting for transfers between devices, body(): x_all = lax.all_to_all(spread(vol, slabs), 'mat', 0, 0, tiled=True)  6.9 us
    all_to_all x1, starting transfers between devices, body(): parts = lax.all_to_all(parts, ('half', 'mat'), 0, 0, tiled=True)  5.94 us
    all_to_all x1, starting transfers between devices, body(): x_all = lax.all_to_all(spread(vol, slabs), 'mat', 0, 0, tiled=True)  4.87 us
    all_to_all x1, waiting for transfers between devices, body(): grad = lax.all_to_all(mine, 'x', 0, 0, tiled=True)  4.79 us
    unnamed x13, local copies, waits for them, and re-layouts  4.77 us
    all_to_all x1, starting transfers between devices, body(): parts = lax.all_to_all(parts, 'x', 0, 0, tiled=True)  4.3 us
  transfers between devices with their start and end apart: 5, of which 4 were waited for; matrix products, arithmetic and copies ran while one was open for 0% of the time, Pallas kernels for 4%

profile of v3, /device:TPU:448, one launch (start us, length us, event | category | flops | bytes accessed | tf_op | source)
XLA Modules:
  0.0 61.3 jit_solution(5543639933728257187)
XLA Ops:
  0.0 0.0 copy-start.1
  0.0 0.9 %copy-done.1 = f32[8,3,2048]{2,0,1:T(8,128)S(1)} copy-done((f32[8,3,2048]{2,0,1:T(8,128)S(1)}, f32[8,3,2048]{2,0,1:T(8,128)}, u32[]{:S(2)}) %copy-start.1) | copy-done | bytes 196632
  0.9 0.8 %shard_map.56 = bf16[4,24,2048]{2,1,0:T(8,128)(2,1)} custom-call(f32[3,8,2048]{2,1,0:T(8,128)S(1)} %bitcast.16), custom_call_target="tpu_custom_call" | custom-call | tf_op jit(solution)/shard_map/pallas_call | solution.py:29
  1.7 4.9 %all-to-all-start = ((bf16[4,24,2048]{2,1,0:T(8,128)(2,1)}), bf16[4,24,2048]{2,1,0:T(8,128)(2,1)S(1)}, u32[]{:S(2)}, u32[]{:S(2)}) async-start(bf16[4,24,2048]{2,1,0:T(8,128)(2,1)} %shard_map.56), calls=%async_computation | async-start | bytes 786432 | tf_op jit(solution)/shard_map/all_to_all | solution.py:250
  6.6 0.0 copy-start
  6.6 2.2 %copy-done = bf16[1,1024,2048]{2,1,0:T(8,128)(2,1)S(1)} copy-done((bf16[1,1024,2048]{2,1,0:T(8,128)(2,1)S(1)}, bf16[1,1024,2048]{2,1,0:T(8,128)(2,1)}, u32[]{:S(2)}) %copy-start) | copy-done | bytes 4194328
  8.8 0.0 copy-start.4
  8.8 0.9 %copy-done.4 = bf16[1,32,4,1024]{3,2,1,0:T(4,128)(2,1)S(1)} copy-done((bf16[1,32,4,1024]{3,2,1,0:T(4,128)(2,1)S(1)}, bf16[1,32,4,1024]{3,2,1,0:T(4,128)(2,1)}, u32[]{:S(2)}) %copy-start.4) | copy-done | bytes 262168
  9.7 0.0 copy-start.5
  9.7 0.7 %copy-done.5 = f32[4,3]{1,0:T(4,128)S(1)} copy-done((f32[4,3]{1,0:T(4,128)S(1)}, f32[4,3]{1,0:T(4,128)}, u32[]{:S(2)}) %copy-start.5) | copy-done | bytes 72
  10.4 1.0 %shard_map.55 = (bf16[512,2048]{1,0:T(8,128)(2,1)S(1)}, f32[4,32,1024]{2,1,0:T(8,128)S(1)}, f32[12,8,128]{2,1,0:T(8,128)S(1)}) custom-call(f32[4,3]{1,0:T(4,128)S(1)} %copy-done.5, bf16[1024,2048]{1,0:T(8,128)(2,1)S(1)} %bitcast.13, bf16[32,4,1024]{2,1,0:T(4,128)(2,1)S(1)} %bitcast.21), custom_call_target="tpu_custom_call" | custom-call | bytes 8388608 | tf_op jit(solution)/shard_map/pallas_call | solution.py:52
  11.4 6.9 %all-to-all-done = bf16[4,24,2048]{2,1,0:T(8,128)(2,1)S(1)} async-done(((bf16[4,24,2048]{2,1,0:T(8,128)(2,1)}), bf16[4,24,2048]{2,1,0:T(8,128)(2,1)S(1)}, u32[]{:S(2)}, u32[]{:S(2)}) %all-to-all-start) | async-done | bytes 393248 | tf_op jit(solution)/shard_map/all_to_all | solution.py:250
  18.3 0.0 copy-start.2
  18.3 0.0 copy-start.3
  18.3 4.2 %shard_map.57 = bf16[4,4,24,512]{3,2,1,0:T(8,128)(2,1)} custom-call(f32[12,8,128]{2,1,0:T(8,128)S(1)} %get-tuple-element.8.tiles_ref, bf16[96,2048]{1,0:T(8,128)(2,1)S(1)} %bitcast.14, bf16[512,2048]{1,0:T(8,128)(2,1)S(1)} %get-tuple-element.9.near_ref, bf16[1024,2048]{1,0:T(8,128)(2,1)} %bitcast.12, f32[4,32,1024]{2,1,0:T(8,128)S(1)} %get-tuple-element.10.counts_ref), custom_call_target="tpu_custom_call" | custom-call | flops 805306368 | bytes 4194304 | tf_op jit(solution)/shard_map/pallas_call | solution.py:120
  22.5 4.3 %all-to-all-start.1 = ((bf16[4,4,24,512]{3,2,1,0:T(8,128)(2,1)}), bf16[4,4,24,512]{3,2,1,0:T(8,128)(2,1)S(1)}, u32[]{:S(2)}, u32[]{:S(2)}) async-start(bf16[4,4,24,512]{3,2,1,0:T(8,128)(2,1)} %shard_map.57), calls=%async_computation.1 | async-start | bytes 786432 | tf_op jit(solution)/shard_map/all_to_all | solution.py:254
  26.8 7.4 %all-to-all-done.1.part_ref = bf16[4,4,24,512]{3,2,1,0:T(8,128)(2,1)S(1)} async-done(((bf16[4,4,24,512]{3,2,1,0:T(8,128)(2,1)}), bf16[4,4,24,512]{3,2,1,0:T(8,128)(2,1)S(1)}, u32[]{:S(2)}, u32[]{:S(2)}) %all-to-all-start.1) | async-done | bytes 393248 | tf_op jit(solution)/shard_map/all_to_all | solution.py:254
  34.2 0.7 %shard_map.58 = bf16[2,4,24,512]{3,2,1,0:T(8,128)(2,1)} custom-call(bf16[4,4,24,512]{3,2,1,0:T(8,128)(2,1)S(1)} %all-to-all-done.1.part_ref), custom_call_target="tpu_custom_call" | custom-call | tf_op jit(solution)/shard_map/pallas_call | solution.py:210
  34.9 5.9 %all-to-all-start.2 = ((bf16[8,24,512]{2,1,0:T(8,128)(2,1)}), bf16[8,24,512]{2,1,0:T(8,128)(2,1)S(1)}, u32[]{:S(2)}, u32[]{:S(2)}) async-start(bf16[8,24,512]{2,1,0:T(8,128)(2,1)} %bitcast.4), calls=%async_computation.2 | async-start | bytes 393216 | tf_op jit(solution)/shard_map/all_to_all | solution.py:256
  40.9 0.0 copy-done.2
  40.9 2.4 %collective-permute-start = (f32[3,2048]{1,0:T(4,128)S(1)}, f32[3,2048]{1,0:T(4,128)S(1)}, u32[]{:S(2)}, u32[]{:S(2)}) collective-permute-start(f32[3,2048]{1,0:T(4,128)S(1)} %bitcast.22), channel_id=1, source_target_pairs={{3,4},{4,3},{7,8},{8,7},{11,12},{12,11},{15,16},{16,15},{19,20},{2... | collective-permute-start | bytes 73736 | tf_op jit(solution)/shard_map/ppermute | solution.py:264
  43.4 7.4 %all-to-all-done.2.part_ref = bf16[8,24,512]{2,1,0:T(8,128)(2,1)S(1)} async-done(((bf16[8,24,512]{2,1,0:T(8,128)(2,1)}), bf16[8,24,512]{2,1,0:T(8,128)(2,1)S(1)}, u32[]{:S(2)}, u32[]{:S(2)}) %all-to-all-start.2) | async-done | bytes 196640 | tf_op jit(solution)/shard_map/all_to_all | solution.py:256
  50.8 0.7 %shard_map.59 = bf16[4,24,512]{2,1,0:T(8,128)(2,1)} custom-call(bf16[8,24,512]{2,1,0:T(8,128)(2,1)S(1)} %all-to-all-done.2.part_ref), custom_call_target="tpu_custom_call" | custom-call | tf_op jit(solution)/shard_map/pallas_call | solution.py:210
  51.5 3.3 %all-to-all-start.3 = ((bf16[4,24,512]{2,1,0:T(8,128)(2,1)}), bf16[4,24,512]{2,1,0:T(8,128)(2,1)S(1)}, u32[]{:S(2)}, u32[]{:S(2)}) async-start(bf16[4,24,512]{2,1,0:T(8,128)(2,1)} %shard_map.59), calls=%async_computation.3 | async-start | bytes 196608 | tf_op jit(solution)/shard_map/all_to_all | solution.py:258
  54.8 0.1 pad_add_fusion.where_ref
  54.9 0.0 collective-permute-done.edge_ref
  54.9 0.9 %shard_map.60.smooth_ref = f32[3,8,2048]{2,1,0:T(8,128)S(1)} custom-call(s32[2]{0:T(128)S(1)} %pad_add_fusion.where_ref, f32[3,8,2048]{2,1,0:T(8,128)S(1)} %bitcast.18, bf16[96,2048]{1,0:T(8,128)(2,1)S(1)} %bitcast.15, f32[3,2048]{1,0:T(4,128)S(1)} %collective-permute-done.edge_ref), custom_call_target="tpu_custom_call" | custom-call | flops 1966080 | bytes 589824 | tf_op jit(solution)/shard_map/pallas_call | solution.py:190
  55.8 4.8 %all-to-all-done.3.grad_ref = bf16[4,24,512]{2,1,0:T(8,128)(2,1)S(1)} async-done(((bf16[4,24,512]{2,1,0:T(8,128)(2,1)}), bf16[4,24,512]{2,1,0:T(8,128)(2,1)S(1)}, u32[]{:S(2)}, u32[]{:S(2)}) %all-to-all-start.3) | async-done | bytes 98336 | tf_op jit(solution)/shard_map/all_to_all | solution.py:258
  60.6 0.0 copy-done.3
  60.6 0.8 %shard_map.61 = f32[3,8,2048]{2,1,0:T(8,128)} custom-call(bf16[4,24,512]{2,1,0:T(8,128)(2,1)S(1)} %all-to-all-done.3.grad_ref, f32[3,8,2048]{2,1,0:T(8,128)S(1)} %shard_map.60.smooth_ref, bf16[3,3,8,2048]{3,2,1,0:T(8,128)(2,1)S(1)} %bitcast.20, f32[3,8,2048]{2,1,0:T(8,128)S(1)} %bitcast.19), custom_call_target="tpu_custom_call" | custom-call | tf_op jit(solution)/shard_map/pallas_call | solution.py:234
  (2 shorter events, 0.0 us)
Async XLA Ops:
  0.0 0.9 %copy-start.1 = (f32[8,3,2048]{2,0,1:T(8,128)S(1)}, f32[8,3,2048]{2,0,1:T(8,128)}, u32[]{:S(2)}) copy-start(f32[8,3,2048]{2,0,1:T(8,128)} %param.5) | copy-start | bytes 589828
  1.7 16.6 %all-to-all-start = ((bf16[4,24,2048]{2,1,0:T(8,128)(2,1)}), bf16[4,24,2048]{2,1,0:T(8,128)(2,1)S(1)}, u32[]{:S(2)}, u32[]{:S(2)}) async-start(bf16[4,24,2048]{2,1,0:T(8,128)(2,1)} %shard_map.56), calls=%async_computation | async-start | bytes 786432 | tf_op jit(solution)/shard_map/all_to_all | solution.py:250
  6.6 2.2 %copy-start = (bf16[1,1024,2048]{2,1,0:T(8,128)(2,1)S(1)}, bf16[1,1024,2048]{2,1,0:T(8,128)(2,1)}, u32[]{:S(2)}) copy-start(bf16[1,1024,2048]{2,1,0:T(8,128)(2,1)} %param.6) | copy-start | bytes 12582916
  8.8 0.9 %copy-start.4 = (bf16[1,32,4,1024]{3,2,1,0:T(4,128)(2,1)S(1)}, bf16[1,32,4,1024]{3,2,1,0:T(4,128)(2,1)}, u32[]{:S(2)}) copy-start(bf16[1,32,4,1024]{3,2,1,0:T(4,128)(2,1)} %param.7) | copy-start | bytes 786436
  9.7 0.7 %copy-start.5 = (f32[4,3]{1,0:T(4,128)S(1)}, f32[4,3]{1,0:T(4,128)}, u32[]{:S(2)}) copy-start(f32[4,3]{1,0:T(4,128)} %atten_ref.1) | copy-start | bytes 148
  18.3 22.6 %copy-start.2 = (f32[8,3,2048]{2,0,1:T(8,128)S(1)}, f32[8,3,2048]{2,0,1:T(8,128)}, u32[]{:S(2)}) copy-start(f32[8,3,2048]{2,0,1:T(8,128)} %param.5) | copy-start | bytes 589828
  18.3 42.3 %copy-start.3 = (bf16[8,3,3,2048]{3,0,2,1:T(8,128)(2,1)S(1)}, bf16[8,3,3,2048]{3,0,2,1:T(8,128)(2,1)}, u32[]{:S(2)}) copy-start(bf16[8,3,3,2048]{3,0,2,1:T(8,128)(2,1)} %param.9) | copy-start | bytes 884740
  22.5 11.7 %all-to-all-start.1 = ((bf16[4,4,24,512]{3,2,1,0:T(8,128)(2,1)}), bf16[4,4,24,512]{3,2,1,0:T(8,128)(2,1)S(1)}, u32[]{:S(2)}, u32[]{:S(2)}) async-start(bf16[4,4,24,512]{3,2,1,0:T(8,128)(2,1)} %shard_map.57), calls=%async_computation.1 | async-start | bytes 786432 | tf_op jit(solution)/shard_map/all_to_all | solution.py:254
  34.9 15.9 %all-to-all-start.2 = ((bf16[8,24,512]{2,1,0:T(8,128)(2,1)}), bf16[8,24,512]{2,1,0:T(8,128)(2,1)S(1)}, u32[]{:S(2)}, u32[]{:S(2)}) async-start(bf16[8,24,512]{2,1,0:T(8,128)(2,1)} %bitcast.4), calls=%async_computation.2 | async-start | bytes 393216 | tf_op jit(solution)/shard_map/all_to_all | solution.py:256
  40.9 14.0 %collective-permute-start = (f32[3,2048]{1,0:T(4,128)S(1)}, f32[3,2048]{1,0:T(4,128)S(1)}, u32[]{:S(2)}, u32[]{:S(2)}) collective-permute-start(f32[3,2048]{1,0:T(4,128)S(1)} %bitcast.22), channel_id=1, source_target_pairs={{3,4},{4,3},{7,8},{8,7},{11,12},{12,11},{15,16},{16,15},{19,20},{2... | collective-permute-start | bytes 73736 | tf_op jit(solution)/shard_map/ppermute | solution.py:264
  51.5 9.1 %all-to-all-start.3 = ((bf16[4,24,512]{2,1,0:T(8,128)(2,1)}), bf16[4,24,512]{2,1,0:T(8,128)(2,1)S(1)}, u32[]{:S(2)}, u32[]{:S(2)}) async-start(bf16[4,24,512]{2,1,0:T(8,128)(2,1)} %shard_map.59), calls=%async_computation.3 | async-start | bytes 196608 | tf_op jit(solution)/shard_map/all_to_all | solution.py:258

commit v4 on v3

--- a/solution.py
+++ b/solution.py
@@ -14,7 +14,7 @@
 SMEM = pl.BlockSpec(memory_space=pltpu.SMEM)
 SMALL = 8 * 1024 * 1024
 MEDIUM = 49 * 1024 * 1024
-LARGE = 47 * 1024 * 1024
+LARGE = 50 * 1024 * 1024
 
 
 def spread_kernel(vol_ref, out_ref):
@@ -218,10 +218,12 @@
 
 def step_kernel(grad_ref, smooth_ref, newton_ref, vol_ref, out_ref):
     mats, depth, pix = vol_ref.shape
-    span = grad_ref.shape[2]
-    for owner in range(grad_ref.shape[0]):
+    owners, copies, _, span = grad_ref.shape
+    for owner in range(owners):
         own = slice(owner * span, (owner + 1) * span)
-        grad = grad_ref[owner].astype(F32)
+        grad = grad_ref[owner, 0].astype(F32)
+        for copy in range(1, copies):
+            grad = grad + grad_ref[owner, copy].astype(F32)
         steps = [grad[k * depth : (k + 1) * depth] + 0.5 * smooth_ref[k, :, own] for k in range(mats)]
         for m in range(mats):
             moved = newton_ref[m, 0, :, own].astype(F32) * steps[0]
@@ -249,19 +251,20 @@
     vol = volume.transpose(1, 0, 2)
     x_all = lax.all_to_all(spread(vol, slabs), "mat", 0, 0, tiled=True)
     x_all = x_all.reshape(slabs * rows, pix)
-    near, binned, tiles = stage(atten, projector[0], counts[0], projector.shape[1] // 2)
-    parts = project(tiles, x_all, near, projector[0], binned, owners, slabs, mats)
-    parts = lax.all_to_all(parts, "x", 0, 0, tiled=True)
-    parts = total_copies(parts, 1.0, copies).reshape(copies * slabs, rows, pix // owners)
-    parts = lax.all_to_all(parts, ("half", "mat"), 0, 0, tiled=True)
-    mine = total_copies(parts, float(views_all) ** (-0.5), owners)
-    grad = lax.all_to_all(mine, "x", 0, 0, tiled=True)
     edge = jnp.where(slab == 0, vol[:, 0], vol[:, -1])
     pairs = []
     for g in range(groups - 1):
         last, start = g * slabs + slabs - 1, (g + 1) * slabs
         pairs += [(last, start), (start, last)]
     edge = lax.ppermute(edge, ("row", "mat"), pairs)
+    near, binned, tiles = stage(atten, projector[0], counts[0], projector.shape[1] // 2)
+    x_all, edge, near = lax.optimization_barrier((x_all, edge, near))
+    parts = project(tiles, x_all, near, projector[0], binned, owners, slabs, mats)
+    parts = parts.reshape(owners * slabs, rows, pix // owners)
+    parts = lax.all_to_all(parts, ("x", "mat"), 0, 0, tiled=True)
+    mine = total_copies(parts, float(views_all) ** (-0.5), owners * copies)
+    grad = lax.all_to_all(mine, ("x", "half"), 0, 0, tiled=True)
+    grad = grad.reshape(owners, copies, rows, pix // owners)
     is_first = jnp.logical_and(slab == 0, group == 0).astype(jnp.int32)
     smoothed = smooth(jnp.stack([slab, is_first]).astype(jnp.int32), vol, x_all, edge)
     updated = newton_step(grad, smoothed, newton.transpose(1, 2, 0, 3), vol)

time: 61.9 us -> 62.2 us (level)
  the two profiles are of different devices: /device:TPU:448 before, /device:TPU:200 now
where the time goes in v4:
time: 62.2 us; the launch traced here: 61.7 us
  blocking collectives  19.9 us (32%)
  waiting for transfers between devices  14.8 us (24%)
  starting transfers between devices  13 us (21%)
  Pallas kernels  8.8 us (14%)
  local copies, waits for them, and re-layouts  3.94 us (6%)
  other arithmetic  1.12 us (2%)
    all_to_all x1, blocking collectives, body(): parts = lax.all_to_all(parts, ('x', 'mat'), 0, 0, tiled=True)  19.9 us
    all_to_all x1, waiting for transfers between devices, body(): grad = lax.all_to_all(mine, ('x', 'half'), 0, 0, tiled=True)  11.1 us
    all_to_all x1, starting transfers between devices, body(): grad = lax.all_to_all(mine, ('x', 'half'), 0, 0, tiled=True)  7.06 us
    all_to_all x1, starting transfers between devices, body(): x_all = lax.all_to_all(spread(vol, slabs), 'mat', 0, 0, tiled=True)  5.32 us
    unnamed x15, local copies, waits for them, and re-layouts  3.94 us
    all_to_all x1, waiting for transfers between devices, body(): x_all = lax.all_to_all(spread(vol, slabs), 'mat', 0, 0, tiled=True)  3.68 us
    pallas_call x1, Pallas kernels, project(): pl.pallas_call(functools.partial(project_kernel, mats, counts.shape[0], s...  3.48 us
    pallas_call x1, Pallas kernels, stage(): pl.pallas_call(stage_kernel, out_shape=[jax.ShapeDtypeStruct((held, proje...  2.16 us
  transfers between devices with their start and end apart: 3, of which 2 were waited for; matrix products, arithmetic and copies ran while one was open for 2% of the time, Pallas kernels for 5%

profile of v4, /device:TPU:200, one launch (start us, length us, event | category | flops | bytes accessed | tf_op | source)
XLA Modules:
  0.0 61.7 jit_solution(10802729653492233063)
XLA Ops:
  0.0 0.0 copy-start
  0.0 0.9 %copy-done = f32[8,3,2048]{2,0,1:T(8,128)S(1)} copy-done((f32[8,3,2048]{2,0,1:T(8,128)S(1)}, f32[8,3,2048]{2,0,1:T(8,128)}, u32[]{:S(2)}) %copy-start) | copy-done | bytes 196632
  0.9 0.8 %shard_map.56 = bf16[4,24,2048]{2,1,0:T(8,128)(2,1)} custom-call(f32[3,8,2048]{2,1,0:T(8,128)S(1)} %bitcast.16), custom_call_target="tpu_custom_call" | custom-call | tf_op jit(solution)/shard_map/pallas_call | solution.py:29
  1.7 5.3 %all-to-all-start = ((bf16[4,24,2048]{2,1,0:T(8,128)(2,1)}), bf16[4,24,2048]{2,1,0:T(8,128)(2,1)S(1)}, u32[]{:S(2)}, u32[]{:S(2)}) async-start(bf16[4,24,2048]{2,1,0:T(8,128)(2,1)} %shard_map.56), calls=%async_computation | async-start | bytes 786432 | tf_op jit(solution)/shard_map/all_to_all | solution.py:252
  7.0 1.0 %broadcast_select_fusion = f32[3,1,2048]{2,1,0:T(1,128)S(1)} fusion(pred[]{:T(512)S(6)} %eq.7, f32[3,8,2048]{2,1,0:T(8,128)} %bitcast.15), kind=kLoop, calls=%fused_computation | loop fusion | flops 6144 | bytes 73729 | tf_op jit(solution)/shard_map/jit(_where)/select_n | solution.py:254
  8.1 0.7 %collective-permute-start = (f32[3,2048]{1,0:T(4,128)S(1)}, f32[3,2048]{1,0:T(4,128)S(1)}, u32[]{:S(2)}, u32[]{:S(2)}) collective-permute-start(f32[3,2048]{1,0:T(4,128)S(1)} %bitcast.25), channel_id=1, source_target_pairs={{3,4},{4,3},{7,8},{8,7},{11,12},{12,11},{15,16},{16,15},{19,20},{2... | collective-permute-start | bytes 73736 | tf_op jit(solution)/shard_map/ppermute | solution.py:259
  8.8 0.0 copy-start.3
  8.8 0.9 %copy-done.3 = bf16[1,32,4,1024]{3,2,1,0:T(4,128)(2,1)S(1)} copy-done((bf16[1,32,4,1024]{3,2,1,0:T(4,128)(2,1)S(1)}, bf16[1,32,4,1024]{3,2,1,0:T(4,128)(2,1)}, u32[]{:S(2)}) %copy-start.3) | copy-done | bytes 262168
  9.7 0.0 copy-start.6
  9.7 0.7 %copy-done.6 = f32[4,3]{1,0:T(4,128)S(1)} copy-done((f32[4,3]{1,0:T(4,128)S(1)}, f32[4,3]{1,0:T(4,128)}, u32[]{:S(2)}) %copy-start.6) | copy-done | bytes 72
  10.4 2.2 %shard_map.55 = (bf16[512,2048]{1,0:T(8,128)(2,1)S(1)}, f32[4,32,1024]{2,1,0:T(8,128)S(1)}, f32[12,8,128]{2,1,0:T(8,128)S(1)}) custom-call(f32[4,3]{1,0:T(4,128)S(1)} %copy-done.6, bf16[1024,2048]{1,0:T(8,128)(2,1)} %bitcast.23, bf16[32,4,1024]{2,1,0:T(4,128)(2,1)S(1)} %bitcast.22), custom_call_target="tpu_custom_call" | custom-call | bytes 8388608 | tf_op jit(solution)/shard_map/pallas_call | solution.py:52
  12.6 0.0 collective-permute-done.edge_ref
  12.6 0.0 copy-start.4
  12.6 0.6 copy-done.4
  13.2 3.7 %all-to-all-done = bf16[4,24,2048]{2,1,0:T(8,128)(2,1)S(1)} async-done(((bf16[4,24,2048]{2,1,0:T(8,128)(2,1)}), bf16[4,24,2048]{2,1,0:T(8,128)(2,1)S(1)}, u32[]{:S(2)}, u32[]{:S(2)}) %all-to-all-start) | async-done | bytes 393248 | tf_op jit(solution)/shard_map/all_to_all | solution.py:252
  16.9 0.0 copy-start.1
  16.9 0.0 copy-start.2
  16.9 3.5 %shard_map.57 = bf16[4,4,24,512]{3,2,1,0:T(8,128)(2,1)S(1)} custom-call(f32[12,8,128]{2,1,0:T(8,128)S(1)} %get-tuple-element.11.tiles_ref, bf16[96,2048]{1,0:T(8,128)(2,1)S(1)} %bitcast.13, bf16[512,2048]{1,0:T(8,128)(2,1)S(1)} %get-tuple-element.14.near_ref, bf16[1024,2048]{1,0:T(8,128)(2,1)} %bitcast.24, f32[4,32,1024]{2,1,0:T(8,128)S(1)} %get-tuple-element.15.counts_ref), custom_call_target="tpu_custom_call" | custom-call | flops 805306368 | bytes 4194304 | tf_op jit(solution)/shard_map/pallas_call | solution.py:120
  20.4 19.9 %all_to_all.15.part_ref = bf16[16,24,512]{2,1,0:T(8,128)(2,1)S(1)} all-to-all(bf16[16,24,512]{2,1,0:T(8,128)(2,1)S(1)} %bitcast.19), channel_id=1, replica_groups=mesh['x'=4,'half'=2,'row'=16,'mat'=4] {'x','mat'}, dimensions={0} | all-to-all | bytes 786432 | tf_op jit(solution)/shard_map/all_to_all | solution.py:264
  40.3 0.7 %shard_map.58 = bf16[8,24,512]{2,1,0:T(8,128)(2,1)} custom-call(bf16[16,24,512]{2,1,0:T(8,128)(2,1)S(1)} %all_to_all.15.part_ref), custom_call_target="tpu_custom_call" | custom-call | tf_op jit(solution)/shard_map/pallas_call | solution.py:210
  41.0 7.1 %all-to-all-start.2 = ((bf16[8,24,512]{2,1,0:T(8,128)(2,1)}), bf16[8,24,512]{2,1,0:T(8,128)(2,1)S(1)}, u32[]{:S(2)}, u32[]{:S(2)}) async-start(bf16[8,24,512]{2,1,0:T(8,128)(2,1)} %shard_map.58), calls=%async_computation.2 | async-start | bytes 393216 | tf_op jit(solution)/shard_map/all_to_all | solution.py:266
  48.1 0.1 pad_add_fusion.where_ref
  48.2 0.0 copy-done.1
  48.2 0.0 copy-start.5
  48.2 0.8 %copy-done.5 = f32[3,2048]{1,0:T(4,128)S(1)} copy-done((f32[3,2048]{1,0:T(4,128)S(1)}, f32[3,2048]{1,0:T(4,128)}, u32[]{:S(2)}) %copy-start.5) | copy-done | bytes 24600
  48.9 0.9 %shard_map.59.smooth_ref = f32[3,8,2048]{2,1,0:T(8,128)S(1)} custom-call(s32[2]{0:T(128)S(1)} %pad_add_fusion.where_ref, f32[3,8,2048]{2,1,0:T(8,128)S(1)} %bitcast.17, bf16[96,2048]{1,0:T(8,128)(2,1)S(1)} %bitcast.14, f32[3,2048]{1,0:T(4,128)S(1)} %copy-done.5), custom_call_target="tpu_custom_call" | custom-call | flops 1966080 | bytes 589824 | tf_op jit(solution)/shard_map/pallas_call | solution.py:190
  49.8 11.1 %all-to-all-done.2 = bf16[8,24,512]{2,1,0:T(8,128)(2,1)S(1)} async-done(((bf16[8,24,512]{2,1,0:T(8,128)(2,1)}), bf16[8,24,512]{2,1,0:T(8,128)(2,1)S(1)}, u32[]{:S(2)}, u32[]{:S(2)}) %all-to-all-start.2) | async-done | bytes 196640 | tf_op jit(solution)/shard_map/all_to_all | solution.py:266
  60.9 0.0 copy-done.2
  61.0 0.8 %shard_map.60 = f32[3,8,2048]{2,1,0:T(8,128)} custom-call(bf16[4,2,24,512]{3,2,1,0:T(8,128)(2,1)S(1)} %bitcast.20, f32[3,8,2048]{2,1,0:T(8,128)S(1)} %shard_map.59.smooth_ref, bf16[3,3,8,2048]{3,2,1,0:T(8,128)(2,1)S(1)} %bitcast.21, f32[3,8,2048]{2,1,0:T(8,128)S(1)} %bitcast.18), custom_call_target="tpu_custom_call" | custom-call | tf_op jit(solution)/shard_map/pallas_call | solution.py:236
  (1 shorter events, 0.0 us)
Async XLA Ops:
  0.0 0.9 %copy-start = (f32[8,3,2048]{2,0,1:T(8,128)S(1)}, f32[8,3,2048]{2,0,1:T(8,128)}, u32[]{:S(2)}) copy-start(f32[8,3,2048]{2,0,1:T(8,128)} %param.5) | copy-start | bytes 589828
  1.7 15.2 %all-to-all-start = ((bf16[4,24,2048]{2,1,0:T(8,128)(2,1)}), bf16[4,24,2048]{2,1,0:T(8,128)(2,1)S(1)}, u32[]{:S(2)}, u32[]{:S(2)}) async-start(bf16[4,24,2048]{2,1,0:T(8,128)(2,1)} %shard_map.56), calls=%async_computation | async-start | bytes 786432 | tf_op jit(solution)/shard_map/all_to_all | solution.py:252
  8.1 4.5 %collective-permute-start = (f32[3,2048]{1,0:T(4,128)S(1)}, f32[3,2048]{1,0:T(4,128)S(1)}, u32[]{:S(2)}, u32[]{:S(2)}) collective-permute-start(f32[3,2048]{1,0:T(4,128)S(1)} %bitcast.25), channel_id=1, source_target_pairs={{3,4},{4,3},{7,8},{8,7},{11,12},{12,11},{15,16},{16,15},{19,20},{2... | collective-permute-start | bytes 73736 | tf_op jit(solution)/shard_map/ppermute | solution.py:259
  8.8 1.0 %copy-start.3 = (bf16[1,32,4,1024]{3,2,1,0:T(4,128)(2,1)S(1)}, bf16[1,32,4,1024]{3,2,1,0:T(4,128)(2,1)}, u32[]{:S(2)}) copy-start(bf16[1,32,4,1024]{3,2,1,0:T(4,128)(2,1)} %param.7) | copy-start | bytes 786436
  9.7 0.7 %copy-start.6 = (f32[4,3]{1,0:T(4,128)S(1)}, f32[4,3]{1,0:T(4,128)}, u32[]{:S(2)}) copy-start(f32[4,3]{1,0:T(4,128)} %atten_ref.1) | copy-start | bytes 148
  12.6 0.6 %copy-start.4 = (f32[3,2048]{1,0:T(4,128)}, f32[3,2048]{1,0:T(4,128)S(1)}, u32[]{:S(2)}) copy-start(f32[3,2048]{1,0:T(4,128)S(1)} %collective-permute-done.edge_ref) | copy-start | bytes 73732
  16.9 31.3 %copy-start.1 = (f32[8,3,2048]{2,0,1:T(8,128)S(1)}, f32[8,3,2048]{2,0,1:T(8,128)}, u32[]{:S(2)}) copy-start(f32[8,3,2048]{2,0,1:T(8,128)} %param.5) | copy-start | bytes 589828
  16.9 44.1 %copy-start.2 = (bf16[8,3,3,2048]{3,0,2,1:T(8,128)(2,1)S(1)}, bf16[8,3,3,2048]{3,0,2,1:T(8,128)(2,1)}, u32[]{:S(2)}) copy-start(bf16[8,3,3,2048]{3,0,2,1:T(8,128)(2,1)} %param.9) | copy-start | bytes 884740
  41.0 19.9 %all-to-all-start.2 = ((bf16[8,24,512]{2,1,0:T(8,128)(2,1)}), bf16[8,24,512]{2,1,0:T(8,128)(2,1)S(1)}, u32[]{:S(2)}, u32[]{:S(2)}) async-start(bf16[8,24,512]{2,1,0:T(8,128)(2,1)} %shard_map.58), calls=%async_computation.2 | async-start | bytes 393216 | tf_op jit(solution)/shard_map/all_to_all | solution.py:266
  48.2 0.8 %copy-start.5 = (f32[3,2048]{1,0:T(4,128)S(1)}, f32[3,2048]{1,0:T(4,128)}, u32[]{:S(2)}) copy-start(f32[3,2048]{1,0:T(4,128)} %copy-done.4) | copy-start | bytes 73732

commit v5 on v4

--- a/solution.py
+++ b/solution.py
@@ -12,16 +12,27 @@
 F32 = jnp.float32
 VMEM = pl.BlockSpec(memory_space=pltpu.VMEM)
 SMEM = pl.BlockSpec(memory_space=pltpu.SMEM)
+HBM = pl.BlockSpec(memory_space=pltpu.HBM)
 SMALL = 8 * 1024 * 1024
 MEDIUM = 49 * 1024 * 1024
 LARGE = 50 * 1024 * 1024
-
-
-def spread_kernel(vol_ref, out_ref):
-    mats, depth, _ = vol_ref.shape
-    rounded = jnp.concatenate([vol_ref[m] for m in range(mats)], 0).astype(BF16)
-    for copy in range(out_ref.shape[0]):
-        out_ref[copy] = rounded
+HUGE = 58 * 1024 * 1024
+
+
+def spread_kernel(vol_ref, out_ref, near_ref, rounded_ref, sems):
+    copy_in = pltpu.make_async_copy(vol_ref, near_ref, sems.at[0])
+    copy_in.start()
+    copy_in.wait()
+    mats = near_ref.shape[0]
+    rounded_ref[...] = jnp.concatenate([near_ref[m] for m in range(mats)], 0).astype(BF16)
+    copies = [
+        pltpu.make_async_copy(rounded_ref, out_ref.at[copy], sems.at[copy + 1])
+        for copy in range(out_ref.shape[0])
+    ]
+    for copy in copies:
+        copy.start()
+    for copy in copies:
+        copy.wait()
 
 
 def spread(volume, copies):
@@ -29,22 +40,35 @@
     return pl.pallas_call(
         spread_kernel,
         out_shape=jax.ShapeDtypeStruct((copies, mats * depth, pix), BF16),
-        in_specs=[VMEM],
-        out_specs=VMEM,
-        compiler_params=pltpu.CompilerParams(vmem_limit_bytes=SMALL),
+        in_specs=[HBM],
+        out_specs=HBM,
+        scratch_shapes=[
+            pltpu.VMEM(volume.shape, F32),
+            pltpu.VMEM((mats * depth, pix), BF16),
+            pltpu.SemaphoreType.DMA((copies + 1,)),
+        ],
+        compiler_params=pltpu.CompilerParams(vmem_limit_bytes=HUGE),
     )(volume)
 
 
-def stage_kernel(atten_ref, proj_ref, counts_ref, near_ref, binned_ref, tiles_ref, sem):
-    copy = pltpu.make_async_copy(proj_ref.at[: near_ref.shape[0]], near_ref, sem)
-    copy.start()
+def stage_kernel(
+    atten_ref, proj_ref, counts_ref, near_ref, binned_ref, tiles_ref, atten_near, counts_near, sems
+):
+    copy_atten = pltpu.make_async_copy(atten_ref, atten_near, sems.at[0])
+    copy_counts = pltpu.make_async_copy(counts_ref, counts_near, sems.at[1])
+    copy_proj = pltpu.make_async_copy(proj_ref.at[: near_ref.shape[0]], near_ref, sems.at[2])
+    copy_atten.start()
+    copy_counts.start()
+    copy_proj.start()
     bins, mats = atten_ref.shape
-    for b in range(bins):
-        binned_ref[b] = counts_ref[:, b, :].astype(F32)
+    copy_atten.wait()
     for b in range(bins):
         for m in range(mats):
-            tiles_ref[b * mats + m] = jnp.full(tiles_ref.shape[1:], atten_ref[b, m], F32)
-    copy.wait()
+            tiles_ref[b * mats + m] = jnp.full(tiles_ref.shape[1:], atten_near[b, m], F32)
+    copy_counts.wait()
+    for b in range(bins):
+        binned_ref[b] = counts_near[:, b, :].astype(F32)
+    copy_proj.wait()
 
 
 def stage(atten, projector, counts, held):
@@ -56,9 +80,13 @@
             jax.ShapeDtypeStruct((bins, slices, cols), F32),
             jax.ShapeDtypeStruct((atten.size, 8, 128), F32),
         ],
-        in_specs=[SMEM, pl.BlockSpec(memory_space=pltpu.HBM), VMEM],
+        in_specs=[HBM, HBM, HBM],
         out_specs=[VMEM] * 3,
-        scratch_shapes=[pltpu.SemaphoreType.DMA(())],
+        scratch_shapes=[
+            pltpu.SMEM(atten.shape, F32),
+            pltpu.VMEM(counts.shape, BF16),
+            pltpu.SemaphoreType.DMA((3,)),
+        ],
         compiler_params=pltpu.CompilerParams(vmem_limit_bytes=LARGE),
         cost_estimate=pl.CostEstimate(flops=0, bytes_accessed=4 * projector.size, transcendentals=0),
     )(atten, projector, counts)
@@ -120,7 +148,7 @@
     return pl.pallas_call(
         functools.partial(project_kernel, mats, counts.shape[0], slabs),
         out_shape=jax.ShapeDtypeStruct((owners, slabs, rows // slabs, pix // owners), BF16),
-        in_specs=[VMEM, VMEM, VMEM, pl.BlockSpec(memory_space=pltpu.HBM), VMEM],
+        in_specs=[VMEM, VMEM, VMEM, HBM, VMEM],
         out_specs=VMEM,
         scratch_shapes=[
             pltpu.VMEM((rows, cols), BF16),
@@ -251,17 +279,18 @@
     vol = volume.transpose(1, 0, 2)
     x_all = lax.all_to_all(spread(vol, slabs), "mat", 0, 0, tiled=True)
     x_all = x_all.reshape(slabs * rows, pix)
+    near, binned, tiles = stage(atten, projector[0], counts[0], projector.shape[1] // 2)
+    parts = project(tiles, x_all, near, projector[0], binned, owners, slabs, mats)
+    parts = parts.reshape(owners * slabs, rows, pix // owners)
     edge = jnp.where(slab == 0, vol[:, 0], vol[:, -1])
     pairs = []
     for g in range(groups - 1):
         last, start = g * slabs + slabs - 1, (g + 1) * slabs
         pairs += [(last, start), (start, last)]
+    parts, edge = lax.optimization_barrier((parts, edge))
+    parts = lax.all_to_all(parts, ("x", "mat"), 0, 0, tiled=True)
     edge = lax.ppermute(edge, ("row", "mat"), pairs)
-    near, binned, tiles = stage(atten, projector[0], counts[0], projector.shape[1] // 2)
-    x_all, edge, near = lax.optimization_barrier((x_all, edge, near))
-    parts = project(tiles, x_all, near, projector[0], binned, owners, slabs, mats)
-    parts = parts.reshape(owners * slabs, rows, pix // owners)
-    parts = lax.all_to_all(parts, ("x", "mat"), 0, 0, tiled=True)
+    parts, edge = lax.optimization_barrier((parts, edge))
     mine = total_copies(parts, float(views_all) ** (-0.5), owners * copies)
     grad = lax.all_to_all(mine, ("x", "half"), 0, 0, tiled=True)
     grad = grad.reshape(owners, copies, rows, pix // owners)

time: 62.2 us -> 60.3 us (0.969)
  the two profiles are of different devices: /device:TPU:200 before, /device:TPU:448 now
where the time goes in v5:
time: 60.3 us; the launch traced here: 59.4 us
  waiting for transfers between devices  26.2 us (43%)
  starting transfers between devices  19.8 us (33%)
  Pallas kernels  9.98 us (17%)
  local copies, waits for them, and re-layouts  2.27 us (4%)
  other arithmetic  1.12 us (2%)
    all_to_all x1, waiting for transfers between devices, body(): grad = lax.all_to_all(mine, ('x', 'half'), 0, 0, tiled=True)  9.9 us
    all_to_all x1, waiting for transfers between devices, body(): x_all = lax.all_to_all(spread(vol, slabs), 'mat', 0, 0, tiled=True)  6.72 us
    all_to_all x1, starting transfers between devices, body(): grad = lax.all_to_all(mine, ('x', 'half'), 0, 0, tiled=True)  6.24 us
    all_to_all x1, starting transfers between devices, body(): parts = lax.all_to_all(parts, ('x', 'mat'), 0, 0, tiled=True)  5.31 us
    ppermute x1, waiting for transfers between devices, body(): edge = lax.ppermute(edge, ('row', 'mat'), pairs)  5.18 us
    all_to_all x1, starting transfers between devices, body(): x_all = lax.all_to_all(spread(vol, slabs), 'mat', 0, 0, tiled=True)  4.88 us
    all_to_all x1, waiting for transfers between devices, body(): parts = lax.all_to_all(parts, ('x', 'mat'), 0, 0, tiled=True)  4.37 us
    pallas_call x1, Pallas kernels, project(): pl.pallas_call(functools.partial(project_kernel, mats, counts.shape[0], s...  4.23 us
  transfers between devices with their start and end apart: 4, of which 4 were waited for; matrix products, arithmetic and copies ran while one was open for 3% of the time, Pallas kernels for 4%

profile of v5, /device:TPU:448, one launch (start us, length us, event | category | flops | bytes accessed | tf_op | source)
XLA Modules:
  0.0 59.4 jit_solution(5502474741109344711)
XLA Ops:
  0.0 1.7 %shard_map.56 = bf16[4,24,2048]{2,1,0:T(8,128)(2,1)} custom-call(f32[3,8,2048]{2,1,0:T(8,128)} %bitcast.15), custom_call_target="tpu_custom_call" | custom-call | tf_op jit(solution)/shard_map/pallas_call | solution.py:40
  1.7 4.9 %all-to-all-start = ((bf16[4,24,2048]{2,1,0:T(8,128)(2,1)}), bf16[4,24,2048]{2,1,0:T(8,128)(2,1)S(1)}, u32[]{:S(2)}, u32[]{:S(2)}) async-start(bf16[4,24,2048]{2,1,0:T(8,128)(2,1)} %shard_map.56), calls=%async_computation | async-start | bytes 786432 | tf_op jit(solution)/shard_map/all_to_all | solution.py:280
  6.6 1.0 %broadcast_select_fusion = f32[3,1,2048]{2,1,0:T(1,128)S(1)} fusion(pred[]{:T(512)S(6)} %eq.7, f32[3,8,2048]{2,1,0:T(8,128)} %bitcast.16), kind=kLoop, calls=%fused_computation | loop fusion | flops 6144 | bytes 73729 | tf_op jit(solution)/shard_map/jit(_where)/select_n | solution.py:285
  7.7 0.6 %copy.8 = f32[3,1,2048]{2,0,1:T(4,128)} copy(f32[3,1,2048]{2,1,0:T(1,128)S(1)} %broadcast_select_fusion) | data formatting | bytes 49152
  8.3 0.0 copy-start.2
  8.3 0.9 %copy-done.2 = bf16[1,32,4,1024]{3,2,1,0:T(4,128)(2,1)S(1)} copy-done((bf16[1,32,4,1024]{3,2,1,0:T(4,128)(2,1)S(1)}, bf16[1,32,4,1024]{3,2,1,0:T(4,128)(2,1)}, u32[]{:S(2)}) %copy-start.2) | copy-done | bytes 262168
  9.2 0.0 copy-start.3
  9.2 0.7 %copy-done.3 = f32[4,3]{1,0:T(4,128)S(1)} copy-done((f32[4,3]{1,0:T(4,128)S(1)}, f32[4,3]{1,0:T(4,128)}, u32[]{:S(2)}) %copy-start.3) | copy-done | bytes 72
  9.9 1.6 %shard_map.55 = (bf16[512,2048]{1,0:T(8,128)(2,1)S(1)}, f32[4,32,1024]{2,1,0:T(8,128)S(1)}, f32[12,8,128]{2,1,0:T(8,128)S(1)}) custom-call(f32[4,3]{1,0:T(4,128)S(1)} %copy-done.3, bf16[1024,2048]{1,0:T(8,128)(2,1)} %bitcast.22, bf16[32,4,1024]{2,1,0:T(4,128)(2,1)S(1)} %bitcast.21), custom_call_target="tpu_custom_call" | custom-call | bytes 8388608 | tf_op jit(solution)/shard_map/pallas_call | solution.py:76
  11.6 6.7 %all-to-all-done = bf16[4,24,2048]{2,1,0:T(8,128)(2,1)S(1)} async-done(((bf16[4,24,2048]{2,1,0:T(8,128)(2,1)}), bf16[4,24,2048]{2,1,0:T(8,128)(2,1)S(1)}, u32[]{:S(2)}, u32[]{:S(2)}) %all-to-all-start) | async-done | bytes 393248 | tf_op jit(solution)/shard_map/all_to_all | solution.py:280
  18.3 0.0 copy-start
  18.3 0.0 copy-start.1
  18.3 4.2 %shard_map.57 = bf16[4,4,24,512]{3,2,1,0:T(8,128)(2,1)} custom-call(f32[12,8,128]{2,1,0:T(8,128)S(1)} %get-tuple-element.12.tiles_ref, bf16[96,2048]{1,0:T(8,128)(2,1)S(1)} %bitcast.13, bf16[512,2048]{1,0:T(8,128)(2,1)S(1)} %get-tuple-element.13.near_ref, bf16[1024,2048]{1,0:T(8,128)(2,1)} %bitcast.23, f32[4,32,1024]{2,1,0:T(8,128)S(1)} %get-tuple-element.14.counts_ref), custom_call_target="tpu_custom_call" | custom-call | flops 805306368 | bytes 4194304 | tf_op jit(solution)/shard_map/pallas_call | solution.py:148
  22.5 5.3 %all-to-all-start.1 = ((bf16[16,24,512]{2,1,0:T(8,128)(2,1)}), bf16[16,24,512]{2,1,0:T(8,128)(2,1)S(1)}, u32[]{:S(2)}, u32[]{:S(2)}) async-start(bf16[16,24,512]{2,1,0:T(8,128)(2,1)} %bitcast.4), calls=%async_computation.1 | async-start | bytes 786432 | tf_op jit(solution)/shard_map/all_to_all | solution.py:291
  27.9 3.4 %collective-permute-start = (f32[3,2048]{1,0:T(4,128)}, f32[3,2048]{1,0:T(4,128)S(1)}, u32[]{:S(2)}, u32[]{:S(2)}) collective-permute-start(f32[3,2048]{1,0:T(4,128)} %bitcast.24), channel_id=1, source_target_pairs={{3,4},{4,3},{7,8},{8,7},{11,12},{12,11},{15,16},{16,15},{19,20},{2... | collective-permute-start | bytes 73736 | tf_op jit(solution)/shard_map/ppermute | solution.py:292
  31.2 5.2 %collective-permute-done.edge_ref = f32[3,2048]{1,0:T(4,128)S(1)} collective-permute-done((f32[3,2048]{1,0:T(4,128)}, f32[3,2048]{1,0:T(4,128)S(1)}, u32[]{:S(2)}, u32[]{:S(2)}) %collective-permute-start) | collective-permute-done | bytes 24608 | tf_op jit(solution)/shard_map/ppermute | solution.py:292
  36.4 4.4 %all-to-all-done.1.part_ref = bf16[16,24,512]{2,1,0:T(8,128)(2,1)S(1)} async-done(((bf16[16,24,512]{2,1,0:T(8,128)(2,1)}), bf16[16,24,512]{2,1,0:T(8,128)(2,1)S(1)}, u32[]{:S(2)}, u32[]{:S(2)}) %all-to-all-start.1) | async-done | bytes 393248 | tf_op jit(solution)/shard_map/all_to_all | solution.py:291
  40.8 0.7 %shard_map.58 = bf16[8,24,512]{2,1,0:T(8,128)(2,1)} custom-call(bf16[16,24,512]{2,1,0:T(8,128)(2,1)S(1)} %all-to-all-done.1.part_ref), custom_call_target="tpu_custom_call" | custom-call | tf_op jit(solution)/shard_map/pallas_call | solution.py:238
  41.5 6.2 %all-to-all-start.2 = ((bf16[8,24,512]{2,1,0:T(8,128)(2,1)}), bf16[8,24,512]{2,1,0:T(8,128)(2,1)S(1)}, u32[]{:S(2)}, u32[]{:S(2)}) async-start(bf16[8,24,512]{2,1,0:T(8,128)(2,1)} %shard_map.58), calls=%async_computation.2 | async-start | bytes 393216 | tf_op jit(solution)/shard_map/all_to_all | solution.py:295
  47.8 0.1 pad_add_fusion.where_ref
  47.8 0.0 copy-done
  47.8 0.9 %shard_map.59.smooth_ref = f32[3,8,2048]{2,1,0:T(8,128)S(1)} custom-call(s32[2]{0:T(128)S(1)} %pad_add_fusion.where_ref, f32[3,8,2048]{2,1,0:T(8,128)S(1)} %bitcast.17, bf16[96,2048]{1,0:T(8,128)(2,1)S(1)} %bitcast.14, f32[3,2048]{1,0:T(4,128)S(1)} %collective-permute-done.edge_ref), custom_call_target="tpu_custom_call" | custom-call | flops 1966080 | bytes 589824 | tf_op jit(solution)/shard_map/pallas_call | solution.py:218
  48.7 9.9 %all-to-all-done.2 = bf16[8,24,512]{2,1,0:T(8,128)(2,1)S(1)} async-done(((bf16[8,24,512]{2,1,0:T(8,128)(2,1)}), bf16[8,24,512]{2,1,0:T(8,128)(2,1)S(1)}, u32[]{:S(2)}, u32[]{:S(2)}) %all-to-all-start.2) | async-done | bytes 196640 | tf_op jit(solution)/shard_map/all_to_all | solution.py:295
  58.6 0.0 copy-done.1
  58.6 0.8 %shard_map.60 = f32[3,8,2048]{2,1,0:T(8,128)} custom-call(bf16[4,2,24,512]{3,2,1,0:T(8,128)(2,1)S(1)} %bitcast.19, f32[3,8,2048]{2,1,0:T(8,128)S(1)} %shard_map.59.smooth_ref, bf16[3,3,8,2048]{3,2,1,0:T(8,128)(2,1)S(1)} %bitcast.20, f32[3,8,2048]{2,1,0:T(8,128)S(1)} %bitcast.18), custom_call_target="tpu_custom_call" | custom-call | tf_op jit(solution)/shard_map/pallas_call | solution.py:264
Async XLA Ops:
  1.7 16.6 %all-to-all-start = ((bf16[4,24,2048]{2,1,0:T(8,128)(2,1)}), bf16[4,24,2048]{2,1,0:T(8,128)(2,1)S(1)}, u32[]{:S(2)}, u32[]{:S(2)}) async-start(bf16[4,24,2048]{2,1,0:T(8,128)(2,1)} %shard_map.56), calls=%async_computation | async-start | bytes 786432 | tf_op jit(solution)/shard_map/all_to_all | solution.py:280
  8.3 0.9 %copy-start.2 = (bf16[1,32,4,1024]{3,2,1,0:T(4,128)(2,1)S(1)}, bf16[1,32,4,1024]{3,2,1,0:T(4,128)(2,1)}, u32[]{:S(2)}) copy-start(bf16[1,32,4,1024]{3,2,1,0:T(4,128)(2,1)} %param.7) | copy-start | bytes 786436
  9.2 0.7 %copy-start.3 = (f32[4,3]{1,0:T(4,128)S(1)}, f32[4,3]{1,0:T(4,128)}, u32[]{:S(2)}) copy-start(f32[4,3]{1,0:T(4,128)} %atten_ref.1) | copy-start | bytes 148
  18.3 29.6 %copy-start = (f32[8,3,2048]{2,0,1:T(8,128)S(1)}, f32[8,3,2048]{2,0,1:T(8,128)}, u32[]{:S(2)}) copy-start(f32[8,3,2048]{2,0,1:T(8,128)} %param.5) | copy-start | bytes 589828
  18.3 40.3 %copy-start.1 = (bf16[8,3,3,2048]{3,0,2,1:T(8,128)(2,1)S(1)}, bf16[8,3,3,2048]{3,0,2,1:T(8,128)(2,1)}, u32[]{:S(2)}) copy-start(bf16[8,3,3,2048]{3,0,2,1:T(8,128)(2,1)} %param.9) | copy-start | bytes 884740
  22.5 18.2 %all-to-all-start.1 = ((bf16[16,24,512]{2,1,0:T(8,128)(2,1)}), bf16[16,24,512]{2,1,0:T(8,128)(2,1)S(1)}, u32[]{:S(2)}, u32[]{:S(2)}) async-start(bf16[16,24,512]{2,1,0:T(8,128)(2,1)} %bitcast.4), calls=%async_computation.1 | async-start | bytes 786432 | tf_op jit(solution)/shard_map/all_to_all | solution.py:291
  27.9 8.6 %collective-permute-start = (f32[3,2048]{1,0:T(4,128)}, f32[3,2048]{1,0:T(4,128)S(1)}, u32[]{:S(2)}, u32[]{:S(2)}) collective-permute-start(f32[3,2048]{1,0:T(4,128)} %bitcast.24), channel_id=1, source_target_pairs={{3,4},{4,3},{7,8},{8,7},{11,12},{12,11},{15,16},{16,15},{19,20},{2... | collective-permute-start | bytes 73736 | tf_op jit(solution)/shard_map/ppermute | solution.py:292
  41.5 17.1 %all-to-all-start.2 = ((bf16[8,24,512]{2,1,0:T(8,128)(2,1)}), bf16[8,24,512]{2,1,0:T(8,128)(2,1)S(1)}, u32[]{:S(2)}, u32[]{:S(2)}) async-start(bf16[8,24,512]{2,1,0:T(8,128)(2,1)} %shard_map.58), calls=%async_computation.2 | async-start | bytes 393216 | tf_op jit(solution)/shard_map/all_to_all | solution.py:295

commit v6 on v5

--- a/solution.py
+++ b/solution.py
@@ -96,7 +96,7 @@
     return jnp.concatenate([tile] * (wide // tile.shape[1]), 1)
 
 
-def project_kernel(mats, bins, slabs, tiles_ref, x_ref, near_ref, proj_ref, counts_ref, out_ref, resid_ref, rest_ref, sems):
+def project_kernel(mats, bins, slabs, tiles_ref, x_ref, near_ref, proj_ref, counts_ref, out_ref, resid_ref, rest_ref, block_ref, sems, out_sems):
     rows, pix = x_ref.shape
     cols, held = proj_ref.shape[0], near_ref.shape[0]
     wide = 256
@@ -133,27 +133,39 @@
                     parts[m] = term if parts[m] is None else parts[m] + term
             blocks += parts
         resid_ref[:, at : at + wide] = jnp.concatenate(blocks, 0).astype(BF16)
-    owners, _, _, span = out_ref.shape
+    owners, sides, pairs, _, span = out_ref.shape
+    copies_out = []
     for owner in range(owners):
         own = slice(owner * span, (owner + 1) * span)
         back = jnp.dot(resid_ref[:, :held], near_ref[:, own], preferred_element_type=F32)
         back = back + jnp.dot(resid_ref[:, held:], rest_ref[:, own], preferred_element_type=F32)
         for slab in range(slabs):
-            out_ref[owner, slab] = back[slab * per_slab : (slab + 1) * per_slab].astype(BF16)
-
-
-def project(tiles, x_all, near, projector, counts, owners, slabs, mats):
+            block_ref[owner, slab % sides, slab // sides] = back[
+                slab * per_slab : (slab + 1) * per_slab
+            ].astype(BF16)
+        copies_out.append(
+            pltpu.make_async_copy(block_ref.at[owner], out_ref.at[owner], out_sems.at[owner])
+        )
+        copies_out[-1].start()
+    for copy in copies_out:
+        copy.wait()
+
+
+def project(tiles, x_all, near, projector, counts, owners, sides, slabs, mats):
     rows, pix = x_all.shape
     cols = counts.shape[2]
+    out = (owners, sides, slabs // sides, rows // slabs, pix // owners)
     return pl.pallas_call(
         functools.partial(project_kernel, mats, counts.shape[0], slabs),
-        out_shape=jax.ShapeDtypeStruct((owners, slabs, rows // slabs, pix // owners), BF16),
+        out_shape=jax.ShapeDtypeStruct(out, BF16),
         in_specs=[VMEM, VMEM, VMEM, HBM, VMEM],
-        out_specs=VMEM,
+        out_specs=HBM,
         scratch_shapes=[
             pltpu.VMEM((rows, cols), BF16),
             pltpu.VMEM((cols - near.shape[0], pix), BF16),
+            pltpu.VMEM(out, BF16),
             pltpu.SemaphoreType.DMA(((cols - near.shape[0]) // 256,)),
+            pltpu.SemaphoreType.DMA((owners,)),
         ],
         compiler_params=pltpu.CompilerParams(vmem_limit_bytes=MEDIUM),
         cost_estimate=pl.CostEstimate(
@@ -272,28 +284,32 @@
 
 def body(volume, projector, counts, atten, newton):
     depth, mats, pix = volume.shape
-    owners, copies, slabs, groups = (lax.axis_size(name) for name in ("x", "half", "mat", "row"))
-    views_all = projector.shape[0] * owners * copies * slabs
-    slab, group = lax.axis_index("mat"), lax.axis_index("row")
-    rows = mats * depth
+    owners, halves, groups, pairs, sides = (
+        lax.axis_size(name) for name in ("x", "half", "row", "pair", "side")
+    )
+    slabs = pairs * sides
+    views_all = projector.shape[0] * owners * halves * slabs
+    slab, group = lax.axis_index(("pair", "side")), lax.axis_index("row")
+    rows, span = mats * depth, pix // owners
     vol = volume.transpose(1, 0, 2)
-    x_all = lax.all_to_all(spread(vol, slabs), "mat", 0, 0, tiled=True)
+    x_all = lax.all_to_all(spread(vol, slabs), ("pair", "side"), 0, 0, tiled=True)
     x_all = x_all.reshape(slabs * rows, pix)
     near, binned, tiles = stage(atten, projector[0], counts[0], projector.shape[1] // 2)
-    parts = project(tiles, x_all, near, projector[0], binned, owners, slabs, mats)
-    parts = parts.reshape(owners * slabs, rows, pix // owners)
+    parts = project(tiles, x_all, near, projector[0], binned, owners, sides, slabs, mats)
+    parts = parts.reshape(owners * sides, pairs, rows, span)
     edge = jnp.where(slab == 0, vol[:, 0], vol[:, -1])
-    pairs = []
+    ends = []
     for g in range(groups - 1):
         last, start = g * slabs + slabs - 1, (g + 1) * slabs
-        pairs += [(last, start), (start, last)]
+        ends += [(last, start), (start, last)]
     parts, edge = lax.optimization_barrier((parts, edge))
-    parts = lax.all_to_all(parts, ("x", "mat"), 0, 0, tiled=True)
-    edge = lax.ppermute(edge, ("row", "mat"), pairs)
+    parts = lax.all_to_all(parts, ("x", "side"), 0, 0, tiled=True)
+    edge = lax.ppermute(edge, ("row", "pair", "side"), ends)
     parts, edge = lax.optimization_barrier((parts, edge))
-    mine = total_copies(parts, float(views_all) ** (-0.5), owners * copies)
-    grad = lax.all_to_all(mine, ("x", "half"), 0, 0, tiled=True)
-    grad = grad.reshape(owners, copies, rows, pix // owners)
+    mine = total_copies(parts, float(views_all) ** (-0.5), owners * halves)
+    mine = mine.reshape(owners * halves * pairs, rows, span)
+    grad = lax.all_to_all(mine, ("x", "half", "pair"), 0, 0, tiled=True)
+    grad = grad.reshape(owners, halves * pairs, rows, span)
     is_first = jnp.logical_and(slab == 0, group == 0).astype(jnp.int32)
     smoothed = smooth(jnp.stack([slab, is_first]).astype(jnp.int32), vol, x_all, edge)
     updated = newton_step(grad, smoothed, newton.transpose(1, 2, 0, 3), vol)
@@ -301,17 +317,18 @@
 
 
 def solution(mesh):
-    shape = mesh.devices.shape
+    views, groups, slabs = mesh.devices.shape
     mesh = jax.sharding.Mesh(
-        mesh.devices.reshape(shape[0] // 2, 2, *shape[1:]), ("x", "half", "row", "mat")
+        mesh.devices.reshape(views // 2, 2, groups, slabs // 2, 2),
+        ("x", "half", "row", "pair", "side"),
     )
-    view = ("x", "half", "mat")
+    view, slice_axes = ("x", "half", "pair", "side"), ("row", "pair", "side")
     in_specs = (
-        P(("row", "mat"), None, None),
+        P(slice_axes, None, None),
         P(view, None, None),
         P(view, "row", None, None),
         P(),
-        P(("row", "mat"), None, None, None),
+        P(slice_axes, None, None, None),
     )
-    out_specs = P(("row", "mat"), None, None)
+    out_specs = P(slice_axes, None, None)
     return jax.shard_map(body, mesh=mesh, in_specs=in_specs, out_specs=out_specs, check_vma=False)

time: 60.3 us -> 61.4 us (1.018)
  the two profiles are of different devices: /device:TPU:448 before, /device:TPU:201 now
where the time goes in v6:
time: 61.4 us; the launch traced here: 60.9 us
  starting transfers between devices  23.8 us (39%)
  waiting for transfers between devices  23.6 us (38%)
  Pallas kernels  9.99 us (16%)
  local copies, waits for them, and re-layouts  2.27 us (4%)
  other arithmetic  1.12 us (2%)
    all_to_all x1, waiting for transfers between devices, body(): grad = lax.all_to_all(mine, ('x', 'half', 'pair'), 0, 0, tiled=True)  15.1 us
    all_to_all x1, starting transfers between devices, body(): grad = lax.all_to_all(mine, ('x', 'half', 'pair'), 0, 0, tiled=True)  11.7 us
    all_to_all x1, starting transfers between devices, body(): parts = lax.all_to_all(parts, ('x', 'side'), 0, 0, tiled=True)  6.74 us
    all_to_all x1, waiting for transfers between devices, body(): parts = lax.all_to_all(parts, ('x', 'side'), 0, 0, tiled=True)  5.28 us
    all_to_all x1, starting transfers between devices, body(): lax.all_to_all(spread(vol, slabs), ('pair', 'side'), 0, 0, tiled=True)  4.77 us
    pallas_call x1, Pallas kernels, project(): pl.pallas_call(functools.partial(project_kernel, mats, counts.shape[0], s...  4.15 us
    all_to_all x1, waiting for transfers between devices, body(): lax.all_to_all(spread(vol, slabs), ('pair', 'side'), 0, 0, tiled=True)  3.22 us
    unnamed x9, local copies, waits for them, and re-layouts  2.27 us
  transfers between devices with their start and end apart: 4, of which 3 were waited for; matrix products, arithmetic and copies ran while one was open for 3% of the time, Pallas kernels for 4%

profile of v6, /device:TPU:201, one launch (start us, length us, event | category | flops | bytes accessed | tf_op | source)
XLA Modules:
  0.0 60.9 jit_solution(14614254478760742670)
XLA Ops:
  0.0 1.7 %shard_map.56 = bf16[4,24,2048]{2,1,0:T(8,128)(2,1)} custom-call(f32[3,8,2048]{2,1,0:T(8,128)} %bitcast.16), custom_call_target="tpu_custom_call" | custom-call | tf_op jit(solution)/shard_map/pallas_call | solution.py:40
  1.7 4.8 %all-to-all-start = ((bf16[4,24,2048]{2,1,0:T(8,128)(2,1)}), bf16[4,24,2048]{2,1,0:T(8,128)(2,1)S(1)}, u32[]{:S(2)}, u32[]{:S(2)}) async-start(bf16[4,24,2048]{2,1,0:T(8,128)(2,1)} %shard_map.56), calls=%async_computation | async-start | bytes 786432 | tf_op jit(solution)/shard_map/all_to_all | solution.py:295
  6.5 1.0 %broadcast_select_fusion = f32[3,1,2048]{2,1,0:T(1,128)S(1)} fusion(pred[]{:T(512)S(6)} %eq.7, f32[3,8,2048]{2,1,0:T(8,128)} %bitcast.17), kind=kLoop, calls=%fused_computation | loop fusion | flops 6144 | bytes 73729 | tf_op jit(solution)/shard_map/jit(_where)/select_n | solution.py:300
  7.6 0.6 %copy.8 = f32[3,1,2048]{2,0,1:T(4,128)} copy(f32[3,1,2048]{2,1,0:T(1,128)S(1)} %broadcast_select_fusion) | data formatting | bytes 49152
  8.2 0.0 copy-start.2
  8.2 0.9 %copy-done.2 = bf16[1,32,4,1024]{3,2,1,0:T(4,128)(2,1)S(1)} copy-done((bf16[1,32,4,1024]{3,2,1,0:T(4,128)(2,1)S(1)}, bf16[1,32,4,1024]{3,2,1,0:T(4,128)(2,1)}, u32[]{:S(2)}) %copy-start.2) | copy-done | bytes 262168
  9.1 0.0 copy-start.3
  9.1 0.7 %copy-done.3 = f32[4,3]{1,0:T(4,128)S(1)} copy-done((f32[4,3]{1,0:T(4,128)S(1)}, f32[4,3]{1,0:T(4,128)}, u32[]{:S(2)}) %copy-start.3) | copy-done | bytes 72
  9.8 1.6 %shard_map.55 = (bf16[512,2048]{1,0:T(8,128)(2,1)S(1)}, f32[4,32,1024]{2,1,0:T(8,128)S(1)}, f32[12,8,128]{2,1,0:T(8,128)S(1)}) custom-call(f32[4,3]{1,0:T(4,128)S(1)} %copy-done.3, bf16[1024,2048]{1,0:T(8,128)(2,1)} %bitcast.23, bf16[32,4,1024]{2,1,0:T(4,128)(2,1)S(1)} %bitcast.22), custom_call_target="tpu_custom_call" | custom-call | bytes 8388608 | tf_op jit(solution)/shard_map/pallas_call | solution.py:76
  11.5 3.2 %all-to-all-done = bf16[4,24,2048]{2,1,0:T(8,128)(2,1)S(1)} async-done(((bf16[4,24,2048]{2,1,0:T(8,128)(2,1)}), bf16[4,24,2048]{2,1,0:T(8,128)(2,1)S(1)}, u32[]{:S(2)}, u32[]{:S(2)}) %all-to-all-start) | async-done | bytes 393248 | tf_op jit(solution)/shard_map/all_to_all | solution.py:295
  14.7 0.0 copy-start
  14.7 0.0 copy-start.1
  14.7 4.1 %shard_map.57 = bf16[4,2,2,24,512]{4,3,2,1,0:T(8,128)(2,1)} custom-call(f32[12,8,128]{2,1,0:T(8,128)S(1)} %get-tuple-element.12.tiles_ref, bf16[96,2048]{1,0:T(8,128)(2,1)S(1)} %bitcast.14, bf16[512,2048]{1,0:T(8,128)(2,1)S(1)} %get-tuple-element.13.near_ref, bf16[1024,2048]{1,0:T(8,128)(2,1)} %bitcast.24, f32[4,32,1024]{2,1,0:T(8,128)S(1)} %get-tuple-element.14.counts_ref), custom_call_target="tpu_custom_call" | custom-call | flops 805306368 | bytes 4194304 | tf_op jit(solution)/shard_map/pallas_call | solution.py:158
  18.8 6.7 %all-to-all-start.1 = ((bf16[8,2,24,512]{3,2,1,0:T(8,128)(2,1)}), bf16[8,2,24,512]{3,2,1,0:T(8,128)(2,1)S(1)}, u32[]{:S(2)}, u32[]{:S(2)}) async-start(bf16[8,2,24,512]{3,2,1,0:T(8,128)(2,1)} %bitcast.4), calls=%async_computation.1 | async-start | bytes 786432 | tf_op jit(solution)/shard_map/all_to_all | solution.py:306
  25.6 0.7 %collective-permute-start = (f32[3,2048]{1,0:T(4,128)}, f32[3,2048]{1,0:T(4,128)S(1)}, u32[]{:S(2)}, u32[]{:S(2)}) collective-permute-start(f32[3,2048]{1,0:T(4,128)} %bitcast.25), channel_id=1, source_target_pairs={{3,4},{4,3},{7,8},{8,7},{11,12},{12,11},{15,16},{16,15},{19,20},{2... | collective-permute-start | bytes 73736 | tf_op jit(solution)/shard_map/ppermute | solution.py:307
  26.2 0.0 collective-permute-done.edge_ref
  26.3 5.3 %all-to-all-done.1.part_ref = bf16[8,2,24,512]{3,2,1,0:T(8,128)(2,1)S(1)} async-done(((bf16[8,2,24,512]{3,2,1,0:T(8,128)(2,1)}), bf16[8,2,24,512]{3,2,1,0:T(8,128)(2,1)S(1)}, u32[]{:S(2)}, u32[]{:S(2)}) %all-to-all-start.1) | async-done | bytes 393248 | tf_op jit(solution)/shard_map/all_to_all | solution.py:306
  31.5 0.8 %shard_map.58 = bf16[8,2,24,512]{3,2,1,0:T(8,128)(2,1)} custom-call(bf16[8,2,24,512]{3,2,1,0:T(8,128)(2,1)S(1)} %all-to-all-done.1.part_ref), custom_call_target="tpu_custom_call" | custom-call | tf_op jit(solution)/shard_map/pallas_call | solution.py:250
  32.3 11.7 %all-to-all-start.2 = ((bf16[16,24,512]{2,1,0:T(8,128)(2,1)}), bf16[16,24,512]{2,1,0:T(8,128)(2,1)S(1)}, u32[]{:S(2)}, u32[]{:S(2)}) async-start(bf16[16,24,512]{2,1,0:T(8,128)(2,1)} %bitcast.5), calls=%async_computation.2 | async-start | bytes 786432 | tf_op jit(solution)/shard_map/all_to_all | solution.py:311
  44.0 0.1 pad_add_fusion.where_ref
  44.1 0.0 copy-done
  44.1 0.9 %shard_map.59.smooth_ref = f32[3,8,2048]{2,1,0:T(8,128)S(1)} custom-call(s32[2]{0:T(128)S(1)} %pad_add_fusion.where_ref, f32[3,8,2048]{2,1,0:T(8,128)S(1)} %bitcast.18, bf16[96,2048]{1,0:T(8,128)(2,1)S(1)} %bitcast.15, f32[3,2048]{1,0:T(4,128)S(1)} %collective-permute-done.edge_ref), custom_call_target="tpu_custom_call" | custom-call | flops 1966080 | bytes 589824 | tf_op jit(solution)/shard_map/pallas_call | solution.py:230
  45.0 15.1 %all-to-all-done.2 = bf16[16,24,512]{2,1,0:T(8,128)(2,1)S(1)} async-done(((bf16[16,24,512]{2,1,0:T(8,128)(2,1)}), bf16[16,24,512]{2,1,0:T(8,128)(2,1)S(1)}, u32[]{:S(2)}, u32[]{:S(2)}) %all-to-all-start.2) | async-done | bytes 393248 | tf_op jit(solution)/shard_map/all_to_all | solution.py:311
  60.1 0.0 copy-done.1
  60.1 0.8 %shard_map.60 = f32[3,8,2048]{2,1,0:T(8,128)} custom-call(bf16[4,4,24,512]{3,2,1,0:T(8,128)(2,1)S(1)} %bitcast.20, f32[3,8,2048]{2,1,0:T(8,128)S(1)} %shard_map.59.smooth_ref, bf16[3,3,8,2048]{3,2,1,0:T(8,128)(2,1)S(1)} %bitcast.21, f32[3,8,2048]{2,1,0:T(8,128)S(1)} %bitcast.19), custom_call_target="tpu_custom_call" | custom-call | tf_op jit(solution)/shard_map/pallas_call | solution.py:276
Async XLA Ops:
  1.7 12.9 %all-to-all-start = ((bf16[4,24,2048]{2,1,0:T(8,128)(2,1)}), bf16[4,24,2048]{2,1,0:T(8,128)(2,1)S(1)}, u32[]{:S(2)}, u32[]{:S(2)}) async-start(bf16[4,24,2048]{2,1,0:T(8,128)(2,1)} %shard_map.56), calls=%async_computation | async-start | bytes 786432 | tf_op jit(solution)/shard_map/all_to_all | solution.py:295
  8.2 0.9 %copy-start.2 = (bf16[1,32,4,1024]{3,2,1,0:T(4,128)(2,1)S(1)}, bf16[1,32,4,1024]{3,2,1,0:T(4,128)(2,1)}, u32[]{:S(2)}) copy-start(bf16[1,32,4,1024]{3,2,1,0:T(4,128)(2,1)} %param.7) | copy-start | bytes 786436
  9.1 0.7 %copy-start.3 = (f32[4,3]{1,0:T(4,128)S(1)}, f32[4,3]{1,0:T(4,128)}, u32[]{:S(2)}) copy-start(f32[4,3]{1,0:T(4,128)} %atten_ref.1) | copy-start | bytes 148
  14.7 29.4 %copy-start = (f32[8,3,2048]{2,0,1:T(8,128)S(1)}, f32[8,3,2048]{2,0,1:T(8,128)}, u32[]{:S(2)}) copy-start(f32[8,3,2048]{2,0,1:T(8,128)} %param.5) | copy-start | bytes 589828
  14.7 45.4 %copy-start.1 = (bf16[8,3,3,2048]{3,0,2,1:T(8,128)(2,1)S(1)}, bf16[8,3,3,2048]{3,0,2,1:T(8,128)(2,1)}, u32[]{:S(2)}) copy-start(bf16[8,3,3,2048]{3,0,2,1:T(8,128)(2,1)} %param.9) | copy-start | bytes 884740
  18.8 12.7 %all-to-all-start.1 = ((bf16[8,2,24,512]{3,2,1,0:T(8,128)(2,1)}), bf16[8,2,24,512]{3,2,1,0:T(8,128)(2,1)S(1)}, u32[]{:S(2)}, u32[]{:S(2)}) async-start(bf16[8,2,24,512]{3,2,1,0:T(8,128)(2,1)} %bitcast.4), calls=%async_computation.1 | async-start | bytes 786432 | tf_op jit(solution)/shard_map/all_to_all | solution.py:306
  25.6 0.7 %collective-permute-start = (f32[3,2048]{1,0:T(4,128)}, f32[3,2048]{1,0:T(4,128)S(1)}, u32[]{:S(2)}, u32[]{:S(2)}) collective-permute-start(f32[3,2048]{1,0:T(4,128)} %bitcast.25), channel_id=1, source_target_pairs={{3,4},{4,3},{7,8},{8,7},{11,12},{12,11},{15,16},{16,15},{19,20},{2... | collective-permute-start | bytes 73736 | tf_op jit(solution)/shard_map/ppermute | solution.py:307
  32.3 27.7 %all-to-all-start.2 = ((bf16[16,24,512]{2,1,0:T(8,128)(2,1)}), bf16[16,24,512]{2,1,0:T(8,128)(2,1)S(1)}, u32[]{:S(2)}, u32[]{:S(2)}) async-start(bf16[16,24,512]{2,1,0:T(8,128)(2,1)} %bitcast.5), calls=%async_computation.2 | async-start | bytes 786432 | tf_op jit(solution)/shard_map/all_to_all | solution.py:311

commit v7 on v6

--- a/solution.py
+++ b/solution.py
@@ -302,11 +302,10 @@
     for g in range(groups - 1):
         last, start = g * slabs + slabs - 1, (g + 1) * slabs
         ends += [(last, start), (start, last)]
-    parts, edge = lax.optimization_barrier((parts, edge))
     parts = lax.all_to_all(parts, ("x", "side"), 0, 0, tiled=True)
+    mine = total_copies(parts, float(views_all) ** (-0.5), owners * halves)
+    mine, edge = lax.optimization_barrier((mine, edge))
     edge = lax.ppermute(edge, ("row", "pair", "side"), ends)
-    parts, edge = lax.optimization_barrier((parts, edge))
-    mine = total_copies(parts, float(views_all) ** (-0.5), owners * halves)
     mine = mine.reshape(owners * halves * pairs, rows, span)
     grad = lax.all_to_all(mine, ("x", "half", "pair"), 0, 0, tiled=True)
     grad = grad.reshape(owners, halves * pairs, rows, span)

time: 61.4 us -> 58.3 us (0.950)
  the two profiles are of different devices: /device:TPU:201 before, /device:TPU:448 now
where the time goes in v7:
time: 58.3 us; the launch traced here: 57.8 us
  waiting for transfers between devices  27.9 us (48%)
  starting transfers between devices  18 us (31%)
  Pallas kernels  9.99 us (17%)
  local copies, waits for them, and re-layouts  1.65 us (3%)
    all_to_all x1, waiting for transfers between devices, body(): lax.all_to_all(spread(vol, slabs), ('pair', 'side'), 0, 0, tiled=True)  8.41 us
    all_to_all x1, waiting for transfers between devices, body(): parts = lax.all_to_all(parts, ('x', 'side'), 0, 0, tiled=True)  7.92 us
    all_to_all x1, starting transfers between devices, body(): grad = lax.all_to_all(mine, ('x', 'half', 'pair'), 0, 0, tiled=True)  6.42 us
    ppermute x1, waiting for transfers between devices, body(): edge = lax.ppermute(edge, ('row', 'pair', 'side'), ends)  6.06 us
    all_to_all x1, waiting for transfers between devices, body(): grad = lax.all_to_all(mine, ('x', 'half', 'pair'), 0, 0, tiled=True)  5.53 us
    all_to_all x1, starting transfers between devices, body(): lax.all_to_all(spread(vol, slabs), ('pair', 'side'), 0, 0, tiled=True)  4.88 us
    all_to_all x1, starting transfers between devices, body(): parts = lax.all_to_all(parts, ('x', 'side'), 0, 0, tiled=True)  4.31 us
    pallas_call x1, Pallas kernels, project(): pl.pallas_call(functools.partial(project_kernel, mats, counts.shape[0], s...  4.15 us
  transfers between devices with their start and end apart: 4, of which 4 were waited for; matrix products, arithmetic and copies ran while one was open for 0% of the time, Pallas kernels for 4%

profile of v7, /device:TPU:448, one launch (start us, length us, event | category | flops | bytes accessed | tf_op | source)
XLA Modules:
  0.0 57.8 jit_solution(5112264856072519025)
XLA Ops:
  0.0 1.7 %shard_map.56 = bf16[4,24,2048]{2,1,0:T(8,128)(2,1)} custom-call(f32[3,8,2048]{2,1,0:T(8,128)} %bitcast.16), custom_call_target="tpu_custom_call" | custom-call | tf_op jit(solution)/shard_map/pallas_call | solution.py:40
  1.7 4.9 %all-to-all-start = ((bf16[4,24,2048]{2,1,0:T(8,128)(2,1)}), bf16[4,24,2048]{2,1,0:T(8,128)(2,1)S(1)}, u32[]{:S(2)}, u32[]{:S(2)}) async-start(bf16[4,24,2048]{2,1,0:T(8,128)(2,1)} %shard_map.56), calls=%async_computation | async-start | bytes 786432 | tf_op jit(solution)/shard_map/all_to_all | solution.py:295
  6.6 0.0 copy-start.2
  6.6 0.9 %copy-done.2 = bf16[1,32,4,1024]{3,2,1,0:T(4,128)(2,1)S(1)} copy-done((bf16[1,32,4,1024]{3,2,1,0:T(4,128)(2,1)S(1)}, bf16[1,32,4,1024]{3,2,1,0:T(4,128)(2,1)}, u32[]{:S(2)}) %copy-start.2) | copy-done | bytes 262168
  7.6 0.0 copy-start.3
  7.6 0.7 %copy-done.3 = f32[4,3]{1,0:T(4,128)S(1)} copy-done((f32[4,3]{1,0:T(4,128)S(1)}, f32[4,3]{1,0:T(4,128)}, u32[]{:S(2)}) %copy-start.3) | copy-done | bytes 72
  8.2 1.6 %shard_map.55 = (bf16[512,2048]{1,0:T(8,128)(2,1)S(1)}, f32[4,32,1024]{2,1,0:T(8,128)S(1)}, f32[12,8,128]{2,1,0:T(8,128)S(1)}) custom-call(f32[4,3]{1,0:T(4,128)S(1)} %copy-done.3, bf16[1024,2048]{1,0:T(8,128)(2,1)} %bitcast.23, bf16[32,4,1024]{2,1,0:T(4,128)(2,1)S(1)} %bitcast.22), custom_call_target="tpu_custom_call" | custom-call | bytes 8388608 | tf_op jit(solution)/shard_map/pallas_call | solution.py:76
  9.9 8.4 %all-to-all-done = bf16[4,24,2048]{2,1,0:T(8,128)(2,1)S(1)} async-done(((bf16[4,24,2048]{2,1,0:T(8,128)(2,1)}), bf16[4,24,2048]{2,1,0:T(8,128)(2,1)S(1)}, u32[]{:S(2)}, u32[]{:S(2)}) %all-to-all-start) | async-done | bytes 393248 | tf_op jit(solution)/shard_map/all_to_all | solution.py:295
  18.3 0.0 copy-start
  18.3 0.0 copy-start.1
  18.3 4.1 %shard_map.57 = bf16[4,2,2,24,512]{4,3,2,1,0:T(8,128)(2,1)} custom-call(f32[12,8,128]{2,1,0:T(8,128)S(1)} %get-tuple-element.10.tiles_ref, bf16[96,2048]{1,0:T(8,128)(2,1)S(1)} %bitcast.14, bf16[512,2048]{1,0:T(8,128)(2,1)S(1)} %get-tuple-element.11.near_ref, bf16[1024,2048]{1,0:T(8,128)(2,1)} %bitcast.24, f32[4,32,1024]{2,1,0:T(8,128)S(1)} %get-tuple-element.12.counts_ref), custom_call_target="tpu_custom_call" | custom-call | flops 805306368 | bytes 4194304 | tf_op jit(solution)/shard_map/pallas_call | solution.py:158
  22.5 4.3 %all-to-all-start.1 = ((bf16[8,2,24,512]{3,2,1,0:T(8,128)(2,1)}), bf16[8,2,24,512]{3,2,1,0:T(8,128)(2,1)S(1)}, u32[]{:S(2)}, u32[]{:S(2)}) async-start(bf16[8,2,24,512]{3,2,1,0:T(8,128)(2,1)} %bitcast.4), calls=%async_computation.1 | async-start | bytes 786432 | tf_op jit(solution)/shard_map/all_to_all | solution.py:305
  26.8 0.0 copy-done
  26.8 7.9 %all-to-all-done.1.part_ref = bf16[8,2,24,512]{3,2,1,0:T(8,128)(2,1)S(1)} async-done(((bf16[8,2,24,512]{3,2,1,0:T(8,128)(2,1)}), bf16[8,2,24,512]{3,2,1,0:T(8,128)(2,1)S(1)}, u32[]{:S(2)}, u32[]{:S(2)}) %all-to-all-start.1) | async-done | bytes 393248 | tf_op jit(solution)/shard_map/all_to_all | solution.py:305
  34.8 0.8 %shard_map.58 = bf16[8,2,24,512]{3,2,1,0:T(8,128)(2,1)} custom-call(bf16[8,2,24,512]{3,2,1,0:T(8,128)(2,1)S(1)} %all-to-all-done.1.part_ref), custom_call_target="tpu_custom_call" | custom-call | tf_op jit(solution)/shard_map/pallas_call | solution.py:250
  35.6 6.4 %all-to-all-start.2 = ((bf16[16,24,512]{2,1,0:T(8,128)(2,1)}), bf16[16,24,512]{2,1,0:T(8,128)(2,1)S(1)}, u32[]{:S(2)}, u32[]{:S(2)}) async-start(bf16[16,24,512]{2,1,0:T(8,128)(2,1)} %bitcast.5), calls=%async_computation.2 | async-start | bytes 786432 | tf_op jit(solution)/shard_map/all_to_all | solution.py:310
  42.0 2.4 %collective-permute-start = (f32[3,2048]{1,0:T(4,128)S(1)}, f32[3,2048]{1,0:T(4,128)S(1)}, u32[]{:S(2)}, u32[]{:S(2)}) collective-permute-start(f32[3,2048]{1,0:T(4,128)S(1)} %bitcast.25), channel_id=1, source_target_pairs={{3,4},{4,3},{7,8},{8,7},{11,12},{12,11},{15,16},{16,15},{19,20},{2... | collective-permute-start | bytes 73736 | tf_op jit(solution)/shard_map/ppermute | solution.py:308
  44.4 0.1 pad_add_fusion.where_ref
  44.5 6.1 %collective-permute-done.edge_ref = f32[3,2048]{1,0:T(4,128)S(1)} collective-permute-done((f32[3,2048]{1,0:T(4,128)S(1)}, f32[3,2048]{1,0:T(4,128)S(1)}, u32[]{:S(2)}, u32[]{:S(2)}) %collective-permute-start) | collective-permute-done | bytes 24608 | tf_op jit(solution)/shard_map/ppermute | solution.py:308
  50.6 0.9 %shard_map.59.smooth_ref = f32[3,8,2048]{2,1,0:T(8,128)S(1)} custom-call(s32[2]{0:T(128)S(1)} %pad_add_fusion.where_ref, f32[3,8,2048]{2,1,0:T(8,128)S(1)} %bitcast.18, bf16[96,2048]{1,0:T(8,128)(2,1)S(1)} %bitcast.15, f32[3,2048]{1,0:T(4,128)S(1)} %collective-permute-done.edge_ref), custom_call_target="tpu_custom_call" | custom-call | flops 1966080 | bytes 589824 | tf_op jit(solution)/shard_map/pallas_call | solution.py:230
  51.4 5.5 %all-to-all-done.2 = bf16[16,24,512]{2,1,0:T(8,128)(2,1)S(1)} async-done(((bf16[16,24,512]{2,1,0:T(8,128)(2,1)}), bf16[16,24,512]{2,1,0:T(8,128)(2,1)S(1)}, u32[]{:S(2)}, u32[]{:S(2)}) %all-to-all-start.2) | async-done | bytes 393248 | tf_op jit(solution)/shard_map/all_to_all | solution.py:310
  57.0 0.0 copy-done.1
  57.0 0.8 %shard_map.60 = f32[3,8,2048]{2,1,0:T(8,128)} custom-call(bf16[4,4,24,512]{3,2,1,0:T(8,128)(2,1)S(1)} %bitcast.20, f32[3,8,2048]{2,1,0:T(8,128)S(1)} %shard_map.59.smooth_ref, bf16[3,3,8,2048]{3,2,1,0:T(8,128)(2,1)S(1)} %bitcast.21, f32[3,8,2048]{2,1,0:T(8,128)S(1)} %bitcast.19), custom_call_target="tpu_custom_call" | custom-call | tf_op jit(solution)/shard_map/pallas_call | solution.py:276
  (2 shorter events, 0.0 us)
Async XLA Ops:
  1.7 16.6 %all-to-all-start = ((bf16[4,24,2048]{2,1,0:T(8,128)(2,1)}), bf16[4,24,2048]{2,1,0:T(8,128)(2,1)S(1)}, u32[]{:S(2)}, u32[]{:S(2)}) async-start(bf16[4,24,2048]{2,1,0:T(8,128)(2,1)} %shard_map.56), calls=%async_computation | async-start | bytes 786432 | tf_op jit(solution)/shard_map/all_to_all | solution.py:295
  6.6 0.9 %copy-start.2 = (bf16[1,32,4,1024]{3,2,1,0:T(4,128)(2,1)S(1)}, bf16[1,32,4,1024]{3,2,1,0:T(4,128)(2,1)}, u32[]{:S(2)}) copy-start(bf16[1,32,4,1024]{3,2,1,0:T(4,128)(2,1)} %param.7) | copy-start | bytes 786436
  7.6 0.7 %copy-start.3 = (f32[4,3]{1,0:T(4,128)S(1)}, f32[4,3]{1,0:T(4,128)}, u32[]{:S(2)}) copy-start(f32[4,3]{1,0:T(4,128)} %atten_ref.1) | copy-start | bytes 148
  18.3 8.5 %copy-start = (f32[8,3,2048]{2,0,1:T(8,128)S(1)}, f32[8,3,2048]{2,0,1:T(8,128)}, u32[]{:S(2)}) copy-start(f32[8,3,2048]{2,0,1:T(8,128)} %param.5) | copy-start | bytes 589828
  18.3 38.7 %copy-start.1 = (bf16[8,3,3,2048]{3,0,2,1:T(8,128)(2,1)S(1)}, bf16[8,3,3,2048]{3,0,2,1:T(8,128)(2,1)}, u32[]{:S(2)}) copy-start(bf16[8,3,3,2048]{3,0,2,1:T(8,128)(2,1)} %param.9) | copy-start | bytes 884740
  22.5 12.3 %all-to-all-start.1 = ((bf16[8,2,24,512]{3,2,1,0:T(8,128)(2,1)}), bf16[8,2,24,512]{3,2,1,0:T(8,128)(2,1)S(1)}, u32[]{:S(2)}, u32[]{:S(2)}) async-start(bf16[8,2,24,512]{3,2,1,0:T(8,128)(2,1)} %bitcast.4), calls=%async_computation.1 | async-start | bytes 786432 | tf_op jit(solution)/shard_map/all_to_all | solution.py:305
  35.6 21.4 %all-to-all-start.2 = ((bf16[16,24,512]{2,1,0:T(8,128)(2,1)}), bf16[16,24,512]{2,1,0:T(8,128)(2,1)S(1)}, u32[]{:S(2)}, u32[]{:S(2)}) async-start(bf16[16,24,512]{2,1,0:T(8,128)(2,1)} %bitcast.5), calls=%async_computation.2 | async-start | bytes 786432 | tf_op jit(solution)/shard_map/all_to_all | solution.py:310
  42.0 8.6 %collective-permute-start = (f32[3,2048]{1,0:T(4,128)S(1)}, f32[3,2048]{1,0:T(4,128)S(1)}, u32[]{:S(2)}, u32[]{:S(2)}) collective-permute-start(f32[3,2048]{1,0:T(4,128)S(1)} %bitcast.25), channel_id=1, source_target_pairs={{3,4},{4,3},{7,8},{8,7},{11,12},{12,11},{15,16},{16,15},{19,20},{2... | collective-permute-start | bytes 73736 | tf_op jit(solution)/shard_map/ppermute | solution.py:308

commit v8 on v7

--- a/solution.py
+++ b/solution.py
@@ -96,7 +96,7 @@
     return jnp.concatenate([tile] * (wide // tile.shape[1]), 1)
 
 
-def project_kernel(mats, bins, slabs, tiles_ref, x_ref, near_ref, proj_ref, counts_ref, out_ref, resid_ref, rest_ref, block_ref, sems, out_sems):
+def project_kernel(mats, bins, slabs, tiles_ref, x_ref, near_ref, proj_ref, counts_ref, out_ref, resid_ref, rest_ref, sems):
     rows, pix = x_ref.shape
     cols, held = proj_ref.shape[0], near_ref.shape[0]
     wide = 256
@@ -133,22 +133,15 @@
                     parts[m] = term if parts[m] is None else parts[m] + term
             blocks += parts
         resid_ref[:, at : at + wide] = jnp.concatenate(blocks, 0).astype(BF16)
-    owners, sides, pairs, _, span = out_ref.shape
-    copies_out = []
+    owners, sides, _, _, span = out_ref.shape
     for owner in range(owners):
         own = slice(owner * span, (owner + 1) * span)
         back = jnp.dot(resid_ref[:, :held], near_ref[:, own], preferred_element_type=F32)
         back = back + jnp.dot(resid_ref[:, held:], rest_ref[:, own], preferred_element_type=F32)
         for slab in range(slabs):
-            block_ref[owner, slab % sides, slab // sides] = back[
+            out_ref[owner, slab % sides, slab // sides] = back[
                 slab * per_slab : (slab + 1) * per_slab
             ].astype(BF16)
-        copies_out.append(
-            pltpu.make_async_copy(block_ref.at[owner], out_ref.at[owner], out_sems.at[owner])
-        )
-        copies_out[-1].start()
-    for copy in copies_out:
-        copy.wait()
 
 
 def project(tiles, x_all, near, projector, counts, owners, sides, slabs, mats):
@@ -159,13 +152,11 @@
         functools.partial(project_kernel, mats, counts.shape[0], slabs),
         out_shape=jax.ShapeDtypeStruct(out, BF16),
         in_specs=[VMEM, VMEM, VMEM, HBM, VMEM],
-        out_specs=HBM,
+        out_specs=VMEM,
         scratch_shapes=[
             pltpu.VMEM((rows, cols), BF16),
             pltpu.VMEM((cols - near.shape[0], pix), BF16),
-            pltpu.VMEM(out, BF16),
             pltpu.SemaphoreType.DMA(((cols - near.shape[0]) // 256,)),
-            pltpu.SemaphoreType.DMA((owners,)),
         ],
         compiler_params=pltpu.CompilerParams(vmem_limit_bytes=MEDIUM),
         cost_estimate=pl.CostEstimate(
@@ -294,23 +285,26 @@
     vol = volume.transpose(1, 0, 2)
     x_all = lax.all_to_all(spread(vol, slabs), ("pair", "side"), 0, 0, tiled=True)
     x_all = x_all.reshape(slabs * rows, pix)
+    where = jnp.stack([slab, jnp.logical_and(slab == 0, group == 0)]).astype(jnp.int32)
+    x_all, where, slab = lax.optimization_barrier((x_all, where, slab))
     near, binned, tiles = stage(atten, projector[0], counts[0], projector.shape[1] // 2)
     parts = project(tiles, x_all, near, projector[0], binned, owners, sides, slabs, mats)
     parts = parts.reshape(owners * sides, pairs, rows, span)
+    parts = lax.all_to_all(parts, ("x", "side"), 0, 0, tiled=True)
+    sums = total_copies(parts, 1.0, halves).reshape(halves * pairs, rows, span)
+    sums, vol = lax.optimization_barrier((sums, vol))
     edge = jnp.where(slab == 0, vol[:, 0], vol[:, -1])
     ends = []
     for g in range(groups - 1):
         last, start = g * slabs + slabs - 1, (g + 1) * slabs
         ends += [(last, start), (start, last)]
-    parts = lax.all_to_all(parts, ("x", "side"), 0, 0, tiled=True)
-    mine = total_copies(parts, float(views_all) ** (-0.5), owners * halves)
-    mine, edge = lax.optimization_barrier((mine, edge))
     edge = lax.ppermute(edge, ("row", "pair", "side"), ends)
-    mine = mine.reshape(owners * halves * pairs, rows, span)
-    grad = lax.all_to_all(mine, ("x", "half", "pair"), 0, 0, tiled=True)
-    grad = grad.reshape(owners, halves * pairs, rows, span)
-    is_first = jnp.logical_and(slab == 0, group == 0).astype(jnp.int32)
-    smoothed = smooth(jnp.stack([slab, is_first]).astype(jnp.int32), vol, x_all, edge)
+    sums = lax.all_to_all(sums, ("half", "pair"), 0, 0, tiled=True)
+    sums, edge = lax.optimization_barrier((sums, edge))
+    mine = total_copies(sums, float(views_all) ** (-0.5), owners)
+    grad = lax.all_to_all(mine, "x", 0, 0, tiled=True)
+    grad = grad.reshape(owners, 1, rows, span)
+    smoothed = smooth(where, vol, x_all, edge)
     updated = newton_step(grad, smoothed, newton.transpose(1, 2, 0, 3), vol)
     return updated.transpose(1, 0, 2)
 

time: 58.3 us -> 61.9 us (1.062)
  the two profiles are of different devices: /device:TPU:448 before, /device:TPU:288 now
where the time goes in v8:
time: 61.9 us; the launch traced here: 61.3 us
  waiting for transfers between devices  27.5 us (44%)
  starting transfers between devices  20.2 us (33%)
  Pallas kernels  10.6 us (17%)
  local copies, waits for them, and re-layouts  2.24 us (4%)
    all_to_all x1, waiting for transfers between devices, body(): lax.all_to_all(spread(vol, slabs), ('pair', 'side'), 0, 0, tiled=True)  8.05 us
    all_to_all x1, waiting for transfers between devices, body(): parts = lax.all_to_all(parts, ('x', 'side'), 0, 0, tiled=True)  7.98 us
    ppermute x1, waiting for transfers between devices, body(): edge = lax.ppermute(edge, ('row', 'pair', 'side'), ends)  7.21 us
    all_to_all x1, starting transfers between devices, body(): sums = lax.all_to_all(sums, ('half', 'pair'), 0, 0, tiled=True)  7.2 us
    all_to_all x1, starting transfers between devices, body(): parts = lax.all_to_all(parts, ('x', 'side'), 0, 0, tiled=True)  4.32 us
    all_to_all x1, waiting for transfers between devices, body(): grad = lax.all_to_all(mine, 'x', 0, 0, tiled=True)  4.28 us
    pallas_call x1, Pallas kernels, project(): pl.pallas_call(functools.partial(project_kernel, mats, counts.shape[0], s...  4.23 us
    all_to_all x1, starting transfers between devices, body(): lax.all_to_all(spread(vol, slabs), ('pair', 'side'), 0, 0, tiled=True)  3.47 us
  transfers between devices with their start and end apart: 5, of which 4 were waited for; matrix products, arithmetic and copies ran while one was open for 1% of the time, Pallas kernels for 4%

profile of v8, /device:TPU:288, one launch (start us, length us, event | category | flops | bytes accessed | tf_op | source)
XLA Modules:
  0.0 61.3 jit_solution(16084358972028470031)
XLA Ops:
  0.0 1.7 %shard_map.56 = bf16[4,24,2048]{2,1,0:T(8,128)(2,1)} custom-call(f32[3,8,2048]{2,1,0:T(8,128)} %bitcast.16), custom_call_target="tpu_custom_call" | custom-call | tf_op jit(solution)/shard_map/pallas_call | solution.py:40
  1.7 3.5 %all-to-all-start = ((bf16[4,24,2048]{2,1,0:T(8,128)(2,1)}), bf16[4,24,2048]{2,1,0:T(8,128)(2,1)S(1)}, u32[]{:S(2)}, u32[]{:S(2)}) async-start(bf16[4,24,2048]{2,1,0:T(8,128)(2,1)} %shard_map.56), calls=%async_computation | async-start | bytes 786432 | tf_op jit(solution)/shard_map/all_to_all | solution.py:286
  5.2 0.0 copy-start.2
  5.2 0.9 %copy-done.2 = bf16[1,32,4,1024]{3,2,1,0:T(4,128)(2,1)S(1)} copy-done((bf16[1,32,4,1024]{3,2,1,0:T(4,128)(2,1)S(1)}, bf16[1,32,4,1024]{3,2,1,0:T(4,128)(2,1)}, u32[]{:S(2)}) %copy-start.2) | copy-done | bytes 262168
  6.2 0.0 copy-start.3
  6.2 0.7 %copy-done.3 = f32[4,3]{1,0:T(4,128)S(1)} copy-done((f32[4,3]{1,0:T(4,128)S(1)}, f32[4,3]{1,0:T(4,128)}, u32[]{:S(2)}) %copy-start.3) | copy-done | bytes 72
  6.9 1.6 %shard_map.55 = (bf16[512,2048]{1,0:T(8,128)(2,1)S(1)}, f32[4,32,1024]{2,1,0:T(8,128)S(1)}, f32[12,8,128]{2,1,0:T(8,128)S(1)}) custom-call(f32[4,3]{1,0:T(4,128)S(1)} %copy-done.3, bf16[1024,2048]{1,0:T(8,128)(2,1)} %bitcast.23, bf16[32,4,1024]{2,1,0:T(4,128)(2,1)S(1)} %bitcast.22), custom_call_target="tpu_custom_call" | custom-call | bytes 8388608 | tf_op jit(solution)/shard_map/pallas_call | solution.py:76
  8.5 0.6 pad_add_fusion.where_ref
  9.1 8.1 %all-to-all-done = bf16[4,24,2048]{2,1,0:T(8,128)(2,1)S(1)} async-done(((bf16[4,24,2048]{2,1,0:T(8,128)(2,1)}), bf16[4,24,2048]{2,1,0:T(8,128)(2,1)S(1)}, u32[]{:S(2)}, u32[]{:S(2)}) %all-to-all-start) | async-done | bytes 393248 | tf_op jit(solution)/shard_map/all_to_all | solution.py:286
  17.1 0.0 copy-start
  17.1 0.0 copy-start.1
  17.1 4.2 %shard_map.57 = bf16[4,2,2,24,512]{4,3,2,1,0:T(8,128)(2,1)} custom-call(f32[12,8,128]{2,1,0:T(8,128)S(1)} %get-tuple-element.15.tiles_ref, bf16[96,2048]{1,0:T(8,128)(2,1)S(1)} %bitcast.14, bf16[512,2048]{1,0:T(8,128)(2,1)S(1)} %get-tuple-element.17.near_ref, bf16[1024,2048]{1,0:T(8,128)(2,1)} %bitcast.24, f32[4,32,1024]{2,1,0:T(8,128)S(1)} %get-tuple-element.18.counts_ref), custom_call_target="tpu_custom_call" | custom-call | flops 805306368 | bytes 4194304 | tf_op jit(solution)/shard_map/pallas_call | solution.py:151
  21.4 4.3 %all-to-all-start.1 = ((bf16[8,2,24,512]{3,2,1,0:T(8,128)(2,1)}), bf16[8,2,24,512]{3,2,1,0:T(8,128)(2,1)S(1)}, u32[]{:S(2)}, u32[]{:S(2)}) async-start(bf16[8,2,24,512]{3,2,1,0:T(8,128)(2,1)} %bitcast.6), calls=%async_computation.1 | async-start | bytes 786432 | tf_op jit(solution)/shard_map/all_to_all | solution.py:293
  25.7 8.0 %all-to-all-done.1.part_ref = bf16[8,2,24,512]{3,2,1,0:T(8,128)(2,1)S(1)} async-done(((bf16[8,2,24,512]{3,2,1,0:T(8,128)(2,1)}), bf16[8,2,24,512]{3,2,1,0:T(8,128)(2,1)S(1)}, u32[]{:S(2)}, u32[]{:S(2)}) %all-to-all-start.1) | async-done | bytes 393248 | tf_op jit(solution)/shard_map/all_to_all | solution.py:293
  33.7 0.7 %shard_map.58 = bf16[2,2,24,512]{3,2,1,0:T(8,128)(2,1)} custom-call(bf16[8,2,24,512]{3,2,1,0:T(8,128)(2,1)S(1)} %all-to-all-done.1.part_ref), custom_call_target="tpu_custom_call" | custom-call | tf_op jit(solution)/shard_map/pallas_call | solution.py:241
  34.4 7.2 %all-to-all-start.2 = ((bf16[4,24,512]{2,1,0:T(8,128)(2,1)}), bf16[4,24,512]{2,1,0:T(8,128)(2,1)S(1)}, u32[]{:S(2)}, u32[]{:S(2)}) async-start(bf16[4,24,512]{2,1,0:T(8,128)(2,1)} %bitcast.7), calls=%async_computation.2 | async-start | bytes 196608 | tf_op jit(solution)/shard_map/all_to_all | solution.py:302
  41.6 0.0 copy-done
  41.6 1.9 %collective-permute-start = (f32[3,2048]{1,0:T(4,128)S(1)}, f32[3,2048]{1,0:T(4,128)S(1)}, u32[]{:S(2)}, u32[]{:S(2)}) collective-permute-start(f32[3,2048]{1,0:T(4,128)S(1)} %bitcast.25), channel_id=1, source_target_pairs={{3,4},{4,3},{7,8},{8,7},{11,12},{12,11},{15,16},{16,15},{19,20},{2... | collective-permute-start | bytes 73736 | tf_op jit(solution)/shard_map/ppermute | solution.py:301
  43.6 7.2 %collective-permute-done.edge_ref = f32[3,2048]{1,0:T(4,128)S(1)} collective-permute-done((f32[3,2048]{1,0:T(4,128)S(1)}, f32[3,2048]{1,0:T(4,128)S(1)}, u32[]{:S(2)}, u32[]{:S(2)}) %collective-permute-start) | collective-permute-done | bytes 24608 | tf_op jit(solution)/shard_map/ppermute | solution.py:301
  50.8 0.0 all-to-all-done.2.part_ref
  50.8 0.7 %shard_map.59 = bf16[4,24,512]{2,1,0:T(8,128)(2,1)} custom-call(bf16[4,24,512]{2,1,0:T(8,128)(2,1)S(1)} %all-to-all-done.2.part_ref), custom_call_target="tpu_custom_call" | custom-call | tf_op jit(solution)/shard_map/pallas_call | solution.py:241
  51.4 3.3 %all-to-all-start.3 = ((bf16[4,24,512]{2,1,0:T(8,128)(2,1)}), bf16[4,24,512]{2,1,0:T(8,128)(2,1)S(1)}, u32[]{:S(2)}, u32[]{:S(2)}) async-start(bf16[4,24,512]{2,1,0:T(8,128)(2,1)} %shard_map.59), calls=%async_computation.3 | async-start | bytes 196608 | tf_op jit(solution)/shard_map/all_to_all | solution.py:305
  54.7 0.0 copy-start.4
  54.8 0.6 copy-done.4
  55.3 0.9 %shard_map.60.smooth_ref = f32[3,8,2048]{2,1,0:T(8,128)S(1)} custom-call(s32[2]{0:T(128)S(1)} %copy-done.4, f32[3,8,2048]{2,1,0:T(8,128)S(1)} %bitcast.18, bf16[96,2048]{1,0:T(8,128)(2,1)S(1)} %bitcast.15, f32[3,2048]{1,0:T(4,128)S(1)} %collective-permute-done.edge_ref), custom_call_target="tpu_custom_call" | custom-call | flops 1966080 | bytes 589824 | tf_op jit(solution)/shard_map/pallas_call | solution.py:221
  56.2 4.3 %all-to-all-done.3 = bf16[4,24,512]{2,1,0:T(8,128)(2,1)S(1)} async-done(((bf16[4,24,512]{2,1,0:T(8,128)(2,1)}), bf16[4,24,512]{2,1,0:T(8,128)(2,1)S(1)}, u32[]{:S(2)}, u32[]{:S(2)}) %all-to-all-start.3) | async-done | bytes 98336 | tf_op jit(solution)/shard_map/all_to_all | solution.py:305
  60.5 0.0 copy-done.1
  60.5 0.8 %shard_map.61 = f32[3,8,2048]{2,1,0:T(8,128)} custom-call(bf16[4,1,24,512]{3,2,1,0:T(8,128)(2,1)S(1)} %bitcast.20, f32[3,8,2048]{2,1,0:T(8,128)S(1)} %shard_map.60.smooth_ref, bf16[3,3,8,2048]{3,2,1,0:T(8,128)(2,1)S(1)} %bitcast.21, f32[3,8,2048]{2,1,0:T(8,128)S(1)} %bitcast.19), custom_call_target="tpu_custom_call" | custom-call | tf_op jit(solution)/shard_map/pallas_call | solution.py:267
  (2 shorter events, 0.0 us)
Async XLA Ops:
  1.7 15.4 %all-to-all-start = ((bf16[4,24,2048]{2,1,0:T(8,128)(2,1)}), bf16[4,24,2048]{2,1,0:T(8,128)(2,1)S(1)}, u32[]{:S(2)}, u32[]{:S(2)}) async-start(bf16[4,24,2048]{2,1,0:T(8,128)(2,1)} %shard_map.56), calls=%async_computation | async-start | bytes 786432 | tf_op jit(solution)/shard_map/all_to_all | solution.py:286
  5.2 1.0 %copy-start.2 = (bf16[1,32,4,1024]{3,2,1,0:T(4,128)(2,1)S(1)}, bf16[1,32,4,1024]{3,2,1,0:T(4,128)(2,1)}, u32[]{:S(2)}) copy-start(bf16[1,32,4,1024]{3,2,1,0:T(4,128)(2,1)} %param.7) | copy-start | bytes 786436
  6.2 0.7 %copy-start.3 = (f32[4,3]{1,0:T(4,128)S(1)}, f32[4,3]{1,0:T(4,128)}, u32[]{:S(2)}) copy-start(f32[4,3]{1,0:T(4,128)} %atten_ref.1) | copy-start | bytes 148
  17.1 24.4 %copy-start = (f32[8,3,2048]{2,0,1:T(8,128)S(1)}, f32[8,3,2048]{2,0,1:T(8,128)}, u32[]{:S(2)}) copy-start(f32[8,3,2048]{2,0,1:T(8,128)} %param.5) | copy-start | bytes 589828
  17.1 43.4 %copy-start.1 = (bf16[8,3,3,2048]{3,0,2,1:T(8,128)(2,1)S(1)}, bf16[8,3,3,2048]{3,0,2,1:T(8,128)(2,1)}, u32[]{:S(2)}) copy-start(bf16[8,3,3,2048]{3,0,2,1:T(8,128)(2,1)} %param.9) | copy-start | bytes 884740
  21.4 12.3 %all-to-all-start.1 = ((bf16[8,2,24,512]{3,2,1,0:T(8,128)(2,1)}), bf16[8,2,24,512]{3,2,1,0:T(8,128)(2,1)S(1)}, u32[]{:S(2)}, u32[]{:S(2)}) async-start(bf16[8,2,24,512]{3,2,1,0:T(8,128)(2,1)} %bitcast.6), calls=%async_computation.1 | async-start | bytes 786432 | tf_op jit(solution)/shard_map/all_to_all | solution.py:293
  34.4 16.4 %all-to-all-start.2 = ((bf16[4,24,512]{2,1,0:T(8,128)(2,1)}), bf16[4,24,512]{2,1,0:T(8,128)(2,1)S(1)}, u32[]{:S(2)}, u32[]{:S(2)}) async-start(bf16[4,24,512]{2,1,0:T(8,128)(2,1)} %bitcast.7), calls=%async_computation.2 | async-start | bytes 196608 | tf_op jit(solution)/shard_map/all_to_all | solution.py:302
  41.6 9.1 %collective-permute-start = (f32[3,2048]{1,0:T(4,128)S(1)}, f32[3,2048]{1,0:T(4,128)S(1)}, u32[]{:S(2)}, u32[]{:S(2)}) collective-permute-start(f32[3,2048]{1,0:T(4,128)S(1)} %bitcast.25), channel_id=1, source_target_pairs={{3,4},{4,3},{7,8},{8,7},{11,12},{12,11},{15,16},{16,15},{19,20},{2... | collective-permute-start | bytes 73736 | tf_op jit(solution)/shard_map/ppermute | solution.py:301
  51.4 9.1 %all-to-all-start.3 = ((bf16[4,24,512]{2,1,0:T(8,128)(2,1)}), bf16[4,24,512]{2,1,0:T(8,128)(2,1)S(1)}, u32[]{:S(2)}, u32[]{:S(2)}) async-start(bf16[4,24,512]{2,1,0:T(8,128)(2,1)} %shard_map.59), calls=%async_computation.3 | async-start | bytes 196608 | tf_op jit(solution)/shard_map/all_to_all | solution.py:305
  54.7 0.6 copy-start.4

commit v9 on v8

--- a/solution.py
+++ b/solution.py
@@ -183,10 +183,15 @@
     return jnp.concatenate([jnp.zeros((flux.shape[0], PX), F32), flux[:, :-PX]], 1)
 
 
-def smooth_kernel(where_ref, vol_ref, x_ref, edge_ref, out_ref):
+def slab_index():
+    return lax.axis_index("pair") * lax.axis_size("side") + lax.axis_index("side")
+
+
+def smooth_kernel(vol_ref, x_ref, edge_ref, out_ref):
     mats, depth, pix = vol_ref.shape
     slabs = x_ref.shape[0] // (mats * depth)
-    slab, first = where_ref[0], where_ref[1]
+    slab = slab_index()
+    first = jnp.logical_and(slab == 0, lax.axis_index("row") == 0)
     row = lax.broadcasted_iota(jnp.int32, (depth, pix), 0)
     vol, above, below = [], [], []
     for m in range(mats):
@@ -210,41 +215,49 @@
         square_below = square_below + (dz * dz + dy * dy + dx * dx)
         steps.append(dz)
     scale = lax.rsqrt(square)
-    scale_below = jnp.where(first == 1, 0.0, lax.rsqrt(square_below))
+    scale_below = jnp.where(first, 0.0, lax.rsqrt(square_below))
     for m in range(mats):
         qz, qy, qx = (d * scale for d in diffs[m])
         prev_z = jnp.where(row == 0, steps[m] * scale_below, pltpu.roll(qz, 1, 0))
         out_ref[m] = prev_z - qz + (prev_row(qy) - qy) + (prev_pixel(qx) - qx)
 
 
-def smooth(where, volume, x_all, edge):
+def smooth(volume, x_all, edge):
     return pl.pallas_call(
         smooth_kernel,
         out_shape=jax.ShapeDtypeStruct(volume.shape, F32),
-        in_specs=[SMEM, VMEM, VMEM, VMEM],
+        in_specs=[VMEM, VMEM, VMEM],
         out_specs=VMEM,
         compiler_params=pltpu.CompilerParams(vmem_limit_bytes=SMALL),
         cost_estimate=pl.CostEstimate(
             flops=40 * volume.size, bytes_accessed=12 * volume.size, transcendentals=volume.size
         ),
-    )(where, volume, x_all, edge)
-
-
-def total_kernel(factor, part_ref, out_ref):
+    )(volume, x_all, edge)
+
+
+def total_kernel(factor, part_ref, vol_ref, out_ref, edge_ref):
     total = jnp.sum(part_ref[...].astype(F32), axis=0) * factor
     total = total.astype(BF16)
     for copy in range(out_ref.shape[0]):
         out_ref[copy] = total
-
-
-def total_copies(parts, factor, copies):
+    slab = slab_index()
+    for m in range(vol_ref.shape[0]):
+        slab_m = vol_ref[m]
+        edge_ref[m : m + 1] = jnp.where(slab == 0, slab_m[:1], slab_m[-1:])
+
+
+def total_copies(parts, volume, factor, copies):
+    mats, _, pix = volume.shape
     return pl.pallas_call(
         functools.partial(total_kernel, factor),
-        out_shape=jax.ShapeDtypeStruct((copies,) + parts.shape[1:], BF16),
-        in_specs=[VMEM],
-        out_specs=VMEM,
+        out_shape=[
+            jax.ShapeDtypeStruct((copies,) + parts.shape[1:], BF16),
+            jax.ShapeDtypeStruct((mats, pix), F32),
+        ],
+        in_specs=[VMEM, VMEM],
+        out_specs=[VMEM, VMEM],
         compiler_params=pltpu.CompilerParams(vmem_limit_bytes=SMALL),
-    )(parts)
+    )(parts, volume)
 
 
 def step_kernel(grad_ref, smooth_ref, newton_ref, vol_ref, out_ref):
@@ -280,31 +293,24 @@
     )
     slabs = pairs * sides
     views_all = projector.shape[0] * owners * halves * slabs
-    slab, group = lax.axis_index(("pair", "side")), lax.axis_index("row")
     rows, span = mats * depth, pix // owners
     vol = volume.transpose(1, 0, 2)
     x_all = lax.all_to_all(spread(vol, slabs), ("pair", "side"), 0, 0, tiled=True)
     x_all = x_all.reshape(slabs * rows, pix)
-    where = jnp.stack([slab, jnp.logical_and(slab == 0, group == 0)]).astype(jnp.int32)
-    x_all, where, slab = lax.optimization_barrier((x_all, where, slab))
     near, binned, tiles = stage(atten, projector[0], counts[0], projector.shape[1] // 2)
     parts = project(tiles, x_all, near, projector[0], binned, owners, sides, slabs, mats)
     parts = parts.reshape(owners * sides, pairs, rows, span)
     parts = lax.all_to_all(parts, ("x", "side"), 0, 0, tiled=True)
-    sums = total_copies(parts, 1.0, halves).reshape(halves * pairs, rows, span)
-    sums, vol = lax.optimization_barrier((sums, vol))
-    edge = jnp.where(slab == 0, vol[:, 0], vol[:, -1])
+    mine, edge = total_copies(parts, vol, float(views_all) ** (-0.5), owners * halves)
     ends = []
     for g in range(groups - 1):
         last, start = g * slabs + slabs - 1, (g + 1) * slabs
         ends += [(last, start), (start, last)]
     edge = lax.ppermute(edge, ("row", "pair", "side"), ends)
-    sums = lax.all_to_all(sums, ("half", "pair"), 0, 0, tiled=True)
-    sums, edge = lax.optimization_barrier((sums, edge))
-    mine = total_copies(sums, float(views_all) ** (-0.5), owners)
-    grad = lax.all_to_all(mine, "x", 0, 0, tiled=True)
-    grad = grad.reshape(owners, 1, rows, span)
-    smoothed = smooth(where, vol, x_all, edge)
+    mine = mine.reshape(owners * halves * pairs, rows, span)
+    grad = lax.all_to_all(mine, ("x", "half", "pair"), 0, 0, tiled=True)
+    grad = grad.reshape(owners, halves * pairs, rows, span)
+    smoothed = smooth(vol, x_all, edge)
     updated = newton_step(grad, smoothed, newton.transpose(1, 2, 0, 3), vol)
     return updated.transpose(1, 0, 2)
 

time: 61.9 us -> 56.6 us (0.914)
  the two profiles are of different devices: /device:TPU:288 before, /device:TPU:448 now
where the time goes in v9:
time: 56.6 us; the launch traced here: 56.2 us
  waiting for transfers between devices  20.1 us (36%)
  starting transfers between devices  13.5 us (24%)
  blocking collectives  12.2 us (22%)
  Pallas kernels  8.8 us (16%)
  local copies, waits for them, and re-layouts  1.64 us (3%)
    all_to_all x1, blocking collectives, body(): parts = lax.all_to_all(parts, ('x', 'side'), 0, 0, tiled=True)  12.2 us
    all_to_all x1, waiting for transfers between devices, body(): lax.all_to_all(spread(vol, slabs), ('pair', 'side'), 0, 0, tiled=True)  8.41 us
    ppermute x1, waiting for transfers between devices, body(): edge = lax.ppermute(edge, ('row', 'pair', 'side'), ends)  7.93 us
    all_to_all x1, starting transfers between devices, body(): grad = lax.all_to_all(mine, ('x', 'half', 'pair'), 0, 0, tiled=True)  6.65 us
    all_to_all x1, starting transfers between devices, body(): lax.all_to_all(spread(vol, slabs), ('pair', 'side'), 0, 0, tiled=True)  4.88 us
    all_to_all x1, waiting for transfers between devices, body(): grad = lax.all_to_all(mine, ('x', 'half', 'pair'), 0, 0, tiled=True)  3.73 us
    pallas_call x1, Pallas kernels, project(): pl.pallas_call(functools.partial(project_kernel, mats, counts.shape[0], s...  3.48 us
    ppermute x1, starting transfers between devices, body(): edge = lax.ppermute(edge, ('row', 'pair', 'side'), ends)  1.92 us
  transfers between devices with their start and end apart: 3, of which 3 were waited for; matrix products, arithmetic and copies ran while one was open for 0% of the time, Pallas kernels for 4%

profile of v9, /device:TPU:448, one launch (start us, length us, event | category | flops | bytes accessed | tf_op | source)
XLA Modules:
  0.0 56.2 jit_solution(8223391527584627643)
XLA Ops:
  0.0 1.7 %shard_map.56 = bf16[4,24,2048]{2,1,0:T(8,128)(2,1)} custom-call(f32[3,8,2048]{2,1,0:T(8,128)} %bitcast.11), custom_call_target="tpu_custom_call" | custom-call | tf_op jit(solution)/shard_map/pallas_call | solution.py:40
  1.7 4.9 %all-to-all-start = ((bf16[4,24,2048]{2,1,0:T(8,128)(2,1)}), bf16[4,24,2048]{2,1,0:T(8,128)(2,1)S(1)}, u32[]{:S(2)}, u32[]{:S(2)}) async-start(bf16[4,24,2048]{2,1,0:T(8,128)(2,1)} %shard_map.56), calls=%async_computation | async-start | bytes 786432 | tf_op jit(solution)/shard_map/all_to_all | solution.py:298
  6.6 0.0 copy-start.2
  6.6 0.9 %copy-done.2 = bf16[1,32,4,1024]{3,2,1,0:T(4,128)(2,1)S(1)} copy-done((bf16[1,32,4,1024]{3,2,1,0:T(4,128)(2,1)S(1)}, bf16[1,32,4,1024]{3,2,1,0:T(4,128)(2,1)}, u32[]{:S(2)}) %copy-start.2) | copy-done | bytes 262168
  7.6 0.0 copy-start.3
  7.6 0.7 %copy-done.3 = f32[4,3]{1,0:T(4,128)S(1)} copy-done((f32[4,3]{1,0:T(4,128)S(1)}, f32[4,3]{1,0:T(4,128)}, u32[]{:S(2)}) %copy-start.3) | copy-done | bytes 72
  8.3 1.6 %shard_map.55 = (bf16[512,2048]{1,0:T(8,128)(2,1)S(1)}, f32[4,32,1024]{2,1,0:T(8,128)S(1)}, f32[12,8,128]{2,1,0:T(8,128)S(1)}) custom-call(f32[4,3]{1,0:T(4,128)S(1)} %copy-done.3, bf16[1024,2048]{1,0:T(8,128)(2,1)} %bitcast.19, bf16[32,4,1024]{2,1,0:T(4,128)(2,1)S(1)} %bitcast.18), custom_call_target="tpu_custom_call" | custom-call | bytes 8388608 | tf_op jit(solution)/shard_map/pallas_call | solution.py:76
  9.9 8.4 %all-to-all-done = bf16[4,24,2048]{2,1,0:T(8,128)(2,1)S(1)} async-done(((bf16[4,24,2048]{2,1,0:T(8,128)(2,1)}), bf16[4,24,2048]{2,1,0:T(8,128)(2,1)S(1)}, u32[]{:S(2)}, u32[]{:S(2)}) %all-to-all-start) | async-done | bytes 393248 | tf_op jit(solution)/shard_map/all_to_all | solution.py:298
  18.3 0.0 copy-start
  18.3 0.0 copy-start.1
  18.3 3.5 %shard_map.57 = bf16[4,2,2,24,512]{4,3,2,1,0:T(8,128)(2,1)S(1)} custom-call(f32[12,8,128]{2,1,0:T(8,128)S(1)} %get-tuple-element.10.tiles_ref, bf16[96,2048]{1,0:T(8,128)(2,1)S(1)} %bitcast.9, bf16[512,2048]{1,0:T(8,128)(2,1)S(1)} %get-tuple-element.11.near_ref, bf16[1024,2048]{1,0:T(8,128)(2,1)} %bitcast.20, f32[4,32,1024]{2,1,0:T(8,128)S(1)} %get-tuple-element.12.counts_ref), custom_call_target="tpu_custom_call" | custom-call | flops 805306368 | bytes 4194304 | tf_op jit(solution)/shard_map/pallas_call | solution.py:151
  21.8 12.2 %all_to_all.15.part_ref = bf16[8,2,24,512]{3,2,1,0:T(8,128)(2,1)S(1)} all-to-all(bf16[8,2,24,512]{3,2,1,0:T(8,128)(2,1)S(1)} %bitcast.16), channel_id=1, replica_groups=mesh['x'=4,'half'=2,'row'=16,'pair'=2,'side'=2] {'x','side'}, dimensions={0} | all-to-all | bytes 786432 | tf_op jit(solution)/shard_map/all_to_all | solution.py:303
  34.0 0.0 copy-done
  34.0 0.8 %shard_map.58 = (bf16[8,2,24,512]{3,2,1,0:T(8,128)(2,1)}, f32[3,2048]{1,0:T(4,128)S(1)}) custom-call(bf16[8,2,24,512]{3,2,1,0:T(8,128)(2,1)S(1)} %all_to_all.15.part_ref, f32[3,8,2048]{2,1,0:T(8,128)S(1)} %bitcast.12), custom_call_target="tpu_custom_call" | custom-call | tf_op jit(solution)/shard_map/pallas_call | solution.py:251
  34.8 6.7 %all-to-all-start.2 = ((bf16[16,24,512]{2,1,0:T(8,128)(2,1)}), bf16[16,24,512]{2,1,0:T(8,128)(2,1)S(1)}, u32[]{:S(2)}, u32[]{:S(2)}) async-start(bf16[16,24,512]{2,1,0:T(8,128)(2,1)} %bitcast.5), calls=%async_computation.2 | async-start | bytes 786432 | tf_op jit(solution)/shard_map/all_to_all | solution.py:311
  41.5 1.9 %collective-permute-start = (f32[3,2048]{1,0:T(4,128)S(1)}, f32[3,2048]{1,0:T(4,128)S(1)}, u32[]{:S(2)}, u32[]{:S(2)}) collective-permute-start(f32[3,2048]{1,0:T(4,128)S(1)} %get-tuple-element.14), channel_id=1, source_target_pairs={{3,4},{4,3},{7,8},{8,7},{11,12},{12,11},{15,16},{16,15},{19,20},{2... | collective-permute-start | bytes 73736 | tf_op jit(solution)/shard_map/ppermute | solution.py:309
  43.4 7.9 %collective-permute-done.edge_ref = f32[3,2048]{1,0:T(4,128)S(1)} collective-permute-done((f32[3,2048]{1,0:T(4,128)S(1)}, f32[3,2048]{1,0:T(4,128)S(1)}, u32[]{:S(2)}, u32[]{:S(2)}) %collective-permute-start) | collective-permute-done | bytes 24608 | tf_op jit(solution)/shard_map/ppermute | solution.py:309
  51.3 0.4 shard_map.59.smooth_ref
  51.7 3.7 %all-to-all-done.2 = bf16[16,24,512]{2,1,0:T(8,128)(2,1)S(1)} async-done(((bf16[16,24,512]{2,1,0:T(8,128)(2,1)}), bf16[16,24,512]{2,1,0:T(8,128)(2,1)S(1)}, u32[]{:S(2)}, u32[]{:S(2)}) %all-to-all-start.2) | async-done | bytes 393248 | tf_op jit(solution)/shard_map/all_to_all | solution.py:311
  55.4 0.0 copy-done.1
  55.4 0.8 %shard_map.60 = f32[3,8,2048]{2,1,0:T(8,128)} custom-call(bf16[4,4,24,512]{3,2,1,0:T(8,128)(2,1)S(1)} %bitcast.15, f32[3,8,2048]{2,1,0:T(8,128)S(1)} %shard_map.59.smooth_ref, bf16[3,3,8,2048]{3,2,1,0:T(8,128)(2,1)S(1)} %bitcast.17, f32[3,8,2048]{2,1,0:T(8,128)S(1)} %bitcast.14), custom_call_target="tpu_custom_call" | custom-call | tf_op jit(solution)/shard_map/pallas_call | solution.py:280
Async XLA Ops:
  1.7 16.6 %all-to-all-start = ((bf16[4,24,2048]{2,1,0:T(8,128)(2,1)}), bf16[4,24,2048]{2,1,0:T(8,128)(2,1)S(1)}, u32[]{:S(2)}, u32[]{:S(2)}) async-start(bf16[4,24,2048]{2,1,0:T(8,128)(2,1)} %shard_map.56), calls=%async_computation | async-start | bytes 786432 | tf_op jit(solution)/shard_map/all_to_all | solution.py:298
  6.6 0.9 %copy-start.2 = (bf16[1,32,4,1024]{3,2,1,0:T(4,128)(2,1)S(1)}, bf16[1,32,4,1024]{3,2,1,0:T(4,128)(2,1)}, u32[]{:S(2)}) copy-start(bf16[1,32,4,1024]{3,2,1,0:T(4,128)(2,1)} %param.7) | copy-start | bytes 786436
  7.6 0.7 %copy-start.3 = (f32[4,3]{1,0:T(4,128)S(1)}, f32[4,3]{1,0:T(4,128)}, u32[]{:S(2)}) copy-start(f32[4,3]{1,0:T(4,128)} %atten_ref.1) | copy-start | bytes 148
  18.3 15.7 %copy-start = (f32[8,3,2048]{2,0,1:T(8,128)S(1)}, f32[8,3,2048]{2,0,1:T(8,128)}, u32[]{:S(2)}) copy-start(f32[8,3,2048]{2,0,1:T(8,128)} %param.5) | copy-start | bytes 589828
  18.3 37.1 %copy-start.1 = (bf16[8,3,3,2048]{3,0,2,1:T(8,128)(2,1)S(1)}, bf16[8,3,3,2048]{3,0,2,1:T(8,128)(2,1)}, u32[]{:S(2)}) copy-start(bf16[8,3,3,2048]{3,0,2,1:T(8,128)(2,1)} %param.9) | copy-start | bytes 884740
  34.8 20.6 %all-to-all-start.2 = ((bf16[16,24,512]{2,1,0:T(8,128)(2,1)}), bf16[16,24,512]{2,1,0:T(8,128)(2,1)S(1)}, u32[]{:S(2)}, u32[]{:S(2)}) async-start(bf16[16,24,512]{2,1,0:T(8,128)(2,1)} %bitcast.5), calls=%async_computation.2 | async-start | bytes 786432 | tf_op jit(solution)/shard_map/all_to_all | solution.py:311
  41.5 9.9 %collective-permute-start = (f32[3,2048]{1,0:T(4,128)S(1)}, f32[3,2048]{1,0:T(4,128)S(1)}, u32[]{:S(2)}, u32[]{:S(2)}) collective-permute-start(f32[3,2048]{1,0:T(4,128)S(1)} %get-tuple-element.14), channel_id=1, source_target_pairs={{3,4},{4,3},{7,8},{8,7},{11,12},{12,11},{15,16},{16,15},{19,20},{2... | collective-permute-start | bytes 73736 | tf_op jit(solution)/shard_map/ppermute | solution.py:309

commit v10 on v9

--- a/solution.py
+++ b/solution.py
@@ -15,81 +15,40 @@
 HBM = pl.BlockSpec(memory_space=pltpu.HBM)
 SMALL = 8 * 1024 * 1024
 MEDIUM = 49 * 1024 * 1024
-LARGE = 50 * 1024 * 1024
-HUGE = 58 * 1024 * 1024
-
-
-def spread_kernel(vol_ref, out_ref, near_ref, rounded_ref, sems):
-    copy_in = pltpu.make_async_copy(vol_ref, near_ref, sems.at[0])
-    copy_in.start()
-    copy_in.wait()
-    mats = near_ref.shape[0]
-    rounded_ref[...] = jnp.concatenate([near_ref[m] for m in range(mats)], 0).astype(BF16)
-    copies = [
-        pltpu.make_async_copy(rounded_ref, out_ref.at[copy], sems.at[copy + 1])
-        for copy in range(out_ref.shape[0])
-    ]
-    for copy in copies:
-        copy.start()
-    for copy in copies:
-        copy.wait()
-
-
-def spread(volume, copies):
-    mats, depth, pix = volume.shape
-    return pl.pallas_call(
-        spread_kernel,
-        out_shape=jax.ShapeDtypeStruct((copies, mats * depth, pix), BF16),
-        in_specs=[HBM],
-        out_specs=HBM,
-        scratch_shapes=[
-            pltpu.VMEM(volume.shape, F32),
-            pltpu.VMEM((mats * depth, pix), BF16),
-            pltpu.SemaphoreType.DMA((copies + 1,)),
-        ],
-        compiler_params=pltpu.CompilerParams(vmem_limit_bytes=HUGE),
-    )(volume)
+LARGE = 49 * 1024 * 1024
 
 
 def stage_kernel(
-    atten_ref, proj_ref, counts_ref, near_ref, binned_ref, tiles_ref, atten_near, counts_near, sems
+    vol_ref, atten_ref, counts_ref, proj_ref, own_ref, tiles_ref, binned_ref, near_ref, sem
 ):
-    copy_atten = pltpu.make_async_copy(atten_ref, atten_near, sems.at[0])
-    copy_counts = pltpu.make_async_copy(counts_ref, counts_near, sems.at[1])
-    copy_proj = pltpu.make_async_copy(proj_ref.at[: near_ref.shape[0]], near_ref, sems.at[2])
-    copy_atten.start()
-    copy_counts.start()
-    copy_proj.start()
+    copy = pltpu.make_async_copy(proj_ref.at[: near_ref.shape[0]], near_ref, sem)
+    copy.start()
     bins, mats = atten_ref.shape
-    copy_atten.wait()
+    own_ref[...] = jnp.concatenate([vol_ref[m] for m in range(mats)], 0).astype(BF16)
     for b in range(bins):
         for m in range(mats):
-            tiles_ref[b * mats + m] = jnp.full(tiles_ref.shape[1:], atten_near[b, m], F32)
-    copy_counts.wait()
+            tiles_ref[b * mats + m] = jnp.full(tiles_ref.shape[1:], atten_ref[b, m], F32)
     for b in range(bins):
-        binned_ref[b] = counts_near[:, b, :].astype(F32)
-    copy_proj.wait()
-
-
-def stage(atten, projector, counts, held):
+        binned_ref[b] = counts_ref[:, b, :].astype(F32)
+    copy.wait()
+
+
+def stage(volume, atten, counts, projector, held):
     slices, bins, cols = counts.shape
+    mats, depth, pix = volume.shape
     return pl.pallas_call(
         stage_kernel,
         out_shape=[
-            jax.ShapeDtypeStruct((held, projector.shape[1]), BF16),
+            jax.ShapeDtypeStruct((mats * depth, pix), BF16),
+            jax.ShapeDtypeStruct((atten.size, 8, 128), F32),
             jax.ShapeDtypeStruct((bins, slices, cols), F32),
-            jax.ShapeDtypeStruct((atten.size, 8, 128), F32),
+            jax.ShapeDtypeStruct((held, pix), BF16),
         ],
-        in_specs=[HBM, HBM, HBM],
-        out_specs=[VMEM] * 3,
-        scratch_shapes=[
-            pltpu.SMEM(atten.shape, F32),
-            pltpu.VMEM(counts.shape, BF16),
-            pltpu.SemaphoreType.DMA((3,)),
-        ],
+        in_specs=[VMEM, SMEM, VMEM, HBM],
+        out_specs=[VMEM] * 4,
+        scratch_shapes=[pltpu.SemaphoreType.DMA(())],
         compiler_params=pltpu.CompilerParams(vmem_limit_bytes=LARGE),
-        cost_estimate=pl.CostEstimate(flops=0, bytes_accessed=4 * projector.size, transcendentals=0),
-    )(atten, projector, counts)
+    )(volume, atten, counts, projector)
 
 
 def wide_tile(tile, wide):
@@ -295,9 +254,9 @@
     views_all = projector.shape[0] * owners * halves * slabs
     rows, span = mats * depth, pix // owners
     vol = volume.transpose(1, 0, 2)
-    x_all = lax.all_to_all(spread(vol, slabs), ("pair", "side"), 0, 0, tiled=True)
-    x_all = x_all.reshape(slabs * rows, pix)
-    near, binned, tiles = stage(atten, projector[0], counts[0], projector.shape[1] // 2)
+    held = projector.shape[1] * 2 // 4
+    own, tiles, binned, near = stage(vol, atten, counts[0], projector[0], held)
+    x_all = lax.all_gather(own, ("pair", "side"), axis=0, tiled=True)
     parts = project(tiles, x_all, near, projector[0], binned, owners, sides, slabs, mats)
     parts = parts.reshape(owners * sides, pairs, rows, span)
     parts = lax.all_to_all(parts, ("x", "side"), 0, 0, tiled=True)

time: 56.6 us -> 58.7 us (1.037)
  blocking collectives: 12.2 us -> 28.6 us
  waiting for transfers between devices: 20.1 us -> 11.2 us
  starting transfers between devices: 13.5 us -> 8.28 us
  Pallas kernels: 8.8 us -> 7.59 us
  local copies, waits for them, and re-layouts: 1.64 us -> 2.56 us
    all_gather x0 -> x1, blocking collectives: none -> 14.8 us  [body(): x_all = lax.all_gather(own, ('pair', 'side'), axis=0, tiled=True)]
    all_to_all x1 -> x0, waiting for transfers between devices: 8.41 us -> none  [body(): lax.all_to_all(spread(vol, slabs), ('pair', 'side'), 0, 0, tiled=True)]
    all_to_all x1 -> x0, starting transfers between devices: 4.88 us -> none  [body(): lax.all_to_all(spread(vol, slabs), ('pair', 'side'), 0, 0, tiled=True)]
    all_to_all x1, blocking collectives: 12.2 us -> 13.8 us  [body(): parts = lax.all_to_all(parts, ('x', 'side'), 0, 0, tiled=True)]
    pallas_call x2 -> x1, Pallas kernels: 3.36 us -> 2.16 us  [stage(): pl.pallas_call(stage_kernel, out_shape=[jax.ShapeDtypeStruct((mats * dept...]
    ppermute x1, waiting for transfers between devices: 7.93 us -> 6.86 us  [body(): edge = lax.ppermute(edge, ('row', 'pair', 'side'), ends)]
    unnamed x8 -> x10, local copies, waits for them, and re-layouts: 1.64 us -> 2.56 us
    all_to_all x1, waiting for transfers between devices: 3.73 us -> 4.38 us  [body(): grad = lax.all_to_all(mine, ('x', 'half', 'pair'), 0, 0, tiled=True)]
  transfers between devices with their start and end apart: 3 -> 2, of which waited for: 3 -> 2; matrix products, arithmetic and copies ran while one was open for 0% -> 0% of each run, Pallas kernels for 4% -> 1%
where the time goes in v10:
time: 58.7 us; the launch traced here: 58.3 us
  blocking collectives  28.6 us (49%)
  waiting for transfers between devices  11.2 us (19%)
  starting transfers between devices  8.28 us (14%)
  Pallas kernels  7.59 us (13%)
  local copies, waits for them, and re-layouts  2.56 us (4%)
    all_gather x1, blocking collectives, body(): x_all = lax.all_gather(own, ('pair', 'side'), axis=0, tiled=True)  14.8 us
    all_to_all x1, blocking collectives, body(): parts = lax.all_to_all(parts, ('x', 'side'), 0, 0, tiled=True)  13.8 us
    ppermute x1, waiting for transfers between devices, body(): edge = lax.ppermute(edge, ('row', 'pair', 'side'), ends)  6.86 us
    all_to_all x1, starting transfers between devices, body(): grad = lax.all_to_all(mine, ('x', 'half', 'pair'), 0, 0, tiled=True)  6.36 us
    all_to_all x1, waiting for transfers between devices, body(): grad = lax.all_to_all(mine, ('x', 'half', 'pair'), 0, 0, tiled=True)  4.38 us
    pallas_call x1, Pallas kernels, project(): pl.pallas_call(functools.partial(project_kernel, mats, counts.shape[0], s...  3.48 us
    unnamed x10, local copies, waits for them, and re-layouts  2.56 us
    pallas_call x1, Pallas kernels, stage(): pl.pallas_call(stage_kernel, out_shape=[jax.ShapeDtypeStruct((mats * dept...  2.16 us
  transfers between devices with their start and end apart: 2, of which 2 were waited for; matrix products, arithmetic and copies ran while one was open for 0% of the time, Pallas kernels for 1%

profile of v10, /device:TPU:448, one launch (start us, length us, event | category | flops | bytes accessed | tf_op | source)
XLA Modules:
  0.0 58.3 jit_solution(17714372500432009358)
XLA Ops:
  0.0 0.0 copy-start
  0.0 0.9 %copy-done = f32[8,3,2048]{2,0,1:T(8,128)S(1)} copy-done((f32[8,3,2048]{2,0,1:T(8,128)S(1)}, f32[8,3,2048]{2,0,1:T(8,128)}, u32[]{:S(2)}) %copy-start) | copy-done | bytes 196632
  0.9 0.0 copy-start.3
  0.9 0.9 %copy-done.3 = bf16[1,32,4,1024]{3,2,1,0:T(4,128)(2,1)S(1)} copy-done((bf16[1,32,4,1024]{3,2,1,0:T(4,128)(2,1)S(1)}, bf16[1,32,4,1024]{3,2,1,0:T(4,128)(2,1)}, u32[]{:S(2)}) %copy-start.3) | copy-done | bytes 262168
  1.9 0.0 copy-start.4
  1.9 0.7 %copy-done.4 = f32[4,3]{1,0:T(4,128)S(1)} copy-done((f32[4,3]{1,0:T(4,128)S(1)}, f32[4,3]{1,0:T(4,128)}, u32[]{:S(2)}) %copy-start.4) | copy-done | bytes 72
  2.6 2.2 %shard_map.55 = (bf16[24,2048]{1,0:T(8,128)(2,1)S(1)}, f32[12,8,128]{2,1,0:T(8,128)S(1)}, f32[4,32,1024]{2,1,0:T(8,128)S(1)}, bf16[512,2048]{1,0:T(8,128)(2,1)S(1)}) custom-call(f32[3,8,2048]{2,1,0:T(8,128)S(1)} %bitcast.8, f32[4,3]{1,0:T(4,128)S(1)} %copy-done.4, bf16[32,4,1024]{2,1,0:T(4,128)(2,1)S(1)} %bitcast.15, bf16[1024,2048]{1,0:T(8,128)(2,1)} %bitcast.16), custom_call_target="tpu_custom_call" | custom-call | tf_op jit(solution)/shard_map/pallas_call | solution.py:39
  4.7 14.8 %all_gather.3.x_ref = bf16[96,2048]{1,0:T(8,128)(2,1)S(1)} all-gather(bf16[24,2048]{1,0:T(8,128)(2,1)S(1)} %get-tuple-element.12), channel_id=1, replica_groups=mesh['x'=4,'half'=2,'row'=16,'pair'=2,'side'=2] {'pair','side'}, dimensions={0}, use_global_device_ids=true | all-gather | bytes 491520 | tf_op jit(solution)/shard_map/all_gather | solution.py:259
  19.5 0.0 copy-start.1
  19.5 0.0 copy-start.2
  19.5 3.5 %shard_map.56 = bf16[4,2,2,24,512]{4,3,2,1,0:T(8,128)(2,1)S(1)} custom-call(f32[12,8,128]{2,1,0:T(8,128)S(1)} %get-tuple-element.11.tiles_ref, bf16[96,2048]{1,0:T(8,128)(2,1)S(1)} %all_gather.3.x_ref, bf16[512,2048]{1,0:T(8,128)(2,1)S(1)} %get-tuple-element.13.near_ref, bf16[1024,2048]{1,0:T(8,128)(2,1)} %bitcast.17, ...), custom_call_target="tpu_custom_call" | custom-call | flops 805306368 | bytes 4194304 | tf_op jit(solution)/shard_map/pallas_call | solution.py:110
  23.0 13.8 %all_to_all.10.part_ref = bf16[8,2,24,512]{3,2,1,0:T(8,128)(2,1)S(1)} all-to-all(bf16[8,2,24,512]{3,2,1,0:T(8,128)(2,1)S(1)} %bitcast.13), channel_id=1, replica_groups=mesh['x'=4,'half'=2,'row'=16,'pair'=2,'side'=2] {'x','side'}, dimensions={0} | all-to-all | bytes 786432 | tf_op jit(solution)/shard_map/all_to_all | solution.py:262
  36.8 0.0 copy-done.1
  36.8 0.8 %shard_map.57 = (bf16[8,2,24,512]{3,2,1,0:T(8,128)(2,1)}, f32[3,2048]{1,0:T(4,128)S(1)}) custom-call(bf16[8,2,24,512]{3,2,1,0:T(8,128)(2,1)S(1)} %all_to_all.10.part_ref, f32[3,8,2048]{2,1,0:T(8,128)S(1)} %bitcast.9), custom_call_target="tpu_custom_call" | custom-call | tf_op jit(solution)/shard_map/pallas_call | solution.py:210
  37.6 6.4 %all-to-all-start.1 = ((bf16[16,24,512]{2,1,0:T(8,128)(2,1)}), bf16[16,24,512]{2,1,0:T(8,128)(2,1)S(1)}, u32[]{:S(2)}, u32[]{:S(2)}) async-start(bf16[16,24,512]{2,1,0:T(8,128)(2,1)} %bitcast.4), calls=%async_computation.1 | async-start | bytes 786432 | tf_op jit(solution)/shard_map/all_to_all | solution.py:270
  44.0 1.9 %collective-permute-start = (f32[3,2048]{1,0:T(4,128)S(1)}, f32[3,2048]{1,0:T(4,128)S(1)}, u32[]{:S(2)}, u32[]{:S(2)}) collective-permute-start(f32[3,2048]{1,0:T(4,128)S(1)} %get-tuple-element.16), channel_id=1, source_target_pairs={{3,4},{4,3},{7,8},{8,7},{11,12},{12,11},{15,16},{16,15},{19,20},{2... | collective-permute-start | bytes 73736 | tf_op jit(solution)/shard_map/ppermute | solution.py:268
  45.9 6.9 %collective-permute-done.edge_ref = f32[3,2048]{1,0:T(4,128)S(1)} collective-permute-done((f32[3,2048]{1,0:T(4,128)S(1)}, f32[3,2048]{1,0:T(4,128)S(1)}, u32[]{:S(2)}, u32[]{:S(2)}) %collective-permute-start) | collective-permute-done | bytes 24608 | tf_op jit(solution)/shard_map/ppermute | solution.py:268
  52.8 0.4 shard_map.58.smooth_ref
  53.1 4.4 %all-to-all-done.1 = bf16[16,24,512]{2,1,0:T(8,128)(2,1)S(1)} async-done(((bf16[16,24,512]{2,1,0:T(8,128)(2,1)}), bf16[16,24,512]{2,1,0:T(8,128)(2,1)S(1)}, u32[]{:S(2)}, u32[]{:S(2)}) %all-to-all-start.1) | async-done | bytes 393248 | tf_op jit(solution)/shard_map/all_to_all | solution.py:270
  57.5 0.0 copy-done.2
  57.5 0.8 %shard_map.59 = f32[3,8,2048]{2,1,0:T(8,128)} custom-call(bf16[4,4,24,512]{3,2,1,0:T(8,128)(2,1)S(1)} %bitcast.12, f32[3,8,2048]{2,1,0:T(8,128)S(1)} %shard_map.58.smooth_ref, bf16[3,3,8,2048]{3,2,1,0:T(8,128)(2,1)S(1)} %bitcast.14, f32[3,8,2048]{2,1,0:T(8,128)S(1)} %bitcast.11), custom_call_target="tpu_custom_call" | custom-call | tf_op jit(solution)/shard_map/pallas_call | solution.py:239
Async XLA Ops:
  0.0 0.9 %copy-start = (f32[8,3,2048]{2,0,1:T(8,128)S(1)}, f32[8,3,2048]{2,0,1:T(8,128)}, u32[]{:S(2)}) copy-start(f32[8,3,2048]{2,0,1:T(8,128)} %param.5) | copy-start | bytes 589828
  0.9 0.9 %copy-start.3 = (bf16[1,32,4,1024]{3,2,1,0:T(4,128)(2,1)S(1)}, bf16[1,32,4,1024]{3,2,1,0:T(4,128)(2,1)}, u32[]{:S(2)}) copy-start(bf16[1,32,4,1024]{3,2,1,0:T(4,128)(2,1)} %param.7) | copy-start | bytes 786436
  1.9 0.7 %copy-start.4 = (f32[4,3]{1,0:T(4,128)S(1)}, f32[4,3]{1,0:T(4,128)}, u32[]{:S(2)}) copy-start(f32[4,3]{1,0:T(4,128)} %atten_ref.1) | copy-start | bytes 148
  19.5 17.3 %copy-start.1 = (f32[8,3,2048]{2,0,1:T(8,128)S(1)}, f32[8,3,2048]{2,0,1:T(8,128)}, u32[]{:S(2)}) copy-start(f32[8,3,2048]{2,0,1:T(8,128)} %param.5) | copy-start | bytes 589828
  19.5 38.0 %copy-start.2 = (bf16[8,3,3,2048]{3,0,2,1:T(8,128)(2,1)S(1)}, bf16[8,3,3,2048]{3,0,2,1:T(8,128)(2,1)}, u32[]{:S(2)}) copy-start(bf16[8,3,3,2048]{3,0,2,1:T(8,128)(2,1)} %param.9) | copy-start | bytes 884740
  37.6 19.9 %all-to-all-start.1 = ((bf16[16,24,512]{2,1,0:T(8,128)(2,1)}), bf16[16,24,512]{2,1,0:T(8,128)(2,1)S(1)}, u32[]{:S(2)}, u32[]{:S(2)}) async-start(bf16[16,24,512]{2,1,0:T(8,128)(2,1)} %bitcast.4), calls=%async_computation.1 | async-start | bytes 786432 | tf_op jit(solution)/shard_map/all_to_all | solution.py:270
  44.0 8.8 %collective-permute-start = (f32[3,2048]{1,0:T(4,128)S(1)}, f32[3,2048]{1,0:T(4,128)S(1)}, u32[]{:S(2)}, u32[]{:S(2)}) collective-permute-start(f32[3,2048]{1,0:T(4,128)S(1)} %get-tuple-element.16), channel_id=1, source_target_pairs={{3,4},{4,3},{7,8},{8,7},{11,12},{12,11},{15,16},{16,15},{19,20},{2... | collective-permute-start | bytes 73736 | tf_op jit(solution)/shard_map/ppermute | solution.py:268

commit v11 on v9

--- a/solution.py
+++ b/solution.py
@@ -99,7 +99,7 @@
 def project_kernel(mats, bins, slabs, tiles_ref, x_ref, near_ref, proj_ref, counts_ref, out_ref, resid_ref, rest_ref, sems):
     rows, pix = x_ref.shape
     cols, held = proj_ref.shape[0], near_ref.shape[0]
-    wide = 256
+    wide = 512
     copies = [
         pltpu.make_async_copy(
             proj_ref.at[at : at + wide], rest_ref.at[at - held : at - held + wide], sems.at[i]
@@ -156,7 +156,7 @@
         scratch_shapes=[
             pltpu.VMEM((rows, cols), BF16),
             pltpu.VMEM((cols - near.shape[0], pix), BF16),
-            pltpu.SemaphoreType.DMA(((cols - near.shape[0]) // 256,)),
+            pltpu.SemaphoreType.DMA(((cols - near.shape[0]) // 512,)),
         ],
         compiler_params=pltpu.CompilerParams(vmem_limit_bytes=MEDIUM),
         cost_estimate=pl.CostEstimate(

time: 56.6 us -> 56.5 us (level)
  no operation moved by 1% of the time
where the time goes in v11:
time: 56.5 us; the launch traced here: 56 us
  waiting for transfers between devices  20.1 us (36%)
  starting transfers between devices  13.5 us (24%)
  blocking collectives  12.2 us (22%)
  Pallas kernels  8.61 us (15%)
  local copies, waits for them, and re-layouts  1.64 us (3%)
    all_to_all x1, blocking collectives, body(): parts = lax.all_to_all(parts, ('x', 'side'), 0, 0, tiled=True)  12.2 us
    all_to_all x1, waiting for transfers between devices, body(): lax.all_to_all(spread(vol, slabs), ('pair', 'side'), 0, 0, tiled=True)  8.41 us
    ppermute x1, waiting for transfers between devices, body(): edge = lax.ppermute(edge, ('row', 'pair', 'side'), ends)  7.92 us
    all_to_all x1, starting transfers between devices, body(): grad = lax.all_to_all(mine, ('x', 'half', 'pair'), 0, 0, tiled=True)  6.65 us
    all_to_all x1, starting transfers between devices, body(): lax.all_to_all(spread(vol, slabs), ('pair', 'side'), 0, 0, tiled=True)  4.88 us
    all_to_all x1, waiting for transfers between devices, body(): grad = lax.all_to_all(mine, ('x', 'half', 'pair'), 0, 0, tiled=True)  3.74 us
    pallas_call x1, Pallas kernels, project(): pl.pallas_call(functools.partial(project_kernel, mats, counts.shape[0], s...  3.29 us
    ppermute x1, starting transfers between devices, body(): edge = lax.ppermute(edge, ('row', 'pair', 'side'), ends)  1.92 us
  transfers between devices with their start and end apart: 3, of which 3 were waited for; matrix products, arithmetic and copies ran while one was open for 0% of the time, Pallas kernels for 4%

profile of v11, /device:TPU:448, one launch (start us, length us, event | category | flops | bytes accessed | tf_op | source)
XLA Modules:
  0.0 56.0 jit_solution(11999797330549924345)
XLA Ops:
  0.0 1.7 %shard_map.56 = bf16[4,24,2048]{2,1,0:T(8,128)(2,1)} custom-call(f32[3,8,2048]{2,1,0:T(8,128)} %bitcast.11), custom_call_target="tpu_custom_call" | custom-call | tf_op jit(solution)/shard_map/pallas_call | solution.py:40
  1.7 4.9 %all-to-all-start = ((bf16[4,24,2048]{2,1,0:T(8,128)(2,1)}), bf16[4,24,2048]{2,1,0:T(8,128)(2,1)S(1)}, u32[]{:S(2)}, u32[]{:S(2)}) async-start(bf16[4,24,2048]{2,1,0:T(8,128)(2,1)} %shard_map.56), calls=%async_computation | async-start | bytes 786432 | tf_op jit(solution)/shard_map/all_to_all | solution.py:298
  6.6 0.0 copy-start.2
  6.6 0.9 %copy-done.2 = bf16[1,32,4,1024]{3,2,1,0:T(4,128)(2,1)S(1)} copy-done((bf16[1,32,4,1024]{3,2,1,0:T(4,128)(2,1)S(1)}, bf16[1,32,4,1024]{3,2,1,0:T(4,128)(2,1)}, u32[]{:S(2)}) %copy-start.2) | copy-done | bytes 262168
  7.6 0.0 copy-start.3
  7.6 0.7 %copy-done.3 = f32[4,3]{1,0:T(4,128)S(1)} copy-done((f32[4,3]{1,0:T(4,128)S(1)}, f32[4,3]{1,0:T(4,128)}, u32[]{:S(2)}) %copy-start.3) | copy-done | bytes 72
  8.3 1.6 %shard_map.55 = (bf16[512,2048]{1,0:T(8,128)(2,1)S(1)}, f32[4,32,1024]{2,1,0:T(8,128)S(1)}, f32[12,8,128]{2,1,0:T(8,128)S(1)}) custom-call(f32[4,3]{1,0:T(4,128)S(1)} %copy-done.3, bf16[1024,2048]{1,0:T(8,128)(2,1)} %bitcast.19, bf16[32,4,1024]{2,1,0:T(4,128)(2,1)S(1)} %bitcast.18), custom_call_target="tpu_custom_call" | custom-call | bytes 8388608 | tf_op jit(solution)/shard_map/pallas_call | solution.py:76
  9.9 8.4 %all-to-all-done = bf16[4,24,2048]{2,1,0:T(8,128)(2,1)S(1)} async-done(((bf16[4,24,2048]{2,1,0:T(8,128)(2,1)}), bf16[4,24,2048]{2,1,0:T(8,128)(2,1)S(1)}, u32[]{:S(2)}, u32[]{:S(2)}) %all-to-all-start) | async-done | bytes 393248 | tf_op jit(solution)/shard_map/all_to_all | solution.py:298
  18.3 0.0 copy-start
  18.3 0.0 copy-start.1
  18.3 3.3 %shard_map.57 = bf16[4,2,2,24,512]{4,3,2,1,0:T(8,128)(2,1)S(1)} custom-call(f32[12,8,128]{2,1,0:T(8,128)S(1)} %get-tuple-element.10.tiles_ref, bf16[96,2048]{1,0:T(8,128)(2,1)S(1)} %bitcast.9, bf16[512,2048]{1,0:T(8,128)(2,1)S(1)} %get-tuple-element.11.near_ref, bf16[1024,2048]{1,0:T(8,128)(2,1)} %bitcast.20, f32[4,32,1024]{2,1,0:T(8,128)S(1)} %get-tuple-element.12.counts_ref), custom_call_target="tpu_custom_call" | custom-call | flops 805306368 | bytes 4194304 | tf_op jit(solution)/shard_map/pallas_call | solution.py:151
  21.6 12.2 %all_to_all.15.part_ref = bf16[8,2,24,512]{3,2,1,0:T(8,128)(2,1)S(1)} all-to-all(bf16[8,2,24,512]{3,2,1,0:T(8,128)(2,1)S(1)} %bitcast.16), channel_id=1, replica_groups=mesh['x'=4,'half'=2,'row'=16,'pair'=2,'side'=2] {'x','side'}, dimensions={0} | all-to-all | bytes 786432 | tf_op jit(solution)/shard_map/all_to_all | solution.py:303
  33.8 0.0 copy-done
  33.8 0.8 %shard_map.58 = (bf16[8,2,24,512]{3,2,1,0:T(8,128)(2,1)}, f32[3,2048]{1,0:T(4,128)S(1)}) custom-call(bf16[8,2,24,512]{3,2,1,0:T(8,128)(2,1)S(1)} %all_to_all.15.part_ref, f32[3,8,2048]{2,1,0:T(8,128)S(1)} %bitcast.12), custom_call_target="tpu_custom_call" | custom-call | tf_op jit(solution)/shard_map/pallas_call | solution.py:251
  34.6 6.7 %all-to-all-start.2 = ((bf16[16,24,512]{2,1,0:T(8,128)(2,1)}), bf16[16,24,512]{2,1,0:T(8,128)(2,1)S(1)}, u32[]{:S(2)}, u32[]{:S(2)}) async-start(bf16[16,24,512]{2,1,0:T(8,128)(2,1)} %bitcast.5), calls=%async_computation.2 | async-start | bytes 786432 | tf_op jit(solution)/shard_map/all_to_all | solution.py:311
  41.3 1.9 %collective-permute-start = (f32[3,2048]{1,0:T(4,128)S(1)}, f32[3,2048]{1,0:T(4,128)S(1)}, u32[]{:S(2)}, u32[]{:S(2)}) collective-permute-start(f32[3,2048]{1,0:T(4,128)S(1)} %get-tuple-element.14), channel_id=1, source_target_pairs={{3,4},{4,3},{7,8},{8,7},{11,12},{12,11},{15,16},{16,15},{19,20},{2... | collective-permute-start | bytes 73736 | tf_op jit(solution)/shard_map/ppermute | solution.py:309
  43.2 7.9 %collective-permute-done.edge_ref = f32[3,2048]{1,0:T(4,128)S(1)} collective-permute-done((f32[3,2048]{1,0:T(4,128)S(1)}, f32[3,2048]{1,0:T(4,128)S(1)}, u32[]{:S(2)}, u32[]{:S(2)}) %collective-permute-start) | collective-permute-done | bytes 24608 | tf_op jit(solution)/shard_map/ppermute | solution.py:309
  51.1 0.4 shard_map.59.smooth_ref
  51.5 3.7 %all-to-all-done.2 = bf16[16,24,512]{2,1,0:T(8,128)(2,1)S(1)} async-done(((bf16[16,24,512]{2,1,0:T(8,128)(2,1)}), bf16[16,24,512]{2,1,0:T(8,128)(2,1)S(1)}, u32[]{:S(2)}, u32[]{:S(2)}) %all-to-all-start.2) | async-done | bytes 393248 | tf_op jit(solution)/shard_map/all_to_all | solution.py:311
  55.2 0.0 copy-done.1
  55.2 0.8 %shard_map.60 = f32[3,8,2048]{2,1,0:T(8,128)} custom-call(bf16[4,4,24,512]{3,2,1,0:T(8,128)(2,1)S(1)} %bitcast.15, f32[3,8,2048]{2,1,0:T(8,128)S(1)} %shard_map.59.smooth_ref, bf16[3,3,8,2048]{3,2,1,0:T(8,128)(2,1)S(1)} %bitcast.17, f32[3,8,2048]{2,1,0:T(8,128)S(1)} %bitcast.14), custom_call_target="tpu_custom_call" | custom-call | tf_op jit(solution)/shard_map/pallas_call | solution.py:280
Async XLA Ops:
  1.7 16.6 %all-to-all-start = ((bf16[4,24,2048]{2,1,0:T(8,128)(2,1)}), bf16[4,24,2048]{2,1,0:T(8,128)(2,1)S(1)}, u32[]{:S(2)}, u32[]{:S(2)}) async-start(bf16[4,24,2048]{2,1,0:T(8,128)(2,1)} %shard_map.56), calls=%async_computation | async-start | bytes 786432 | tf_op jit(solution)/shard_map/all_to_all | solution.py:298
  6.6 0.9 %copy-start.2 = (bf16[1,32,4,1024]{3,2,1,0:T(4,128)(2,1)S(1)}, bf16[1,32,4,1024]{3,2,1,0:T(4,128)(2,1)}, u32[]{:S(2)}) copy-start(bf16[1,32,4,1024]{3,2,1,0:T(4,128)(2,1)} %param.7) | copy-start | bytes 786436
  7.6 0.7 %copy-start.3 = (f32[4,3]{1,0:T(4,128)S(1)}, f32[4,3]{1,0:T(4,128)}, u32[]{:S(2)}) copy-start(f32[4,3]{1,0:T(4,128)} %atten_ref.1) | copy-start | bytes 148
  18.3 15.5 %copy-start = (f32[8,3,2048]{2,0,1:T(8,128)S(1)}, f32[8,3,2048]{2,0,1:T(8,128)}, u32[]{:S(2)}) copy-start(f32[8,3,2048]{2,0,1:T(8,128)} %param.5) | copy-start | bytes 589828
  18.3 36.9 %copy-start.1 = (bf16[8,3,3,2048]{3,0,2,1:T(8,128)(2,1)S(1)}, bf16[8,3,3,2048]{3,0,2,1:T(8,128)(2,1)}, u32[]{:S(2)}) copy-start(bf16[8,3,3,2048]{3,0,2,1:T(8,128)(2,1)} %param.9) | copy-start | bytes 884740
  34.6 20.6 %all-to-all-start.2 = ((bf16[16,24,512]{2,1,0:T(8,128)(2,1)}), bf16[16,24,512]{2,1,0:T(8,128)(2,1)S(1)}, u32[]{:S(2)}, u32[]{:S(2)}) async-start(bf16[16,24,512]{2,1,0:T(8,128)(2,1)} %bitcast.5), calls=%async_computation.2 | async-start | bytes 786432 | tf_op jit(solution)/shard_map/all_to_all | solution.py:311
  41.3 9.9 %collective-permute-start = (f32[3,2048]{1,0:T(4,128)S(1)}, f32[3,2048]{1,0:T(4,128)S(1)}, u32[]{:S(2)}, u32[]{:S(2)}) collective-permute-start(f32[3,2048]{1,0:T(4,128)S(1)} %get-tuple-element.14), channel_id=1, source_target_pairs={{3,4},{4,3},{7,8},{8,7},{11,12},{12,11},{15,16},{16,15},{19,20},{2... | collective-permute-start | bytes 73736 | tf_op jit(solution)/shard_map/ppermute | solution.py:309

commit v12 on v11

--- a/solution.py
+++ b/solution.py
@@ -133,13 +133,13 @@
                     parts[m] = term if parts[m] is None else parts[m] + term
             blocks += parts
         resid_ref[:, at : at + wide] = jnp.concatenate(blocks, 0).astype(BF16)
-    owners, sides, _, _, span = out_ref.shape
+    owners, _, sides, _, span = out_ref.shape
     for owner in range(owners):
         own = slice(owner * span, (owner + 1) * span)
         back = jnp.dot(resid_ref[:, :held], near_ref[:, own], preferred_element_type=F32)
         back = back + jnp.dot(resid_ref[:, held:], rest_ref[:, own], preferred_element_type=F32)
         for slab in range(slabs):
-            out_ref[owner, slab % sides, slab // sides] = back[
+            out_ref[owner, slab // sides, slab % sides] = back[
                 slab * per_slab : (slab + 1) * per_slab
             ].astype(BF16)
 
@@ -147,7 +147,7 @@
 def project(tiles, x_all, near, projector, counts, owners, sides, slabs, mats):
     rows, pix = x_all.shape
     cols = counts.shape[2]
-    out = (owners, sides, slabs // sides, rows // slabs, pix // owners)
+    out = (owners, slabs // sides, sides, rows // slabs, pix // owners)
     return pl.pallas_call(
         functools.partial(project_kernel, mats, counts.shape[0], slabs),
         out_shape=jax.ShapeDtypeStruct(out, BF16),
@@ -299,17 +299,16 @@
     x_all = x_all.reshape(slabs * rows, pix)
     near, binned, tiles = stage(atten, projector[0], counts[0], projector.shape[1] // 2)
     parts = project(tiles, x_all, near, projector[0], binned, owners, sides, slabs, mats)
-    parts = parts.reshape(owners * sides, pairs, rows, span)
-    parts = lax.all_to_all(parts, ("x", "side"), 0, 0, tiled=True)
+    parts = parts.reshape(owners * slabs, rows, span)
+    parts = lax.all_to_all(parts, ("x", "pair", "side"), 0, 0, tiled=True)
     mine, edge = total_copies(parts, vol, float(views_all) ** (-0.5), owners * halves)
     ends = []
     for g in range(groups - 1):
         last, start = g * slabs + slabs - 1, (g + 1) * slabs
         ends += [(last, start), (start, last)]
     edge = lax.ppermute(edge, ("row", "pair", "side"), ends)
-    mine = mine.reshape(owners * halves * pairs, rows, span)
-    grad = lax.all_to_all(mine, ("x", "half", "pair"), 0, 0, tiled=True)
-    grad = grad.reshape(owners, halves * pairs, rows, span)
+    grad = lax.all_to_all(mine, ("x", "half"), 0, 0, tiled=True)
+    grad = grad.reshape(owners, halves, rows, span)
     smoothed = smooth(vol, x_all, edge)
     updated = newton_step(grad, smoothed, newton.transpose(1, 2, 0, 3), vol)
     return updated.transpose(1, 0, 2)

time: 56.5 us -> 58.4 us (1.034)
  blocking collectives: 12.2 us -> 17.7 us
  waiting for transfers between devices: 20.1 us -> 17 us
    all_to_all x1, blocking collectives: 12.2 us -> 17.7 us  [body(): parts = lax.all_to_all(parts, ('x', 'pair', 'side'), 0, 0, tiled=True)]
    all_to_all x1, waiting for transfers between devices: 3.74 us -> 1.98 us  [body(): grad = lax.all_to_all(mine, ('x', 'half'), 0, 0, tiled=True)]
    ppermute x1, waiting for transfers between devices: 7.92 us -> 6.61 us  [body(): edge = lax.ppermute(edge, ('row', 'pair', 'side'), ends)]
  transfers between devices with their start and end apart: 3 -> 3, of which waited for: 3 -> 3; matrix products, arithmetic and copies ran while one was open for 0% -> 0% of each run, Pallas kernels for 4% -> 3%
where the time goes in v12:
time: 58.4 us; the launch traced here: 57.9 us
  blocking collectives  17.7 us (30%)
  waiting for transfers between devices  17 us (29%)
  starting transfers between devices  13 us (22%)
  Pallas kernels  8.52 us (15%)
  local copies, waits for them, and re-layouts  1.64 us (3%)
    all_to_all x1, blocking collectives, body(): parts = lax.all_to_all(parts, ('x', 'pair', 'side'), 0, 0, tiled=True)  17.7 us
    all_to_all x1, waiting for transfers between devices, body(): lax.all_to_all(spread(vol, slabs), ('pair', 'side'), 0, 0, tiled=True)  8.41 us
    ppermute x1, waiting for transfers between devices, body(): edge = lax.ppermute(edge, ('row', 'pair', 'side'), ends)  6.61 us
    all_to_all x1, starting transfers between devices, body(): grad = lax.all_to_all(mine, ('x', 'half'), 0, 0, tiled=True)  6.24 us
    all_to_all x1, starting transfers between devices, body(): lax.all_to_all(spread(vol, slabs), ('pair', 'side'), 0, 0, tiled=True)  4.88 us
    pallas_call x1, Pallas kernels, project(): pl.pallas_call(functools.partial(project_kernel, mats, counts.shape[0], s...  3.29 us
    all_to_all x1, waiting for transfers between devices, body(): grad = lax.all_to_all(mine, ('x', 'half'), 0, 0, tiled=True)  1.98 us
    ppermute x1, starting transfers between devices, body(): edge = lax.ppermute(edge, ('row', 'pair', 'side'), ends)  1.91 us
  transfers between devices with their start and end apart: 3, of which 3 were waited for; matrix products, arithmetic and copies ran while one was open for 0% of the time, Pallas kernels for 3%

profile of v12, /device:TPU:448, one launch (start us, length us, event | category | flops | bytes accessed | tf_op | source)
XLA Modules:
  0.0 57.9 jit_solution(15685408762956041744)
XLA Ops:
  0.0 1.7 %shard_map.56 = bf16[4,24,2048]{2,1,0:T(8,128)(2,1)} custom-call(f32[3,8,2048]{2,1,0:T(8,128)} %bitcast.10), custom_call_target="tpu_custom_call" | custom-call | tf_op jit(solution)/shard_map/pallas_call | solution.py:40
  1.7 4.9 %all-to-all-start = ((bf16[4,24,2048]{2,1,0:T(8,128)(2,1)}), bf16[4,24,2048]{2,1,0:T(8,128)(2,1)S(1)}, u32[]{:S(2)}, u32[]{:S(2)}) async-start(bf16[4,24,2048]{2,1,0:T(8,128)(2,1)} %shard_map.56), calls=%async_computation | async-start | bytes 786432 | tf_op jit(solution)/shard_map/all_to_all | solution.py:298
  6.6 0.0 copy-start.2
  6.6 0.9 %copy-done.2 = bf16[1,32,4,1024]{3,2,1,0:T(4,128)(2,1)S(1)} copy-done((bf16[1,32,4,1024]{3,2,1,0:T(4,128)(2,1)S(1)}, bf16[1,32,4,1024]{3,2,1,0:T(4,128)(2,1)}, u32[]{:S(2)}) %copy-start.2) | copy-done | bytes 262168
  7.6 0.0 copy-start.3
  7.6 0.7 %copy-done.3 = f32[4,3]{1,0:T(4,128)S(1)} copy-done((f32[4,3]{1,0:T(4,128)S(1)}, f32[4,3]{1,0:T(4,128)}, u32[]{:S(2)}) %copy-start.3) | copy-done | bytes 72
  8.3 1.6 %shard_map.55 = (bf16[512,2048]{1,0:T(8,128)(2,1)S(1)}, f32[4,32,1024]{2,1,0:T(8,128)S(1)}, f32[12,8,128]{2,1,0:T(8,128)S(1)}) custom-call(f32[4,3]{1,0:T(4,128)S(1)} %copy-done.3, bf16[1024,2048]{1,0:T(8,128)(2,1)} %bitcast.18, bf16[32,4,1024]{2,1,0:T(4,128)(2,1)S(1)} %bitcast.17), custom_call_target="tpu_custom_call" | custom-call | bytes 8388608 | tf_op jit(solution)/shard_map/pallas_call | solution.py:76
  9.9 8.4 %all-to-all-done = bf16[4,24,2048]{2,1,0:T(8,128)(2,1)S(1)} async-done(((bf16[4,24,2048]{2,1,0:T(8,128)(2,1)}), bf16[4,24,2048]{2,1,0:T(8,128)(2,1)S(1)}, u32[]{:S(2)}, u32[]{:S(2)}) %all-to-all-start) | async-done | bytes 393248 | tf_op jit(solution)/shard_map/all_to_all | solution.py:298
  18.3 0.0 copy-start
  18.3 0.0 copy-start.1
  18.3 3.3 %shard_map.57 = bf16[4,2,2,24,512]{4,3,2,1,0:T(8,128)(2,1)S(1)} custom-call(f32[12,8,128]{2,1,0:T(8,128)S(1)} %get-tuple-element.10.tiles_ref, bf16[96,2048]{1,0:T(8,128)(2,1)S(1)} %bitcast.8, bf16[512,2048]{1,0:T(8,128)(2,1)S(1)} %get-tuple-element.11.near_ref, bf16[1024,2048]{1,0:T(8,128)(2,1)} %bitcast.19, f32[4,32,1024]{2,1,0:T(8,128)S(1)} %get-tuple-element.12.counts_ref), custom_call_target="tpu_custom_call" | custom-call | flops 805306368 | bytes 4194304 | tf_op jit(solution)/shard_map/pallas_call | solution.py:151
  21.6 17.7 %all_to_all.15.part_ref = bf16[16,24,512]{2,1,0:T(8,128)(2,1)S(1)} all-to-all(bf16[16,24,512]{2,1,0:T(8,128)(2,1)S(1)} %bitcast.14), channel_id=1, replica_groups=mesh['x'=4,'half'=2,'row'=16,'pair'=2,'side'=2] {'x','pair','side'}, dimensions={0} | all-to-all | bytes 786432 | tf_op jit(solution)/shard_map/all_to_all | solution.py:303
  39.3 0.0 copy-done
  39.3 0.7 %shard_map.58 = (bf16[8,24,512]{2,1,0:T(8,128)(2,1)}, f32[3,2048]{1,0:T(4,128)S(1)}) custom-call(bf16[16,24,512]{2,1,0:T(8,128)(2,1)S(1)} %all_to_all.15.part_ref, f32[3,8,2048]{2,1,0:T(8,128)S(1)} %bitcast.11), custom_call_target="tpu_custom_call" | custom-call | tf_op jit(solution)/shard_map/pallas_call | solution.py:251
  40.0 6.2 %all-to-all-start.2 = ((bf16[8,24,512]{2,1,0:T(8,128)(2,1)}), bf16[8,24,512]{2,1,0:T(8,128)(2,1)S(1)}, u32[]{:S(2)}, u32[]{:S(2)}) async-start(bf16[8,24,512]{2,1,0:T(8,128)(2,1)} %get-tuple-element.13), calls=%async_computation.2 | async-start | bytes 393216 | tf_op jit(solution)/shard_map/all_to_all | solution.py:310
  46.3 1.9 %collective-permute-start = (f32[3,2048]{1,0:T(4,128)S(1)}, f32[3,2048]{1,0:T(4,128)S(1)}, u32[]{:S(2)}, u32[]{:S(2)}) collective-permute-start(f32[3,2048]{1,0:T(4,128)S(1)} %get-tuple-element.14), channel_id=1, source_target_pairs={{3,4},{4,3},{7,8},{8,7},{11,12},{12,11},{15,16},{16,15},{19,20},{2... | collective-permute-start | bytes 73736 | tf_op jit(solution)/shard_map/ppermute | solution.py:309
  48.2 6.6 %collective-permute-done.edge_ref = f32[3,2048]{1,0:T(4,128)S(1)} collective-permute-done((f32[3,2048]{1,0:T(4,128)S(1)}, f32[3,2048]{1,0:T(4,128)S(1)}, u32[]{:S(2)}, u32[]{:S(2)}) %collective-permute-start) | collective-permute-done | bytes 24608 | tf_op jit(solution)/shard_map/ppermute | solution.py:309
  54.8 0.4 shard_map.59.smooth_ref
  55.2 2.0 %all-to-all-done.2 = bf16[8,24,512]{2,1,0:T(8,128)(2,1)S(1)} async-done(((bf16[8,24,512]{2,1,0:T(8,128)(2,1)}), bf16[8,24,512]{2,1,0:T(8,128)(2,1)S(1)}, u32[]{:S(2)}, u32[]{:S(2)}) %all-to-all-start.2) | async-done | bytes 196640 | tf_op jit(solution)/shard_map/all_to_all | solution.py:310
  57.1 0.0 copy-done.1
  57.1 0.8 %shard_map.60 = f32[3,8,2048]{2,1,0:T(8,128)} custom-call(bf16[4,2,24,512]{3,2,1,0:T(8,128)(2,1)S(1)} %bitcast.15, f32[3,8,2048]{2,1,0:T(8,128)S(1)} %shard_map.59.smooth_ref, bf16[3,3,8,2048]{3,2,1,0:T(8,128)(2,1)S(1)} %bitcast.16, f32[3,8,2048]{2,1,0:T(8,128)S(1)} %bitcast.13), custom_call_target="tpu_custom_call" | custom-call | tf_op jit(solution)/shard_map/pallas_call | solution.py:280
Async XLA Ops:
  1.7 16.6 %all-to-all-start = ((bf16[4,24,2048]{2,1,0:T(8,128)(2,1)}), bf16[4,24,2048]{2,1,0:T(8,128)(2,1)S(1)}, u32[]{:S(2)}, u32[]{:S(2)}) async-start(bf16[4,24,2048]{2,1,0:T(8,128)(2,1)} %shard_map.56), calls=%async_computation | async-start | bytes 786432 | tf_op jit(solution)/shard_map/all_to_all | solution.py:298
  6.6 0.9 %copy-start.2 = (bf16[1,32,4,1024]{3,2,1,0:T(4,128)(2,1)S(1)}, bf16[1,32,4,1024]{3,2,1,0:T(4,128)(2,1)}, u32[]{:S(2)}) copy-start(bf16[1,32,4,1024]{3,2,1,0:T(4,128)(2,1)} %param.7) | copy-start | bytes 786436
  7.6 0.7 %copy-start.3 = (f32[4,3]{1,0:T(4,128)S(1)}, f32[4,3]{1,0:T(4,128)}, u32[]{:S(2)}) copy-start(f32[4,3]{1,0:T(4,128)} %atten_ref.1) | copy-start | bytes 148
  18.3 21.0 %copy-start = (f32[8,3,2048]{2,0,1:T(8,128)S(1)}, f32[8,3,2048]{2,0,1:T(8,128)}, u32[]{:S(2)}) copy-start(f32[8,3,2048]{2,0,1:T(8,128)} %param.5) | copy-start | bytes 589828
  18.3 38.8 %copy-start.1 = (bf16[8,3,3,2048]{3,0,2,1:T(8,128)(2,1)S(1)}, bf16[8,3,3,2048]{3,0,2,1:T(8,128)(2,1)}, u32[]{:S(2)}) copy-start(bf16[8,3,3,2048]{3,0,2,1:T(8,128)(2,1)} %param.9) | copy-start | bytes 884740
  40.0 17.1 %all-to-all-start.2 = ((bf16[8,24,512]{2,1,0:T(8,128)(2,1)}), bf16[8,24,512]{2,1,0:T(8,128)(2,1)S(1)}, u32[]{:S(2)}, u32[]{:S(2)}) async-start(bf16[8,24,512]{2,1,0:T(8,128)(2,1)} %get-tuple-element.13), calls=%async_computation.2 | async-start | bytes 393216 | tf_op jit(solution)/shard_map/all_to_all | solution.py:310
  46.3 8.5 %collective-permute-start = (f32[3,2048]{1,0:T(4,128)S(1)}, f32[3,2048]{1,0:T(4,128)S(1)}, u32[]{:S(2)}, u32[]{:S(2)}) collective-permute-start(f32[3,2048]{1,0:T(4,128)S(1)} %get-tuple-element.14), channel_id=1, source_target_pairs={{3,4},{4,3},{7,8},{8,7},{11,12},{12,11},{15,16},{16,15},{19,20},{2... | collective-permute-start | bytes 73736 | tf_op jit(solution)/shard_map/ppermute | solution.py:309

commit v13 on v10

--- a/solution.py
+++ b/solution.py
@@ -15,16 +15,32 @@
 HBM = pl.BlockSpec(memory_space=pltpu.HBM)
 SMALL = 8 * 1024 * 1024
 MEDIUM = 49 * 1024 * 1024
-LARGE = 49 * 1024 * 1024
-
-
-def stage_kernel(
-    vol_ref, atten_ref, counts_ref, proj_ref, own_ref, tiles_ref, binned_ref, near_ref, sem
-):
+LARGE = 50 * 1024 * 1024
+HUGE = 58 * 1024 * 1024
+
+
+def spread_kernel(vol_ref, out_ref):
+    mats = vol_ref.shape[0]
+    rounded = jnp.concatenate([vol_ref[m] for m in range(mats)], 0).astype(BF16)
+    for copy in range(out_ref.shape[0]):
+        out_ref[copy] = rounded
+
+
+def spread(volume, copies):
+    mats, depth, pix = volume.shape
+    return pl.pallas_call(
+        spread_kernel,
+        out_shape=jax.ShapeDtypeStruct((copies, mats * depth, pix), BF16),
+        in_specs=[VMEM],
+        out_specs=VMEM,
+        compiler_params=pltpu.CompilerParams(vmem_limit_bytes=HUGE),
+    )(volume)
+
+
+def stage_kernel(atten_ref, proj_ref, counts_ref, near_ref, binned_ref, tiles_ref, sem):
     copy = pltpu.make_async_copy(proj_ref.at[: near_ref.shape[0]], near_ref, sem)
     copy.start()
     bins, mats = atten_ref.shape
-    own_ref[...] = jnp.concatenate([vol_ref[m] for m in range(mats)], 0).astype(BF16)
     for b in range(bins):
         for m in range(mats):
             tiles_ref[b * mats + m] = jnp.full(tiles_ref.shape[1:], atten_ref[b, m], F32)
@@ -33,22 +49,21 @@
     copy.wait()
 
 
-def stage(volume, atten, counts, projector, held):
+def stage(atten, projector, counts, held):
     slices, bins, cols = counts.shape
-    mats, depth, pix = volume.shape
     return pl.pallas_call(
         stage_kernel,
         out_shape=[
-            jax.ShapeDtypeStruct((mats * depth, pix), BF16),
+            jax.ShapeDtypeStruct((held, projector.shape[1]), BF16),
+            jax.ShapeDtypeStruct((bins, slices, cols), F32),
             jax.ShapeDtypeStruct((atten.size, 8, 128), F32),
-            jax.ShapeDtypeStruct((bins, slices, cols), F32),
-            jax.ShapeDtypeStruct((held, pix), BF16),
         ],
-        in_specs=[VMEM, SMEM, VMEM, HBM],
-        out_specs=[VMEM] * 4,
+        in_specs=[SMEM, HBM, VMEM],
+        out_specs=[VMEM] * 3,
         scratch_shapes=[pltpu.SemaphoreType.DMA(())],
         compiler_params=pltpu.CompilerParams(vmem_limit_bytes=LARGE),
-    )(volume, atten, counts, projector)
+        cost_estimate=pl.CostEstimate(flops=0, bytes_accessed=4 * projector.size, transcendentals=0),
+    )(atten, projector, counts)
 
 
 def wide_tile(tile, wide):
@@ -58,7 +73,7 @@
 def project_kernel(mats, bins, slabs, tiles_ref, x_ref, near_ref, proj_ref, counts_ref, out_ref, resid_ref, rest_ref, sems):
     rows, pix = x_ref.shape
     cols, held = proj_ref.shape[0], near_ref.shape[0]
-    wide = 256
+    wide = 512
     copies = [
         pltpu.make_async_copy(
             proj_ref.at[at : at + wide], rest_ref.at[at - held : at - held + wide], sems.at[i]
@@ -115,7 +130,7 @@
         scratch_shapes=[
             pltpu.VMEM((rows, cols), BF16),
             pltpu.VMEM((cols - near.shape[0], pix), BF16),
-            pltpu.SemaphoreType.DMA(((cols - near.shape[0]) // 256,)),
+            pltpu.SemaphoreType.DMA(((cols - near.shape[0]) // 512,)),
         ],
         compiler_params=pltpu.CompilerParams(vmem_limit_bytes=MEDIUM),
         cost_estimate=pl.CostEstimate(
@@ -254,9 +269,9 @@
     views_all = projector.shape[0] * owners * halves * slabs
     rows, span = mats * depth, pix // owners
     vol = volume.transpose(1, 0, 2)
-    held = projector.shape[1] * 2 // 4
-    own, tiles, binned, near = stage(vol, atten, counts[0], projector[0], held)
-    x_all = lax.all_gather(own, ("pair", "side"), axis=0, tiled=True)
+    x_all = lax.all_to_all(spread(vol, slabs), ("pair", "side"), 0, 0, tiled=True)
+    x_all = x_all.reshape(slabs * rows, pix)
+    near, binned, tiles = stage(atten, projector[0], counts[0], projector.shape[1] // 2)
     parts = project(tiles, x_all, near, projector[0], binned, owners, sides, slabs, mats)
     parts = parts.reshape(owners * sides, pairs, rows, span)
     parts = lax.all_to_all(parts, ("x", "side"), 0, 0, tiled=True)

time: 58.7 us -> 56.4 us (0.961)
  blocking collectives: 28.6 us -> 12.2 us
  waiting for transfers between devices: 11.2 us -> 19.5 us
  starting transfers between devices: 8.28 us -> 13.4 us
  Pallas kernels: 7.59 us -> 9.11 us
  local copies, waits for them, and re-layouts: 2.56 us -> 1.64 us
    all_gather x1 -> x0, blocking collectives: 14.8 us -> none  [body(): x_all = lax.all_gather(own, ('pair', 'side'), axis=0, tiled=True)]
    all_to_all x0 -> x1, waiting for transfers between devices: none -> 7.88 us  [body(): lax.all_to_all(spread(vol, slabs), ('pair', 'side'), 0, 0, tiled=True)]
    all_to_all x0 -> x1, starting transfers between devices: none -> 4.87 us  [body(): lax.all_to_all(spread(vol, slabs), ('pair', 'side'), 0, 0, tiled=True)]
    pallas_call x1 -> x2, Pallas kernels: 2.16 us -> 3.86 us  [the longest x1 2.16 us: stage(): pl.pallas_call(stage_kernel, out_shape=[jax.ShapeDtypeStruct((held, proje...]
    all_to_all x1, blocking collectives: 13.8 us -> 12.2 us  [body(): parts = lax.all_to_all(parts, ('x', 'side'), 0, 0, tiled=True)]
    ppermute x1, waiting for transfers between devices: 6.86 us -> 7.92 us  [body(): edge = lax.ppermute(edge, ('row', 'pair', 'side'), ends)]
    unnamed x10 -> x8, local copies, waits for them, and re-layouts: 2.56 us -> 1.64 us
    all_to_all x1, waiting for transfers between devices: 4.38 us -> 3.74 us  [body(): grad = lax.all_to_all(mine, ('x', 'half', 'pair'), 0, 0, tiled=True)]
  transfers between devices with their start and end apart: 2 -> 3, of which waited for: 2 -> 3; matrix products, arithmetic and copies ran while one was open for 0% -> 0% of each run, Pallas kernels for 1% -> 4%
where the time goes in v13:
time: 56.4 us; the launch traced here: 56 us
  waiting for transfers between devices  19.5 us (35%)
  starting transfers between devices  13.4 us (24%)
  blocking collectives  12.2 us (22%)
  Pallas kernels  9.11 us (16%)
  local copies, waits for them, and re-layouts  1.64 us (3%)
    all_to_all x1, blocking collectives, body(): parts = lax.all_to_all(parts, ('x', 'side'), 0, 0, tiled=True)  12.2 us
    ppermute x1, waiting for transfers between devices, body(): edge = lax.ppermute(edge, ('row', 'pair', 'side'), ends)  7.92 us
    all_to_all x1, waiting for transfers between devices, body(): lax.all_to_all(spread(vol, slabs), ('pair', 'side'), 0, 0, tiled=True)  7.88 us
    all_to_all x1, starting transfers between devices, body(): grad = lax.all_to_all(mine, ('x', 'half', 'pair'), 0, 0, tiled=True)  6.65 us
    all_to_all x1, starting transfers between devices, body(): lax.all_to_all(spread(vol, slabs), ('pair', 'side'), 0, 0, tiled=True)  4.87 us
    all_to_all x1, waiting for transfers between devices, body(): grad = lax.all_to_all(mine, ('x', 'half', 'pair'), 0, 0, tiled=True)  3.74 us
    pallas_call x1, Pallas kernels, project(): pl.pallas_call(functools.partial(project_kernel, mats, counts.shape[0], s...  3.29 us
    pallas_call x1, Pallas kernels, stage(): pl.pallas_call(stage_kernel, out_shape=[jax.ShapeDtypeStruct((held, proje...  2.16 us
  transfers between devices with their start and end apart: 3, of which 3 were waited for; matrix products, arithmetic and copies ran while one was open for 0% of the time, Pallas kernels for 4%

profile of v13, /device:TPU:448, one launch (start us, length us, event | category | flops | bytes accessed | tf_op | source)
XLA Modules:
  0.0 56.0 jit_solution(14260654235138124035)
XLA Ops:
  0.0 1.7 %shard_map.56 = bf16[4,24,2048]{2,1,0:T(8,128)(2,1)} custom-call(f32[3,8,2048]{2,1,0:T(8,128)} %bitcast.11), custom_call_target="tpu_custom_call" | custom-call | tf_op jit(solution)/shard_map/pallas_call | solution.py:31
  1.7 4.9 %all-to-all-start = ((bf16[4,24,2048]{2,1,0:T(8,128)(2,1)}), bf16[4,24,2048]{2,1,0:T(8,128)(2,1)S(1)}, u32[]{:S(2)}, u32[]{:S(2)}) async-start(bf16[4,24,2048]{2,1,0:T(8,128)(2,1)} %shard_map.56), calls=%async_computation | async-start | bytes 786432 | tf_op jit(solution)/shard_map/all_to_all | solution.py:272
  6.6 0.0 copy-start.2
  6.6 0.9 %copy-done.2 = bf16[1,32,4,1024]{3,2,1,0:T(4,128)(2,1)S(1)} copy-done((bf16[1,32,4,1024]{3,2,1,0:T(4,128)(2,1)S(1)}, bf16[1,32,4,1024]{3,2,1,0:T(4,128)(2,1)}, u32[]{:S(2)}) %copy-start.2) | copy-done | bytes 262168
  7.5 0.0 copy-start.3
  7.5 0.7 %copy-done.3 = f32[4,3]{1,0:T(4,128)S(1)} copy-done((f32[4,3]{1,0:T(4,128)S(1)}, f32[4,3]{1,0:T(4,128)}, u32[]{:S(2)}) %copy-start.3) | copy-done | bytes 72
  8.2 2.2 %shard_map.55 = (bf16[512,2048]{1,0:T(8,128)(2,1)S(1)}, f32[4,32,1024]{2,1,0:T(8,128)S(1)}, f32[12,8,128]{2,1,0:T(8,128)S(1)}) custom-call(f32[4,3]{1,0:T(4,128)S(1)} %copy-done.3, bf16[1024,2048]{1,0:T(8,128)(2,1)} %bitcast.19, bf16[32,4,1024]{2,1,0:T(4,128)(2,1)S(1)} %bitcast.18), custom_call_target="tpu_custom_call" | custom-call | bytes 8388608 | tf_op jit(solution)/shard_map/pallas_call | solution.py:54
  10.4 7.9 %all-to-all-done = bf16[4,24,2048]{2,1,0:T(8,128)(2,1)S(1)} async-done(((bf16[4,24,2048]{2,1,0:T(8,128)(2,1)}), bf16[4,24,2048]{2,1,0:T(8,128)(2,1)S(1)}, u32[]{:S(2)}, u32[]{:S(2)}) %all-to-all-start) | async-done | bytes 393248 | tf_op jit(solution)/shard_map/all_to_all | solution.py:272
  18.3 0.0 copy-start
  18.3 0.0 copy-start.1
  18.3 3.3 %shard_map.57 = bf16[4,2,2,24,512]{4,3,2,1,0:T(8,128)(2,1)S(1)} custom-call(f32[12,8,128]{2,1,0:T(8,128)S(1)} %get-tuple-element.10.tiles_ref, bf16[96,2048]{1,0:T(8,128)(2,1)S(1)} %bitcast.9, bf16[512,2048]{1,0:T(8,128)(2,1)S(1)} %get-tuple-element.11.near_ref, bf16[1024,2048]{1,0:T(8,128)(2,1)} %bitcast.20, f32[4,32,1024]{2,1,0:T(8,128)S(1)} %get-tuple-element.12.counts_ref), custom_call_target="tpu_custom_call" | custom-call | flops 805306368 | bytes 4194304 | tf_op jit(solution)/shard_map/pallas_call | solution.py:125
  21.6 12.2 %all_to_all.15.part_ref = bf16[8,2,24,512]{3,2,1,0:T(8,128)(2,1)S(1)} all-to-all(bf16[8,2,24,512]{3,2,1,0:T(8,128)(2,1)S(1)} %bitcast.16), channel_id=1, replica_groups=mesh['x'=4,'half'=2,'row'=16,'pair'=2,'side'=2] {'x','side'}, dimensions={0} | all-to-all | bytes 786432 | tf_op jit(solution)/shard_map/all_to_all | solution.py:277
  33.8 0.0 copy-done
  33.8 0.8 %shard_map.58 = (bf16[8,2,24,512]{3,2,1,0:T(8,128)(2,1)}, f32[3,2048]{1,0:T(4,128)S(1)}) custom-call(bf16[8,2,24,512]{3,2,1,0:T(8,128)(2,1)S(1)} %all_to_all.15.part_ref, f32[3,8,2048]{2,1,0:T(8,128)S(1)} %bitcast.12), custom_call_target="tpu_custom_call" | custom-call | tf_op jit(solution)/shard_map/pallas_call | solution.py:225
  34.6 6.7 %all-to-all-start.2 = ((bf16[16,24,512]{2,1,0:T(8,128)(2,1)}), bf16[16,24,512]{2,1,0:T(8,128)(2,1)S(1)}, u32[]{:S(2)}, u32[]{:S(2)}) async-start(bf16[16,24,512]{2,1,0:T(8,128)(2,1)} %bitcast.5), calls=%async_computation.2 | async-start | bytes 786432 | tf_op jit(solution)/shard_map/all_to_all | solution.py:285
  41.2 1.9 %collective-permute-start = (f32[3,2048]{1,0:T(4,128)S(1)}, f32[3,2048]{1,0:T(4,128)S(1)}, u32[]{:S(2)}, u32[]{:S(2)}) collective-permute-start(f32[3,2048]{1,0:T(4,128)S(1)} %get-tuple-element.14), channel_id=1, source_target_pairs={{3,4},{4,3},{7,8},{8,7},{11,12},{12,11},{15,16},{16,15},{19,20},{2... | collective-permute-start | bytes 73736 | tf_op jit(solution)/shard_map/ppermute | solution.py:283
  43.2 7.9 %collective-permute-done.edge_ref = f32[3,2048]{1,0:T(4,128)S(1)} collective-permute-done((f32[3,2048]{1,0:T(4,128)S(1)}, f32[3,2048]{1,0:T(4,128)S(1)}, u32[]{:S(2)}, u32[]{:S(2)}) %collective-permute-start) | collective-permute-done | bytes 24608 | tf_op jit(solution)/shard_map/ppermute | solution.py:283
  51.1 0.4 shard_map.59.smooth_ref
  51.4 3.7 %all-to-all-done.2 = bf16[16,24,512]{2,1,0:T(8,128)(2,1)S(1)} async-done(((bf16[16,24,512]{2,1,0:T(8,128)(2,1)}), bf16[16,24,512]{2,1,0:T(8,128)(2,1)S(1)}, u32[]{:S(2)}, u32[]{:S(2)}) %all-to-all-start.2) | async-done | bytes 393248 | tf_op jit(solution)/shard_map/all_to_all | solution.py:285
  55.2 0.0 copy-done.1
  55.2 0.8 %shard_map.60 = f32[3,8,2048]{2,1,0:T(8,128)} custom-call(bf16[4,4,24,512]{3,2,1,0:T(8,128)(2,1)S(1)} %bitcast.15, f32[3,8,2048]{2,1,0:T(8,128)S(1)} %shard_map.59.smooth_ref, bf16[3,3,8,2048]{3,2,1,0:T(8,128)(2,1)S(1)} %bitcast.17, f32[3,8,2048]{2,1,0:T(8,128)S(1)} %bitcast.14), custom_call_target="tpu_custom_call" | custom-call | tf_op jit(solution)/shard_map/pallas_call | solution.py:254
Async XLA Ops:
  1.7 16.6 %all-to-all-start = ((bf16[4,24,2048]{2,1,0:T(8,128)(2,1)}), bf16[4,24,2048]{2,1,0:T(8,128)(2,1)S(1)}, u32[]{:S(2)}, u32[]{:S(2)}) async-start(bf16[4,24,2048]{2,1,0:T(8,128)(2,1)} %shard_map.56), calls=%async_computation | async-start | bytes 786432 | tf_op jit(solution)/shard_map/all_to_all | solution.py:272
  6.6 0.9 %copy-start.2 = (bf16[1,32,4,1024]{3,2,1,0:T(4,128)(2,1)S(1)}, bf16[1,32,4,1024]{3,2,1,0:T(4,128)(2,1)}, u32[]{:S(2)}) copy-start(bf16[1,32,4,1024]{3,2,1,0:T(4,128)(2,1)} %param.7) | copy-start | bytes 786436
  7.5 0.7 %copy-start.3 = (f32[4,3]{1,0:T(4,128)S(1)}, f32[4,3]{1,0:T(4,128)}, u32[]{:S(2)}) copy-start(f32[4,3]{1,0:T(4,128)} %atten_ref.1) | copy-start | bytes 148
  18.3 15.5 %copy-start = (f32[8,3,2048]{2,0,1:T(8,128)S(1)}, f32[8,3,2048]{2,0,1:T(8,128)}, u32[]{:S(2)}) copy-start(f32[8,3,2048]{2,0,1:T(8,128)} %param.5) | copy-start | bytes 589828
  18.3 36.9 %copy-start.1 = (bf16[8,3,3,2048]{3,0,2,1:T(8,128)(2,1)S(1)}, bf16[8,3,3,2048]{3,0,2,1:T(8,128)(2,1)}, u32[]{:S(2)}) copy-start(bf16[8,3,3,2048]{3,0,2,1:T(8,128)(2,1)} %param.9) | copy-start | bytes 884740
  34.6 20.6 %all-to-all-start.2 = ((bf16[16,24,512]{2,1,0:T(8,128)(2,1)}), bf16[16,24,512]{2,1,0:T(8,128)(2,1)S(1)}, u32[]{:S(2)}, u32[]{:S(2)}) async-start(bf16[16,24,512]{2,1,0:T(8,128)(2,1)} %bitcast.5), calls=%async_computation.2 | async-start | bytes 786432 | tf_op jit(solution)/shard_map/all_to_all | solution.py:285
  41.2 9.8 %collective-permute-start = (f32[3,2048]{1,0:T(4,128)S(1)}, f32[3,2048]{1,0:T(4,128)S(1)}, u32[]{:S(2)}, u32[]{:S(2)}) collective-permute-start(f32[3,2048]{1,0:T(4,128)S(1)} %get-tuple-element.14), channel_id=1, source_target_pairs={{3,4},{4,3},{7,8},{8,7},{11,12},{12,11},{15,16},{16,15},{19,20},{2... | collective-permute-start | bytes 73736 | tf_op jit(solution)/shard_map/ppermute | solution.py:283

commit v14 on v13

--- a/solution.py
+++ b/solution.py
@@ -212,20 +212,21 @@
 def total_kernel(factor, part_ref, vol_ref, out_ref, edge_ref):
     total = jnp.sum(part_ref[...].astype(F32), axis=0) * factor
     total = total.astype(BF16)
-    for copy in range(out_ref.shape[0]):
-        out_ref[copy] = total
+    for half in range(out_ref.shape[0]):
+        for owner in range(out_ref.shape[2]):
+            out_ref[half, :, owner] = total
     slab = slab_index()
     for m in range(vol_ref.shape[0]):
         slab_m = vol_ref[m]
         edge_ref[m : m + 1] = jnp.where(slab == 0, slab_m[:1], slab_m[-1:])
 
 
-def total_copies(parts, volume, factor, copies):
+def total_copies(parts, volume, factor, halves, owners):
     mats, _, pix = volume.shape
     return pl.pallas_call(
         functools.partial(total_kernel, factor),
         out_shape=[
-            jax.ShapeDtypeStruct((copies,) + parts.shape[1:], BF16),
+            jax.ShapeDtypeStruct((halves, parts.shape[1], owners) + parts.shape[2:], BF16),
             jax.ShapeDtypeStruct((mats, pix), F32),
         ],
         in_specs=[VMEM, VMEM],
@@ -236,12 +237,12 @@
 
 def step_kernel(grad_ref, smooth_ref, newton_ref, vol_ref, out_ref):
     mats, depth, pix = vol_ref.shape
-    owners, copies, _, span = grad_ref.shape
+    copies, owners, _, span = grad_ref.shape
     for owner in range(owners):
         own = slice(owner * span, (owner + 1) * span)
-        grad = grad_ref[owner, 0].astype(F32)
+        grad = grad_ref[0, owner].astype(F32)
         for copy in range(1, copies):
-            grad = grad + grad_ref[owner, copy].astype(F32)
+            grad = grad + grad_ref[copy, owner].astype(F32)
         steps = [grad[k * depth : (k + 1) * depth] + 0.5 * smooth_ref[k, :, own] for k in range(mats)]
         for m in range(mats):
             moved = newton_ref[m, 0, :, own].astype(F32) * steps[0]
@@ -275,15 +276,15 @@
     parts = project(tiles, x_all, near, projector[0], binned, owners, sides, slabs, mats)
     parts = parts.reshape(owners * sides, pairs, rows, span)
     parts = lax.all_to_all(parts, ("x", "side"), 0, 0, tiled=True)
-    mine, edge = total_copies(parts, vol, float(views_all) ** (-0.5), owners * halves)
+    mine, edge = total_copies(parts, vol, float(views_all) ** (-0.5), halves, owners)
     ends = []
     for g in range(groups - 1):
         last, start = g * slabs + slabs - 1, (g + 1) * slabs
         ends += [(last, start), (start, last)]
     edge = lax.ppermute(edge, ("row", "pair", "side"), ends)
     mine = mine.reshape(owners * halves * pairs, rows, span)
-    grad = lax.all_to_all(mine, ("x", "half", "pair"), 0, 0, tiled=True)
-    grad = grad.reshape(owners, halves * pairs, rows, span)
+    grad = lax.all_to_all(mine, ("half", "pair", "x"), 0, 0, tiled=True)
+    grad = grad.reshape(halves * pairs, owners, rows, span)
     smoothed = smooth(vol, x_all, edge)
     updated = newton_step(grad, smoothed, newton.transpose(1, 2, 0, 3), vol)
     return updated.transpose(1, 0, 2)

time: 56.4 us -> 55.8 us (0.989)
  transfers between devices with their start and end apart: 3 -> 3, of which waited for: 3 -> 3; matrix products, arithmetic and copies ran while one was open for 0% -> 0% of each run, Pallas kernels for 4% -> 5%
where the time goes in v14:
time: 55.8 us; the launch traced here: 55.4 us
  waiting for transfers between devices  19 us (34%)
  starting transfers between devices  13.4 us (24%)
  blocking collectives  12.2 us (22%)
  Pallas kernels  9.11 us (16%)
  local copies, waits for them, and re-layouts  1.64 us (3%)
    all_to_all x1, blocking collectives, body(): parts = lax.all_to_all(parts, ('x', 'side'), 0, 0, tiled=True)  12.2 us
    all_to_all x1, waiting for transfers between devices, body(): lax.all_to_all(spread(vol, slabs), ('pair', 'side'), 0, 0, tiled=True)  7.88 us
    ppermute x1, waiting for transfers between devices, body(): edge = lax.ppermute(edge, ('row', 'pair', 'side'), ends)  7.75 us
    all_to_all x1, starting transfers between devices, body(): grad = lax.all_to_all(mine, ('half', 'pair', 'x'), 0, 0, tiled=True)  6.65 us
    all_to_all x1, starting transfers between devices, body(): lax.all_to_all(spread(vol, slabs), ('pair', 'side'), 0, 0, tiled=True)  4.87 us
    all_to_all x1, waiting for transfers between devices, body(): grad = lax.all_to_all(mine, ('half', 'pair', 'x'), 0, 0, tiled=True)  3.33 us
    pallas_call x1, Pallas kernels, project(): pl.pallas_call(functools.partial(project_kernel, mats, counts.shape[0], s...  3.29 us
    pallas_call x1, Pallas kernels, stage(): pl.pallas_call(stage_kernel, out_shape=[jax.ShapeDtypeStruct((held, proje...  2.16 us
  transfers between devices with their start and end apart: 3, of which 3 were waited for; matrix products, arithmetic and copies ran while one was open for 0% of the time, Pallas kernels for 5%

profile of v14, /device:TPU:448, one launch (start us, length us, event | category | flops | bytes accessed | tf_op | source)
XLA Modules:
  0.0 55.4 jit_solution(837204255507866259)
XLA Ops:
  0.0 1.7 %shard_map.56 = bf16[4,24,2048]{2,1,0:T(8,128)(2,1)} custom-call(f32[3,8,2048]{2,1,0:T(8,128)} %bitcast.11), custom_call_target="tpu_custom_call" | custom-call | tf_op jit(solution)/shard_map/pallas_call | solution.py:31
  1.7 4.9 %all-to-all-start = ((bf16[4,24,2048]{2,1,0:T(8,128)(2,1)}), bf16[4,24,2048]{2,1,0:T(8,128)(2,1)S(1)}, u32[]{:S(2)}, u32[]{:S(2)}) async-start(bf16[4,24,2048]{2,1,0:T(8,128)(2,1)} %shard_map.56), calls=%async_computation | async-start | bytes 786432 | tf_op jit(solution)/shard_map/all_to_all | solution.py:273
  6.6 0.0 copy-start.2
  6.6 0.9 %copy-done.2 = bf16[1,32,4,1024]{3,2,1,0:T(4,128)(2,1)S(1)} copy-done((bf16[1,32,4,1024]{3,2,1,0:T(4,128)(2,1)S(1)}, bf16[1,32,4,1024]{3,2,1,0:T(4,128)(2,1)}, u32[]{:S(2)}) %copy-start.2) | copy-done | bytes 262168
  7.5 0.0 copy-start.3
  7.5 0.7 %copy-done.3 = f32[4,3]{1,0:T(4,128)S(1)} copy-done((f32[4,3]{1,0:T(4,128)S(1)}, f32[4,3]{1,0:T(4,128)}, u32[]{:S(2)}) %copy-start.3) | copy-done | bytes 72
  8.2 2.2 %shard_map.55 = (bf16[512,2048]{1,0:T(8,128)(2,1)S(1)}, f32[4,32,1024]{2,1,0:T(8,128)S(1)}, f32[12,8,128]{2,1,0:T(8,128)S(1)}) custom-call(f32[4,3]{1,0:T(4,128)S(1)} %copy-done.3, bf16[1024,2048]{1,0:T(8,128)(2,1)} %bitcast.19, bf16[32,4,1024]{2,1,0:T(4,128)(2,1)S(1)} %bitcast.18), custom_call_target="tpu_custom_call" | custom-call | bytes 8388608 | tf_op jit(solution)/shard_map/pallas_call | solution.py:54
  10.4 7.9 %all-to-all-done = bf16[4,24,2048]{2,1,0:T(8,128)(2,1)S(1)} async-done(((bf16[4,24,2048]{2,1,0:T(8,128)(2,1)}), bf16[4,24,2048]{2,1,0:T(8,128)(2,1)S(1)}, u32[]{:S(2)}, u32[]{:S(2)}) %all-to-all-start) | async-done | bytes 393248 | tf_op jit(solution)/shard_map/all_to_all | solution.py:273
  18.3 0.0 copy-start
  18.3 0.0 copy-start.1
  18.3 3.3 %shard_map.57 = bf16[4,2,2,24,512]{4,3,2,1,0:T(8,128)(2,1)S(1)} custom-call(f32[12,8,128]{2,1,0:T(8,128)S(1)} %get-tuple-element.10.tiles_ref, bf16[96,2048]{1,0:T(8,128)(2,1)S(1)} %bitcast.9, bf16[512,2048]{1,0:T(8,128)(2,1)S(1)} %get-tuple-element.11.near_ref, bf16[1024,2048]{1,0:T(8,128)(2,1)} %bitcast.20, f32[4,32,1024]{2,1,0:T(8,128)S(1)} %get-tuple-element.12.counts_ref), custom_call_target="tpu_custom_call" | custom-call | flops 805306368 | bytes 4194304 | tf_op jit(solution)/shard_map/pallas_call | solution.py:125
  21.6 12.2 %all_to_all.15.part_ref = bf16[8,2,24,512]{3,2,1,0:T(8,128)(2,1)S(1)} all-to-all(bf16[8,2,24,512]{3,2,1,0:T(8,128)(2,1)S(1)} %bitcast.16), channel_id=1, replica_groups=mesh['x'=4,'half'=2,'row'=16,'pair'=2,'side'=2] {'x','side'}, dimensions={0} | all-to-all | bytes 786432 | tf_op jit(solution)/shard_map/all_to_all | solution.py:278
  33.8 0.0 copy-done
  33.8 0.8 %shard_map.58 = (bf16[2,2,4,24,512]{4,3,2,1,0:T(8,128)(2,1)}, f32[3,2048]{1,0:T(4,128)S(1)}) custom-call(bf16[8,2,24,512]{3,2,1,0:T(8,128)(2,1)S(1)} %all_to_all.15.part_ref, f32[3,8,2048]{2,1,0:T(8,128)S(1)} %bitcast.12), custom_call_target="tpu_custom_call" | custom-call | tf_op jit(solution)/shard_map/pallas_call | solution.py:226
  34.6 6.7 %all-to-all-start.2 = ((bf16[16,24,512]{2,1,0:T(8,128)(2,1)}), bf16[16,24,512]{2,1,0:T(8,128)(2,1)S(1)}, u32[]{:S(2)}, u32[]{:S(2)}) async-start(bf16[16,24,512]{2,1,0:T(8,128)(2,1)} %bitcast.5), calls=%async_computation.2 | async-start | bytes 786432 | tf_op jit(solution)/shard_map/all_to_all | solution.py:286
  41.2 1.9 %collective-permute-start = (f32[3,2048]{1,0:T(4,128)S(1)}, f32[3,2048]{1,0:T(4,128)S(1)}, u32[]{:S(2)}, u32[]{:S(2)}) collective-permute-start(f32[3,2048]{1,0:T(4,128)S(1)} %get-tuple-element.14), channel_id=1, source_target_pairs={{3,4},{4,3},{7,8},{8,7},{11,12},{12,11},{15,16},{16,15},{19,20},{2... | collective-permute-start | bytes 73736 | tf_op jit(solution)/shard_map/ppermute | solution.py:284
  43.2 7.7 %collective-permute-done.edge_ref = f32[3,2048]{1,0:T(4,128)S(1)} collective-permute-done((f32[3,2048]{1,0:T(4,128)S(1)}, f32[3,2048]{1,0:T(4,128)S(1)}, u32[]{:S(2)}, u32[]{:S(2)}) %collective-permute-start) | collective-permute-done | bytes 24608 | tf_op jit(solution)/shard_map/ppermute | solution.py:284
  50.9 0.4 shard_map.59.smooth_ref
  51.3 3.3 %all-to-all-done.2 = bf16[16,24,512]{2,1,0:T(8,128)(2,1)S(1)} async-done(((bf16[16,24,512]{2,1,0:T(8,128)(2,1)}), bf16[16,24,512]{2,1,0:T(8,128)(2,1)S(1)}, u32[]{:S(2)}, u32[]{:S(2)}) %all-to-all-start.2) | async-done | bytes 393248 | tf_op jit(solution)/shard_map/all_to_all | solution.py:286
  54.6 0.0 copy-done.1
  54.6 0.8 %shard_map.60 = f32[3,8,2048]{2,1,0:T(8,128)} custom-call(bf16[4,4,24,512]{3,2,1,0:T(8,128)(2,1)S(1)} %bitcast.15, f32[3,8,2048]{2,1,0:T(8,128)S(1)} %shard_map.59.smooth_ref, bf16[3,3,8,2048]{3,2,1,0:T(8,128)(2,1)S(1)} %bitcast.17, f32[3,8,2048]{2,1,0:T(8,128)S(1)} %bitcast.14), custom_call_target="tpu_custom_call" | custom-call | tf_op jit(solution)/shard_map/pallas_call | solution.py:255
Async XLA Ops:
  1.7 16.6 %all-to-all-start = ((bf16[4,24,2048]{2,1,0:T(8,128)(2,1)}), bf16[4,24,2048]{2,1,0:T(8,128)(2,1)S(1)}, u32[]{:S(2)}, u32[]{:S(2)}) async-start(bf16[4,24,2048]{2,1,0:T(8,128)(2,1)} %shard_map.56), calls=%async_computation | async-start | bytes 786432 | tf_op jit(solution)/shard_map/all_to_all | solution.py:273
  6.6 0.9 %copy-start.2 = (bf16[1,32,4,1024]{3,2,1,0:T(4,128)(2,1)S(1)}, bf16[1,32,4,1024]{3,2,1,0:T(4,128)(2,1)}, u32[]{:S(2)}) copy-start(bf16[1,32,4,1024]{3,2,1,0:T(4,128)(2,1)} %param.7) | copy-start | bytes 786436
  7.5 0.7 %copy-start.3 = (f32[4,3]{1,0:T(4,128)S(1)}, f32[4,3]{1,0:T(4,128)}, u32[]{:S(2)}) copy-start(f32[4,3]{1,0:T(4,128)} %atten_ref.1) | copy-start | bytes 148
  18.3 15.5 %copy-start = (f32[8,3,2048]{2,0,1:T(8,128)S(1)}, f32[8,3,2048]{2,0,1:T(8,128)}, u32[]{:S(2)}) copy-start(f32[8,3,2048]{2,0,1:T(8,128)} %param.5) | copy-start | bytes 589828
  18.3 36.3 %copy-start.1 = (bf16[8,3,3,2048]{3,0,2,1:T(8,128)(2,1)S(1)}, bf16[8,3,3,2048]{3,0,2,1:T(8,128)(2,1)}, u32[]{:S(2)}) copy-start(bf16[8,3,3,2048]{3,0,2,1:T(8,128)(2,1)} %param.9) | copy-start | bytes 884740
  34.6 20.0 %all-to-all-start.2 = ((bf16[16,24,512]{2,1,0:T(8,128)(2,1)}), bf16[16,24,512]{2,1,0:T(8,128)(2,1)S(1)}, u32[]{:S(2)}, u32[]{:S(2)}) async-start(bf16[16,24,512]{2,1,0:T(8,128)(2,1)} %bitcast.5), calls=%async_computation.2 | async-start | bytes 786432 | tf_op jit(solution)/shard_map/all_to_all | solution.py:286
  41.2 9.7 %collective-permute-start = (f32[3,2048]{1,0:T(4,128)S(1)}, f32[3,2048]{1,0:T(4,128)S(1)}, u32[]{:S(2)}, u32[]{:S(2)}) collective-permute-start(f32[3,2048]{1,0:T(4,128)S(1)} %get-tuple-element.14), channel_id=1, source_target_pairs={{3,4},{4,3},{7,8},{8,7},{11,12},{12,11},{15,16},{16,15},{19,20},{2... | collective-permute-start | bytes 73736 | tf_op jit(solution)/shard_map/ppermute | solution.py:284

commit v15 on v14

--- a/solution.py
+++ b/solution.py
@@ -107,13 +107,13 @@
                     parts[m] = term if parts[m] is None else parts[m] + term
             blocks += parts
         resid_ref[:, at : at + wide] = jnp.concatenate(blocks, 0).astype(BF16)
-    owners, sides, _, _, span = out_ref.shape
+    sides, owners, _, _, span = out_ref.shape
     for owner in range(owners):
         own = slice(owner * span, (owner + 1) * span)
         back = jnp.dot(resid_ref[:, :held], near_ref[:, own], preferred_element_type=F32)
         back = back + jnp.dot(resid_ref[:, held:], rest_ref[:, own], preferred_element_type=F32)
         for slab in range(slabs):
-            out_ref[owner, slab % sides, slab // sides] = back[
+            out_ref[slab % sides, owner, slab // sides] = back[
                 slab * per_slab : (slab + 1) * per_slab
             ].astype(BF16)
 
@@ -121,7 +121,7 @@
 def project(tiles, x_all, near, projector, counts, owners, sides, slabs, mats):
     rows, pix = x_all.shape
     cols = counts.shape[2]
-    out = (owners, sides, slabs // sides, rows // slabs, pix // owners)
+    out = (sides, owners, slabs // sides, rows // slabs, pix // owners)
     return pl.pallas_call(
         functools.partial(project_kernel, mats, counts.shape[0], slabs),
         out_shape=jax.ShapeDtypeStruct(out, BF16),
@@ -275,7 +275,7 @@
     near, binned, tiles = stage(atten, projector[0], counts[0], projector.shape[1] // 2)
     parts = project(tiles, x_all, near, projector[0], binned, owners, sides, slabs, mats)
     parts = parts.reshape(owners * sides, pairs, rows, span)
-    parts = lax.all_to_all(parts, ("x", "side"), 0, 0, tiled=True)
+    parts = lax.all_to_all(parts, ("side", "x"), 0, 0, tiled=True)
     mine, edge = total_copies(parts, vol, float(views_all) ** (-0.5), halves, owners)
     ends = []
     for g in range(groups - 1):

time: 55.8 us -> 56.2 us (level)
    all_to_all x1, waiting for transfers between devices: 3.33 us -> 4.07 us  [body(): grad = lax.all_to_all(mine, ('half', 'pair', 'x'), 0, 0, tiled=True)]
where the time goes in v15:
time: 56.2 us; the launch traced here: 55.8 us
  waiting for transfers between devices  19.5 us (35%)
  starting transfers between devices  13.4 us (24%)
  blocking collectives  12.1 us (22%)
  Pallas kernels  9.11 us (16%)
  local copies, waits for them, and re-layouts  1.64 us (3%)
    all_to_all x1, blocking collectives, body(): parts = lax.all_to_all(parts, ('side', 'x'), 0, 0, tiled=True)  12.1 us
    all_to_all x1, waiting for transfers between devices, body(): lax.all_to_all(spread(vol, slabs), ('pair', 'side'), 0, 0, tiled=True)  7.88 us
    ppermute x1, waiting for transfers between devices, body(): edge = lax.ppermute(edge, ('row', 'pair', 'side'), ends)  7.57 us
    all_to_all x1, starting transfers between devices, body(): grad = lax.all_to_all(mine, ('half', 'pair', 'x'), 0, 0, tiled=True)  6.59 us
    all_to_all x1, starting transfers between devices, body(): lax.all_to_all(spread(vol, slabs), ('pair', 'side'), 0, 0, tiled=True)  4.87 us
    all_to_all x1, waiting for transfers between devices, body(): grad = lax.all_to_all(mine, ('half', 'pair', 'x'), 0, 0, tiled=True)  4.07 us
    pallas_call x1, Pallas kernels, project(): pl.pallas_call(functools.partial(project_kernel, mats, counts.shape[0], s...  3.29 us
    pallas_call x1, Pallas kernels, stage(): pl.pallas_call(stage_kernel, out_shape=[jax.ShapeDtypeStruct((held, proje...  2.16 us
  transfers between devices with their start and end apart: 3, of which 3 were waited for; matrix products, arithmetic and copies ran while one was open for 0% of the time, Pallas kernels for 5%

profile of v15, /device:TPU:448, one launch (start us, length us, event | category | flops | bytes accessed | tf_op | source)
XLA Modules:
  0.0 55.8 jit_solution(10842986352049325966)
XLA Ops:
  0.0 1.7 %shard_map.56 = bf16[4,24,2048]{2,1,0:T(8,128)(2,1)} custom-call(f32[3,8,2048]{2,1,0:T(8,128)} %bitcast.11), custom_call_target="tpu_custom_call" | custom-call | tf_op jit(solution)/shard_map/pallas_call | solution.py:31
  1.7 4.9 %all-to-all-start = ((bf16[4,24,2048]{2,1,0:T(8,128)(2,1)}), bf16[4,24,2048]{2,1,0:T(8,128)(2,1)S(1)}, u32[]{:S(2)}, u32[]{:S(2)}) async-start(bf16[4,24,2048]{2,1,0:T(8,128)(2,1)} %shard_map.56), calls=%async_computation | async-start | bytes 786432 | tf_op jit(solution)/shard_map/all_to_all | solution.py:273
  6.6 0.0 copy-start.2
  6.6 0.9 %copy-done.2 = bf16[1,32,4,1024]{3,2,1,0:T(4,128)(2,1)S(1)} copy-done((bf16[1,32,4,1024]{3,2,1,0:T(4,128)(2,1)S(1)}, bf16[1,32,4,1024]{3,2,1,0:T(4,128)(2,1)}, u32[]{:S(2)}) %copy-start.2) | copy-done | bytes 262168
  7.5 0.0 copy-start.3
  7.5 0.7 %copy-done.3 = f32[4,3]{1,0:T(4,128)S(1)} copy-done((f32[4,3]{1,0:T(4,128)S(1)}, f32[4,3]{1,0:T(4,128)}, u32[]{:S(2)}) %copy-start.3) | copy-done | bytes 72
  8.2 2.2 %shard_map.55 = (bf16[512,2048]{1,0:T(8,128)(2,1)S(1)}, f32[4,32,1024]{2,1,0:T(8,128)S(1)}, f32[12,8,128]{2,1,0:T(8,128)S(1)}) custom-call(f32[4,3]{1,0:T(4,128)S(1)} %copy-done.3, bf16[1024,2048]{1,0:T(8,128)(2,1)} %bitcast.19, bf16[32,4,1024]{2,1,0:T(4,128)(2,1)S(1)} %bitcast.18), custom_call_target="tpu_custom_call" | custom-call | bytes 8388608 | tf_op jit(solution)/shard_map/pallas_call | solution.py:54
  10.4 7.9 %all-to-all-done = bf16[4,24,2048]{2,1,0:T(8,128)(2,1)S(1)} async-done(((bf16[4,24,2048]{2,1,0:T(8,128)(2,1)}), bf16[4,24,2048]{2,1,0:T(8,128)(2,1)S(1)}, u32[]{:S(2)}, u32[]{:S(2)}) %all-to-all-start) | async-done | bytes 393248 | tf_op jit(solution)/shard_map/all_to_all | solution.py:273
  18.3 0.0 copy-start
  18.3 0.0 copy-start.1
  18.3 3.3 %shard_map.57 = bf16[2,4,2,24,512]{4,3,2,1,0:T(8,128)(2,1)S(1)} custom-call(f32[12,8,128]{2,1,0:T(8,128)S(1)} %get-tuple-element.10.tiles_ref, bf16[96,2048]{1,0:T(8,128)(2,1)S(1)} %bitcast.9, bf16[512,2048]{1,0:T(8,128)(2,1)S(1)} %get-tuple-element.11.near_ref, bf16[1024,2048]{1,0:T(8,128)(2,1)} %bitcast.20, f32[4,32,1024]{2,1,0:T(8,128)S(1)} %get-tuple-element.12.counts_ref), custom_call_target="tpu_custom_call" | custom-call | flops 805306368 | bytes 4194304 | tf_op jit(solution)/shard_map/pallas_call | solution.py:125
  21.6 12.1 %all_to_all.15.part_ref = bf16[8,2,24,512]{3,2,1,0:T(8,128)(2,1)S(1)} all-to-all(bf16[8,2,24,512]{3,2,1,0:T(8,128)(2,1)S(1)} %bitcast.16), channel_id=1, replica_groups=mesh['x'=4,'half'=2,'row'=16,'pair'=2,'side'=2] {'side','x'}, dimensions={0} | all-to-all | bytes 786432 | tf_op jit(solution)/shard_map/all_to_all | solution.py:278
  33.6 0.0 copy-done
  33.6 0.8 %shard_map.58 = (bf16[2,2,4,24,512]{4,3,2,1,0:T(8,128)(2,1)}, f32[3,2048]{1,0:T(4,128)S(1)}) custom-call(bf16[8,2,24,512]{3,2,1,0:T(8,128)(2,1)S(1)} %all_to_all.15.part_ref, f32[3,8,2048]{2,1,0:T(8,128)S(1)} %bitcast.12), custom_call_target="tpu_custom_call" | custom-call | tf_op jit(solution)/shard_map/pallas_call | solution.py:226
  34.5 6.6 %all-to-all-start.2 = ((bf16[16,24,512]{2,1,0:T(8,128)(2,1)}), bf16[16,24,512]{2,1,0:T(8,128)(2,1)S(1)}, u32[]{:S(2)}, u32[]{:S(2)}) async-start(bf16[16,24,512]{2,1,0:T(8,128)(2,1)} %bitcast.5), calls=%async_computation.2 | async-start | bytes 786432 | tf_op jit(solution)/shard_map/all_to_all | solution.py:286
  41.1 1.9 %collective-permute-start = (f32[3,2048]{1,0:T(4,128)S(1)}, f32[3,2048]{1,0:T(4,128)S(1)}, u32[]{:S(2)}, u32[]{:S(2)}) collective-permute-start(f32[3,2048]{1,0:T(4,128)S(1)} %get-tuple-element.14), channel_id=1, source_target_pairs={{3,4},{4,3},{7,8},{8,7},{11,12},{12,11},{15,16},{16,15},{19,20},{2... | collective-permute-start | bytes 73736 | tf_op jit(solution)/shard_map/ppermute | solution.py:284
  43.0 7.6 %collective-permute-done.edge_ref = f32[3,2048]{1,0:T(4,128)S(1)} collective-permute-done((f32[3,2048]{1,0:T(4,128)S(1)}, f32[3,2048]{1,0:T(4,128)S(1)}, u32[]{:S(2)}, u32[]{:S(2)}) %collective-permute-start) | collective-permute-done | bytes 24608 | tf_op jit(solution)/shard_map/ppermute | solution.py:284
  50.5 0.4 shard_map.59.smooth_ref
  50.9 4.1 %all-to-all-done.2 = bf16[16,24,512]{2,1,0:T(8,128)(2,1)S(1)} async-done(((bf16[16,24,512]{2,1,0:T(8,128)(2,1)}), bf16[16,24,512]{2,1,0:T(8,128)(2,1)S(1)}, u32[]{:S(2)}, u32[]{:S(2)}) %all-to-all-start.2) | async-done | bytes 393248 | tf_op jit(solution)/shard_map/all_to_all | solution.py:286
  55.0 0.0 copy-done.1
  55.0 0.8 %shard_map.60 = f32[3,8,2048]{2,1,0:T(8,128)} custom-call(bf16[4,4,24,512]{3,2,1,0:T(8,128)(2,1)S(1)} %bitcast.15, f32[3,8,2048]{2,1,0:T(8,128)S(1)} %shard_map.59.smooth_ref, bf16[3,3,8,2048]{3,2,1,0:T(8,128)(2,1)S(1)} %bitcast.17, f32[3,8,2048]{2,1,0:T(8,128)S(1)} %bitcast.14), custom_call_target="tpu_custom_call" | custom-call | tf_op jit(solution)/shard_map/pallas_call | solution.py:255
Async XLA Ops:
  1.7 16.6 %all-to-all-start = ((bf16[4,24,2048]{2,1,0:T(8,128)(2,1)}), bf16[4,24,2048]{2,1,0:T(8,128)(2,1)S(1)}, u32[]{:S(2)}, u32[]{:S(2)}) async-start(bf16[4,24,2048]{2,1,0:T(8,128)(2,1)} %shard_map.56), calls=%async_computation | async-start | bytes 786432 | tf_op jit(solution)/shard_map/all_to_all | solution.py:273
  6.6 0.9 %copy-start.2 = (bf16[1,32,4,1024]{3,2,1,0:T(4,128)(2,1)S(1)}, bf16[1,32,4,1024]{3,2,1,0:T(4,128)(2,1)}, u32[]{:S(2)}) copy-start(bf16[1,32,4,1024]{3,2,1,0:T(4,128)(2,1)} %param.7) | copy-start | bytes 786436
  7.5 0.7 %copy-start.3 = (f32[4,3]{1,0:T(4,128)S(1)}, f32[4,3]{1,0:T(4,128)}, u32[]{:S(2)}) copy-start(f32[4,3]{1,0:T(4,128)} %atten_ref.1) | copy-start | bytes 148
  18.3 15.4 %copy-start = (f32[8,3,2048]{2,0,1:T(8,128)S(1)}, f32[8,3,2048]{2,0,1:T(8,128)}, u32[]{:S(2)}) copy-start(f32[8,3,2048]{2,0,1:T(8,128)} %param.5) | copy-start | bytes 589828
  18.3 36.7 %copy-start.1 = (bf16[8,3,3,2048]{3,0,2,1:T(8,128)(2,1)S(1)}, bf16[8,3,3,2048]{3,0,2,1:T(8,128)(2,1)}, u32[]{:S(2)}) copy-start(bf16[8,3,3,2048]{3,0,2,1:T(8,128)(2,1)} %param.9) | copy-start | bytes 884740
  34.5 20.5 %all-to-all-start.2 = ((bf16[16,24,512]{2,1,0:T(8,128)(2,1)}), bf16[16,24,512]{2,1,0:T(8,128)(2,1)S(1)}, u32[]{:S(2)}, u32[]{:S(2)}) async-start(bf16[16,24,512]{2,1,0:T(8,128)(2,1)} %bitcast.5), calls=%async_computation.2 | async-start | bytes 786432 | tf_op jit(solution)/shard_map/all_to_all | solution.py:286
  41.1 9.5 %collective-permute-start = (f32[3,2048]{1,0:T(4,128)S(1)}, f32[3,2048]{1,0:T(4,128)S(1)}, u32[]{:S(2)}, u32[]{:S(2)}) collective-permute-start(f32[3,2048]{1,0:T(4,128)S(1)} %get-tuple-element.14), channel_id=1, source_target_pairs={{3,4},{4,3},{7,8},{8,7},{11,12},{12,11},{15,16},{16,15},{19,20},{2... | collective-permute-start | bytes 73736 | tf_op jit(solution)/shard_map/ppermute | solution.py:284
